TPU v7x, 768 devices: a whole 4x8x12 slice. The times are simulated.
768 devices in a mesh: dp: 12 (over z), cls: 64 (over y, x, core).
Axes of the slice: x: 4, y: 8, z: 12, core: 2. Of those that a mesh axis runs over, the one named last changes fastest.
Arguments:
- features: bfloat16 [3072, 256], P('dp'), may hold values from -1 to 1
- prototypes: bfloat16 [196608, 256], P('cls'), may hold values from -0.101 to 0.101
- prior_counts: int32 [196608], P('cls'), may hold values from 1 to 4096, as said below
- cotangent: bfloat16 [3072, 196608], P('dp', 'cls'), may hold values from -6 to 6
Outputs:
- feature_grad: float32 [3072, 256], P('dp')
- prototype_grad: float32 [196608, 256], P(('cls', 'dp'))
Inputs may be any that keep to these rules, and one draw needn't show every extreme that they name: `prior_counts`: counts of the labeled pool for each class, some class holding exactly the maximum.
All inputs are finite; a program needn't handle non-finite values.
Results may differ from a plain program's by a relative error of at most 0.0022.
Values may be sent and summed in bfloat16 or wider, within the bound.
No kernel may reach another device: no remote copies, remote signals or barrier semaphores. Data moves between devices by JAX's collectives and lax.ppermute only.
A program may use at most 32 MiB of HBM per device.

v0:
```python
import jax
import jax.numpy as jnp
from jax import lax
from jax.sharding import PartitionSpec as P

ITERS = 3


sharpness = 4.0
relax_power = 0.7


def matvec(kernel, vector):
    return jnp.dot(kernel, vector, precision=lax.Precision.HIGHEST)


def vecmat(vector, kernel):
    return jnp.dot(vector, kernel, precision=lax.Precision.HIGHEST)


def row_total(partial_rows):
    return lax.psum(partial_rows, "cls")


def column_total(partial_columns):
    return lax.psum(partial_columns, "dp")


def per_device(features, prototypes, prior_counts, cotangent):
    logits = jnp.einsum("nd,kd->nk", features, prototypes, preferred_element_type=jnp.float32)
    kernel = jnp.exp(sharpness * logits)
    rows_all = features.shape[0] * lax.axis_size("dp")
    protos_all = prototypes.shape[0] * lax.axis_size("cls")
    total = lax.psum(jnp.sum(prior_counts.astype(jnp.float32)), "cls")
    target = rows_all * prior_counts.astype(jnp.float32) / total
    vectors_v = [jnp.ones((prototypes.shape[0],), jnp.float32)]
    vectors_u = []
    sums_x = []
    sums_y = []
    for step in range(ITERS):
        x_now = row_total(matvec(kernel, vectors_v[-1]))
        u_now = 1.0 / x_now
        y_now = column_total(vecmat(u_now, kernel))
        v_now = (target / y_now) ** relax_power
        sums_x.append(x_now)
        sums_y.append(y_now)
        vectors_u.append(u_now)
        vectors_v.append(v_now)
    scaled_grad = protos_all * cotangent.astype(jnp.float32)
    weighted = scaled_grad * kernel
    u_last = vectors_u[-1]
    v_last = vectors_v[-1]
    du_local = matvec(weighted, v_last)
    d_v = column_total(vecmat(u_last, weighted))
    dkernel = scaled_grad * u_last[:, None] * v_last[None, :]
    for step in range(ITERS - 1, -1, -1):
        d_y = -relax_power * d_v * vectors_v[step + 1] / sums_y[step]
        partial_u = matvec(kernel, d_y)
        if step == ITERS - 1:
            partial_u = du_local + partial_u
        d_u = row_total(partial_u)
        d_x = -d_u * vectors_u[step] / sums_x[step]
        if step > 0:
            d_v = column_total(vecmat(d_x, kernel))
        dkernel = (
            dkernel
            + vectors_u[step][:, None] * d_y[None, :]
            + d_x[:, None] * vectors_v[step][None, :]
        )
    dlogits = (sharpness * kernel * dkernel).astype(jnp.bfloat16)
    feature_grad = lax.psum(jnp.dot(dlogits, prototypes, preferred_element_type=jnp.float32), "cls")
    prototype_grad = lax.psum_scatter(
        lax.dot_general(
            dlogits, features, (((0,), (0,)), ((), ())), preferred_element_type=jnp.float32
        ),
        "dp",
        scatter_dimension=0,
        tiled=True,
    )
    return (feature_grad, prototype_grad)


def solution(mesh):
    return jax.shard_map(
        per_device,
        mesh=mesh,
        in_specs=(P("dp", None), P("cls", None), P("cls"), P("dp", "cls")),
        out_specs=(P("dp", None), P(("cls", "dp"), None)),
        check_vma=False,
    )
```

profile of v0, /device:TPU:1, one launch (start us, length us, event | category | flops | bytes accessed | tf_op | source)
XLA Modules:
  0.0 1229.9 jit_solution(4817436120843874892)
XLA Ops:
  8.0 0.0 copy-start
  8.0 0.0 all-reduce.4.cloned.1.call-start
  8.1 1.4 convert_reduce_fusion
  9.5 0.0 copy-done
  9.5 1.5 fusion
  11.0 0.0 copy-start.1
  11.0 1.7 copy-done.1
  12.7 2.5 fusion.17
  15.2 134.6 %all-reduce = (f32[256]{0:T(256)S(1)}, f32[]{:T(128)}) all-reduce(f32[256]{0:T(256)S(1)} %bitcast.78, f32[]{:T(128)} %convert_reduce_fusion), channel_id=1, replica_groups=mesh['dp'=12,'cls'=64] {'cls'}, use_global_device_ids=true, to_apply=%region_2.0 | all-reduce | flops 257 | bytes 2056 | tf_op jit(solution)/shard_map/psum | solution.py:22
  149.8 3.5 fusion.22
  153.3 33.7 %psum.100 = f32[3072]{0:T(1024)S(1)} all-reduce(f32[3072]{0:T(1024)S(1)} %bitcast.61), channel_id=1, replica_groups=mesh['dp'=12,'cls'=64] {'dp'}, use_global_device_ids=true, to_apply=%region_3.0 | all-reduce | flops 3072 | bytes 24576 | tf_op jit(solution)/shard_map/psum | solution.py:26
  187.0 0.0 copy-done.6
  187.0 0.7 divide_power_fusion.2
  187.6 4.4 fusion.23
  192.1 138.8 %psum.101 = f32[256]{0:T(256)S(1)} all-reduce(f32[256]{0:T(256)S(1)} %bitcast.74), channel_id=1, replica_groups=mesh['dp'=12,'cls'=64] {'cls'}, use_global_device_ids=true, to_apply=%region_4.0 | all-reduce | flops 256 | bytes 2048 | tf_op jit(solution)/shard_map/psum | solution.py:22
  330.9 3.5 fusion.24
  334.4 29.9 %psum.102 = f32[3072]{0:T(1024)S(1)} all-reduce(f32[3072]{0:T(1024)S(1)} %bitcast.62), channel_id=1, replica_groups=mesh['dp'=12,'cls'=64] {'dp'}, use_global_device_ids=true, to_apply=%region_5.0 | all-reduce | flops 3072 | bytes 24576 | tf_op jit(solution)/shard_map/psum | solution.py:26
  364.3 0.7 divide_power_fusion.1
  365.0 0.0 copy-start.4
  365.0 4.5 fusion.25
  369.5 134.2 %psum.103 = f32[256]{0:T(256)S(1)} all-reduce(f32[256]{0:T(256)S(1)} %bitcast.75), channel_id=1, replica_groups=mesh['dp'=12,'cls'=64] {'cls'}, use_global_device_ids=true, to_apply=%region_6.0 | all-reduce | flops 256 | bytes 2048 | tf_op jit(solution)/shard_map/psum | solution.py:22
  503.7 3.6 fusion.26
  507.3 0.0 copy-done.4
  507.3 0.0 copy-done.2
  507.3 1.9 fusion.13
  509.2 30.0 %all-reduce.1 = (f32[3072]{0:T(1024)S(1)}, f32[3072]{0:T(1024)S(1)}) all-reduce(f32[3072]{0:T(1024)S(1)} %bitcast.60, f32[3072]{0:T(1024)S(1)} %bitcast.65), channel_id=1, replica_groups=mesh['dp'=12,'cls'=64] {'dp'}, use_global_device_ids=true, to_apply=%region_7.0 | all-reduce | flops 6144 | bytes 49152 | tf_op jit(solution)/shard_map/psum | solution.py:26
  539.2 0.8 multiply_divide_fusion.2
  540.0 4.7 fusion.11
  544.7 0.0 copy-done.3
  544.7 2.5 fusion.27
  547.2 134.5 %psum.106 = f32[256]{0:T(256)S(1)} all-reduce(f32[256]{0:T(256)S(1)} %add.52), channel_id=1, replica_groups=mesh['dp'=12,'cls'=64] {'cls'}, use_global_device_ids=true, to_apply=%region_9.0 | all-reduce | flops 256 | bytes 2048 | tf_op jit(solution)/shard_map/psum | solution.py:22
  681.7 3.5 fusion.28
  685.2 29.9 %psum.107 = f32[3072]{0:T(1024)S(1)} all-reduce(f32[3072]{0:T(1024)S(1)} %bitcast.63), channel_id=1, replica_groups=mesh['dp'=12,'cls'=64] {'dp'}, use_global_device_ids=true, to_apply=%region_10.0 | all-reduce | flops 3072 | bytes 24576 | tf_op jit(solution)/shard_map/psum | solution.py:26
  715.2 4.4 fusion.29
  719.6 134.3 %psum.108 = f32[256]{0:T(256)S(1)} all-reduce(f32[256]{0:T(256)S(1)} %bitcast.76), channel_id=1, replica_groups=mesh['dp'=12,'cls'=64] {'cls'}, use_global_device_ids=true, to_apply=%region_11.0 | all-reduce | flops 256 | bytes 2048 | tf_op jit(solution)/shard_map/psum | solution.py:22
  853.8 3.5 fusion.30
  857.3 29.9 %psum.109 = f32[3072]{0:T(1024)S(1)} all-reduce(f32[3072]{0:T(1024)S(1)} %bitcast.64), channel_id=1, replica_groups=mesh['dp'=12,'cls'=64] {'dp'}, use_global_device_ids=true, to_apply=%region_12.0 | all-reduce | flops 3072 | bytes 24576 | tf_op jit(solution)/shard_map/psum | solution.py:26
  887.2 4.4 fusion.31
  891.6 134.5 %psum.110 = f32[256]{0:T(256)S(1)} all-reduce(f32[256]{0:T(256)S(1)} %bitcast.77), channel_id=1, replica_groups=mesh['dp'=12,'cls'=64] {'cls'}, use_global_device_ids=true, to_apply=%region_13.0 | all-reduce | flops 256 | bytes 2048 | tf_op jit(solution)/shard_map/psum | solution.py:22
  1026.2 3.8 fusion.9
  1030.0 0.0 copy-start.5
  1030.0 1.3 fusion.32
  1031.3 0.0 all-reduce.4.cloned.1.call-update
  1031.3 0.0 reduce-scatter.2.cloned.1.call-start
  1031.4 2.3 fusion.33
  1033.7 0.0 reduce-scatter.2.cloned.1.call-update
  1033.7 187.1 %all-reduce.4.cloned.1.call-done = f32[256,256]{1,0:T(8,128)} async-done(((f32[256,256]{1,0:T(8,128)}), f32[256,256]{1,0:T(8,128)}) %all-reduce.4.cloned.1.call-update) | async-done | bytes 262160 | tf_op jit(solution)/shard_map/psum | solution.py:71
  1220.8 1.7 copy.7
  (14 shorter events, 0.1 us)
Async XLA Ops:
  8.0 1.5 copy-start
  8.0 1212.8 %all-reduce.4.cloned.1.call-start = ((), (), s32[]{:S(2)}) async-start(), calls=%async_computation.1 | async-start | bytes 524288 | tf_op jit(solution)/shard_map/psum | solution.py:71
  11.0 1.7 copy-start.1
  12.7 174.3 %copy-start.6 = (s32[3072]{0:T(1024)S(1)}, s32[3072]{0:T(1024)}, u32[]{:S(2)}) copy-start(s32[3072]{0:T(1024)} %param.6) | copy-start | bytes 36868
  365.0 142.4 %copy-start.4 = (bf16[256,3072]{1,0:T(8,128)(2,1)S(1)}, bf16[256,3072]{1,0:T(8,128)(2,1)}, u32[]{:S(2)}) copy-start(bf16[256,3072]{1,0:T(8,128)(2,1)} %param.7) | copy-start | bytes 4718596
  503.7 3.6 copy-start.2
  539.2 5.5 copy-start.3
  1030.0 1.4 copy-start.5
  1031.3 189.5 %reduce-scatter.2.cloned.1.call-start = ((), (), s32[]{:S(2)}) async-start(), calls=%async_computation.2 | async-start | bytes 3407872 | tf_op jit(solution)/shard_map/reduce_scatter | solution.py:72
Sparse Core Ops, SparseCore 0:
  1031.4 189.3 all-reduce.3
Sparse Core Ops, SparseCore 1:
  1035.8 48.1 reduce-scatter.1
where the time goes:
time: 1230 us
  blocking collectives  964 us (78%)
  waiting for transfers between devices  187 us (15%)
  matrix products  52.1 us (4%)
  between operations  15.6 us (1%)
    psum x6, blocking collectives, row_total(): return lax.psum(partial_rows, 'cls')  811 us
    psum x1, waiting for transfers between devices, per_device(): lax.psum(jnp.dot(dlogits, prototypes, preferred_element_type=jnp.float32)...  187 us
    psum x5, blocking collectives, column_total(): return lax.psum(partial_columns, 'dp')  153 us
    dot_general x7, matrix products, matvec(): return jnp.dot(kernel, vector, precision=lax.Precision.HIGHEST)  27.5 us
  transfers between devices with their start and end apart: 2, of which 1 were waited for; matrix products, arithmetic and copies ran while one was open for 0% of the time, Pallas kernels for 0%

commit v1 on v0

v1 whole, which is shorter than its diff:
```python
import functools

import jax
import jax.numpy as jnp
from jax import lax
from jax.experimental import pallas as pl
from jax.experimental.pallas import tpu as pltpu
from jax.sharding import PartitionSpec as P

sharpness = 4.0
relax_power = 0.7

LANES = 128
F32 = jnp.float32
BF16 = jnp.bfloat16


def call(body, outs, args, name, smem=0, flops=0):
    specs = [pl.BlockSpec(memory_space=pltpu.SMEM)] * smem
    specs += [pl.BlockSpec(memory_space=pltpu.VMEM)] * (len(args) - smem)
    moved = sum(a.size * a.dtype.itemsize for a in (*args, *outs))
    return pl.pallas_call(
        body,
        out_shape=outs,
        in_specs=specs,
        out_specs=[pl.BlockSpec(memory_space=pltpu.VMEM)] * len(outs),
        compiler_params=pltpu.CompilerParams(vmem_limit_bytes=16 * 2**20),
        cost_estimate=pl.CostEstimate(flops=flops, bytes_accessed=moved, transcendentals=0),
        name=name,
    )(*args)


def f32(*shape):
    return jax.ShapeDtypeStruct(shape, F32)


def tiles(size, width):
    return [slice(start, start + width) for start in range(0, size, width)]


def down(row, width=LANES):
    return jnp.transpose(jnp.broadcast_to(row, (width, row.shape[1])))


def flat(sums):
    return jnp.sum(jnp.transpose(sums), axis=0, keepdims=True)


def copies(row, count):
    return jnp.broadcast_to(row[None], (count,) + row.shape)


def parts(value):
    high = value.astype(BF16)
    return high, (value - high.astype(F32)).astype(BF16)


def rows_of(kernel_ref, weight):
    sums = 0.0
    for at in tiles(kernel_ref.shape[1], LANES):
        sums = sums + kernel_ref[:, at] * weight(at)
    return flat(sums)


def received(ref, start, stop):
    return jnp.sum(ref[:, :, start:stop], axis=0)


def expo_body(left_ref, right_ref, kernel_ref):
    left = left_ref[...]
    for at in tiles(right_ref.shape[0], 512):
        logits = lax.dot_general(left, right_ref[at, :], (((1,), (1,)), ((), ())), preferred_element_type=F32)
        kernel_ref[:, at] = jnp.exp(sharpness * logits)


def start_body(features_ref, prototypes_ref, counts_ref, kernel_ref, out_ref):
    rows = features_ref.shape[0]
    left = features_ref[...]
    sums = 0.0
    for at in tiles(prototypes_ref.shape[0], 512):
        logits = lax.dot_general(left, prototypes_ref[at, :], (((1,), (1,)), ((), ())), preferred_element_type=F32)
        block = jnp.exp(sharpness * logits)
        kernel_ref[:, at] = block
        for inner in tiles(512, LANES):
            sums = sums + block[:, inner]
    out_ref[:, :, :rows] = copies(flat(sums), out_ref.shape[0])
    total = jnp.sum(counts_ref[...].astype(F32), axis=1, keepdims=True)
    out_ref[:, :, rows:] = jnp.broadcast_to(total[None], (out_ref.shape[0], 1, LANES))


def columns_body(first, x_ref, kernel_ref, *rest):
    if first:
        total_ref, u_ref, out_ref = rest
    else:
        u_ref, out_ref = rest
    rows, columns = kernel_ref.shape
    count = out_ref.shape[0]
    u = 1.0 / received(x_ref, 0, rows)
    u_ref[...] = u
    if first:
        total_ref[...] = received(x_ref, rows, rows + LANES)
    wide = down(u)
    for at in tiles(columns, LANES):
        out_ref[:, :, at] = copies(jnp.sum(kernel_ref[:, at] * wide, axis=0, keepdims=True), count)
    out_ref[:, :, columns:] = copies(u, count)


def columns_last_body(protos_all, x_ref, kernel_ref, cotangent_ref, u_ref, out_ref):
    rows, columns = kernel_ref.shape
    count = out_ref.shape[0]
    u = 1.0 / received(x_ref, 0, rows)
    u_ref[...] = u
    wide = down(u)
    for at in tiles(columns, LANES):
        weighted = kernel_ref[:, at] * wide
        out_ref[:, :, at] = copies(jnp.sum(weighted, axis=0, keepdims=True), count)
        weighted = weighted * cotangent_ref[:, at].astype(F32)
        later = slice(columns + at.start, columns + at.stop)
        out_ref[:, :, later] = copies(protos_all * jnp.sum(weighted, axis=0, keepdims=True), count)
    out_ref[:, :, 2 * columns :] = copies(u, count)


def spread(ref, all_ref, start):
    rows = all_ref.shape[1] // ref.shape[0]
    for i in range(ref.shape[0]):
        all_ref[:, i * rows : (i + 1) * rows] = ref[i, :, start : start + rows]


def relaxed(y, counts_ref, total_ref, samples_all):
    target = samples_all * counts_ref[...].astype(F32) / total_ref[:, :1]
    return jnp.exp(relax_power * jnp.log(target / y))


def rows_body(samples_all, y_ref, counts_ref, total_ref, kernel_ref, y_out_ref, v_ref, all_ref, out_ref):
    columns = kernel_ref.shape[1]
    y = received(y_ref, 0, columns)
    y_out_ref[...] = y
    v_ref[...] = relaxed(y, counts_ref, total_ref, samples_all)
    spread(y_ref, all_ref, columns)
    out_ref[...] = copies(rows_of(kernel_ref, lambda at: v_ref[:, at]), out_ref.shape[0])


def rows_last_body(
    samples_all, protos_all, y_ref, counts_ref, total_ref, kernel_ref, cotangent_ref, v_ref, dy_ref, all_ref, out_ref
):
    columns = kernel_ref.shape[1]
    y = received(y_ref, 0, columns)
    v = relaxed(y, counts_ref, total_ref, samples_all)
    v_ref[...] = v
    dy_ref[...] = -relax_power * received(y_ref, columns, 2 * columns) * v / y
    spread(y_ref, all_ref, 2 * columns)
    weight = lambda at: protos_all * cotangent_ref[:, at].astype(F32) * v_ref[:, at] + dy_ref[:, at]
    out_ref[...] = copies(rows_of(kernel_ref, weight), out_ref.shape[0])


def back_columns_body(has_slice, du_ref, u_ref, kernel_ref, *rest):
    if has_slice:
        dx_ref, slice_ref, out_ref = rest
    else:
        dx_ref, out_ref = rest
    rows, columns = kernel_ref.shape
    count = out_ref.shape[0]
    u = u_ref[...]
    dx = -received(du_ref, 0, rows) * u * u
    dx_ref[...] = dx
    if has_slice:
        slice_ref[...] = received(du_ref, rows, du_ref.shape[2])
    wide = down(dx)
    for at in tiles(columns, LANES):
        out_ref[:, :, at] = copies(jnp.sum(kernel_ref[:, at] * wide, axis=0, keepdims=True), count)
    out_ref[:, :, columns:] = copies(dx, count)


def back_rows_body(dv_ref, v_ref, y_ref, kernel_ref, extra_ref, dy_ref, all_ref, out_ref):
    rows, columns = kernel_ref.shape
    dy_ref[...] = -relax_power * received(dv_ref, 0, columns) * v_ref[...] / y_ref[...]
    spread(dv_ref, all_ref, columns)
    row = rows_of(kernel_ref, lambda at: dy_ref[:, at])
    out_ref[:, :, :rows] = copies(row, out_ref.shape[0])
    out_ref[:, :, rows:] = extra_ref[...]


def scatter_rows(value, out_ref, start):
    count = out_ref.shape[0]
    width = value.shape[1]
    for r in range(value.shape[0] // count):
        block = value[r * count : (r + 1) * count, :]
        out_ref[:, :, start + r * width : start + (r + 1) * width] = block[:, None, :]


def product(value, right):
    high, low = parts(value)
    return jnp.dot(high, right, preferred_element_type=F32) + jnp.dot(low, right, preferred_element_type=F32)


def plain_product_body(kernel_ref, prototypes_ref, out_ref):
    total = 0.0
    for at in tiles(kernel_ref.shape[1], 512):
        total = total + product(kernel_ref[:, at], prototypes_ref[at, :])
    scatter_rows(sharpness * total, out_ref, 0)


def known_product_body(
    protos_all, kernel_ref, cotangent_ref, prototypes_ref, u2_ref, u3_ref, dx2_ref, dx3_ref,
    v1_ref, v2_ref, v3_ref, dy2_ref, dy3_ref, out_ref,
):
    width = 256
    u2, u3, dx2, dx3 = (down(ref[...], width) for ref in (u2_ref, u3_ref, dx2_ref, dx3_ref))
    total = 0.0
    for at in tiles(kernel_ref.shape[1], width):
        grad = protos_all * cotangent_ref[:, at].astype(F32)
        inner = u3 * (grad * v3_ref[:, at] + dy3_ref[:, at])
        inner = inner + dx3 * v2_ref[:, at] + u2 * dy2_ref[:, at] + dx2 * v1_ref[:, at]
        total = total + product(kernel_ref[:, at] * inner, prototypes_ref[at, :])
    out_ref[...] = sharpness * total


def last_rows_body(dv_ref, v_ref, y_ref, kernel_ref, prototypes_ref, known_ref, u_ref, dy_ref, all_ref, out_ref):
    rows, columns = kernel_ref.shape
    dy_ref[...] = -relax_power * received(dv_ref, 0, columns) * v_ref[...] / y_ref[...]
    spread(dv_ref, all_ref, columns)
    width = 256
    sums, total = 0.0, 0.0
    for at in tiles(columns, width):
        weighted = kernel_ref[:, at] * dy_ref[:, at]
        for inner in tiles(width, LANES):
            sums = sums + weighted[:, inner]
        total = total + product(weighted, prototypes_ref[at, :])
    out_ref[:, :, :rows] = copies(flat(sums), out_ref.shape[0])
    total = known_ref[...] + sharpness * down(u_ref[...], total.shape[1]) * total
    scatter_rows(total, out_ref, rows)


def finish_rows_body(place_ref, du_ref, u_ref, slice_ref, dx_out_ref, out_ref):
    rows = u_ref.shape[1]
    u = u_ref[...]
    dx = -received(du_ref, 0, rows) * u * u
    dx_out_ref[...] = copies(dx, dx_out_ref.shape[0])
    count = out_ref.shape[0]
    mine = received(du_ref, rows, du_ref.shape[2])
    width = mine.shape[1] * count // rows
    lane = lax.broadcasted_iota(jnp.int32, dx.shape, 1)
    for r in range(rows // count):
        at = slice(r * width, (r + 1) * width)
        value = jnp.sum(jnp.where(lane == r * count + place_ref[0], dx, 0.0), axis=1, keepdims=True)
        out_ref[:, :, at] = copies(mine[:, at] + value * slice_ref[:, at], count)


def weighted_product_body(protos_all, kernel_ref, cotangent_ref, u_ref, features_ref, out_ref):
    width = 256
    wide = protos_all * down(u_ref[...], width)
    features = features_ref[...]
    rows = (((0,), (0,)), ((), ()))
    for at in tiles(kernel_ref.shape[1], width):
        high, low = parts(kernel_ref[:, at] * cotangent_ref[:, at].astype(F32) * wide)
        out_ref[at, :] = lax.dot_general(high, features, rows, preferred_element_type=F32) + lax.dot_general(
            low, features, rows, preferred_element_type=F32
        )


def own_columns(place_ref, ref, own, width=LANES):
    start = pl.multiple_of(place_ref[0] * own, own)
    return down(ref[:, pl.ds(start, own)], width)


def known_columns_body(
    place_ref, kernel_ref, u1_ref, u2_ref, u3_ref, dx2_ref, dx3_ref, v1_ref, v2_ref, dy1_ref, dy2_ref, dy3_ref, out_ref
):
    own, samples = kernel_ref.shape
    v1, v2, dy1, dy2, dy3 = (own_columns(place_ref, ref, own) for ref in (v1_ref, v2_ref, dy1_ref, dy2_ref, dy3_ref))
    for at in tiles(samples, LANES):
        inner = u3_ref[:, at] * dy3 + dx3_ref[:, at] * v2
        inner = inner + u2_ref[:, at] * dy2 + dx2_ref[:, at] * v1 + u1_ref[:, at] * dy1
        out_ref[:, at] = sharpness * kernel_ref[:, at] * inner


def finish_columns_body(place_ref, dx_ref, kernel_ref, known_ref, features_ref, v_ref, weighted_ref, out_ref):
    own = kernel_ref.shape[0]
    rows = dx_ref.shape[2]
    total = sharpness * own_columns(place_ref, v_ref, own, out_ref.shape[1]) * weighted_ref[...]
    for i in range(dx_ref.shape[0]):
        at = slice(i * rows, (i + 1) * rows)
        dlogits = known_ref[:, at] + sharpness * kernel_ref[:, at] * dx_ref[i]
        total = total + product(dlogits, features_ref[at, :])
    out_ref[...] = total


def gather_rows_body(ref, out_ref):
    count = ref.shape[0]
    width = out_ref.shape[1]
    for r in range(out_ref.shape[0] // count):
        out_ref[r * count : (r + 1) * count, :] = ref[:, 0, r * width : (r + 1) * width]


def exchange(messages, axis):
    return lax.all_to_all(messages, axis, 0, 0, tiled=True)


def together(*arrays):
    return lax.optimization_barrier(arrays)


def per_device(features, prototypes, prior_counts, cotangent):
    rows, width = features.shape
    columns = prototypes.shape[0]
    samples = lax.axis_size("dp")
    classes = lax.axis_size("cls")
    own = columns // samples
    rows_all = rows * samples
    protos_all = float(columns * classes)
    sliced = rows * width // classes
    counts = prior_counts.reshape(1, columns)
    dp_place = lax.axis_index("dp").astype(jnp.int32).reshape(1)
    cls_place = lax.axis_index("cls").astype(jnp.int32).reshape(1)
    block_flops = 2 * rows * columns

    features_all = lax.all_gather(features, "dp", axis=0, tiled=True)

    row, column = f32(1, rows), f32(1, columns)
    everyone = f32(1, rows_all)
    kernel, message = call(
        start_body, [f32(rows, columns), f32(classes, 1, rows + LANES)], [features, prototypes, counts], "start",
        flops=block_flops * width,
    )
    u, v, y, u_all = [], [], [], []
    for step in range(2):
        x_message = exchange(message, "cls")
        outs = [row, f32(samples, 1, columns + rows)]
        if step == 0:
            total, u_now, message = call(
                functools.partial(columns_body, True), [f32(1, LANES)] + outs, [x_message, kernel], "columns_first", flops=block_flops
            )
        else:
            u_now, message = call(functools.partial(columns_body, False), outs, [x_message, kernel], "columns", flops=block_flops)
        y_message = exchange(message, "dp")
        y_now, v_now, all_now, message = call(
            functools.partial(rows_body, float(rows_all)), [column, column, everyone, f32(classes, 1, rows)],
            [y_message, counts, total, kernel], "rows", flops=block_flops,
        )
        u.append(u_now)
        v.append(v_now)
        y.append(y_now)
        u_all.append(all_now)
    x_message = exchange(message, "cls")
    x_message, features_all = together(x_message, features_all)
    u_now, message = call(
        functools.partial(columns_last_body, protos_all), [row, f32(samples, 1, 2 * columns + rows)],
        [x_message, kernel, cotangent], "columns_last", flops=2 * block_flops,
    )
    u.append(u_now)
    message, u_late = together(message, u_now)
    (weighted,) = call(
        functools.partial(weighted_product_body, protos_all), [f32(columns, width)], [kernel, cotangent, u_late, features],
        "weighted_product", flops=2 * block_flops * width,
    )
    y_message, weighted = together(exchange(message, "dp"), weighted)
    weighted = lax.psum_scatter(weighted, "dp", scatter_dimension=0, tiled=True)
    v_now, dy3, all_now, message = call(
        functools.partial(rows_last_body, float(rows_all), protos_all),
        [column, column, everyone, f32(classes, 1, rows)],
        [y_message, counts, total, kernel, cotangent], "rows_last", flops=2 * block_flops,
    )
    v.append(v_now)
    u_all.append(all_now)

    message, right = together(message, prototypes)
    (plain,) = call(plain_product_body, [f32(classes, 1, sliced)], [kernel, right], "plain_product", flops=2 * block_flops * width)
    du_message, plain = together(exchange(message, "cls"), plain)
    dx3, message = call(
        functools.partial(back_columns_body, False), [row, f32(samples, 1, columns + rows)], [du_message, u[2], kernel],
        "back_columns", flops=block_flops,
    )
    message, right = together(message, features_all)
    own_prototypes = lax.dynamic_slice_in_dim(prototypes, dp_place[0] * own, own, 0)
    (kernel_columns,) = call(expo_body, [f32(own, rows_all)], [own_prototypes, right], "expo", flops=block_flops * width)
    dv_message, kernel_columns = together(exchange(message, "dp"), kernel_columns)
    dy2, dx3_all, message = call(
        back_rows_body, [column, everyone, f32(classes, 1, rows + sliced)], [dv_message, v[1], y[1], kernel, plain],
        "back_rows", flops=block_flops,
    )
    du_message = exchange(message, "cls")
    dx2, plain_slice, message = call(
        functools.partial(back_columns_body, True), [row, f32(1, sliced), f32(samples, 1, columns + rows)],
        [du_message, u[1], kernel], "back_columns_slice", flops=block_flops,
    )
    message, dx2_late = together(message, dx2)
    (known,) = call(
        functools.partial(known_product_body, protos_all), [f32(rows, width)],
        [kernel, cotangent, prototypes, u[1], u[2], dx2_late, dx3, v[0], v[1], v[2], dy2, dy3], "known_product",
        flops=2 * block_flops * width,
    )
    dv_message, known = together(exchange(message, "dp"), known)
    dy1, dx2_all, message = call(
        last_rows_body, [column, everyone, f32(classes, 1, rows + sliced)],
        [dv_message, v[0], y[0], kernel, prototypes, known, u[0]], "last_rows", flops=2 * block_flops * width,
    )
    message, dy1 = together(message, dy1)
    (known_columns,) = call(
        known_columns_body, [f32(own, rows_all)],
        [dp_place, kernel_columns, *u_all, dx2_all, dx3_all, v[0], v[1], dy1, dy2, dy3], "known_columns",
        smem=1, flops=20 * own * rows_all,
    )
    du_message, known_columns = together(exchange(message, "cls"), known_columns)
    dx_message, message = call(
        finish_rows_body, [f32(samples, 1, rows), f32(classes, 1, sliced)], [cls_place, du_message, u[0], plain_slice],
        "finish_rows", smem=1,
    )
    dx1 = exchange(dx_message, "dp")
    gathered = exchange(message, "cls")
    (prototype_grad,) = call(
        finish_columns_body, [f32(own, width)],
        [dp_place, dx1, kernel_columns, known_columns, features_all, v[2], weighted], "finish_columns", smem=1,
        flops=2 * block_flops * width,
    )
    (feature_grad,) = call(gather_rows_body, [f32(rows, width)], [gathered], "gather_rows")
    return (feature_grad, prototype_grad)


def solution(mesh):
    return jax.shard_map(
        per_device,
        mesh=mesh,
        in_specs=(P("dp", None), P("cls", None), P("cls"), P("dp", "cls")),
        out_specs=(P("dp", None), P(("cls", "dp"), None)),
        check_vma=False,
    )
```

time: 1230 us -> 286 us (0.23)
  blocking collectives: 964 us -> 135 us
  waiting for transfers between devices: 187 us -> 48.2 us
  matrix products: 52.1 us -> 0 us
  local copies, waits for them, and re-layouts: 3.36 us -> 37.5 us
  starting transfers between devices: 0.08 us -> 30.1 us
  Pallas kernels: 0 us -> 19 us
    psum x11 -> x0, blocking collectives: 964 us -> none  [the longest x6 811 us: row_total(): return lax.psum(partial_rows, 'cls')]
    psum x1 -> x0, waiting for transfers between devices: 187 us -> none  [per_device(): lax.psum(jnp.dot(dlogits, prototypes, preferred_element_type=jnp.float32)...]
    all_to_all x0 -> x7, blocking collectives: none -> 135 us  [exchange(): return lax.all_to_all(messages, axis, 0, 0, tiled=True)]
    dot_general x16 -> x0, matrix products: 52.1 us -> none  [the longest x7 27.5 us: matvec(): return jnp.dot(kernel, vector, precision=lax.Precision.HIGHEST)]
    all_to_all x0 -> x6, waiting for transfers between devices: none -> 47.5 us  [exchange(): return lax.all_to_all(messages, axis, 0, 0, tiled=True)]
    unnamed x15 -> x92, local copies, waits for them, and re-layouts: 3.36 us -> 36.6 us
    all_to_all x0 -> x6, starting transfers between devices: none -> 30 us  [exchange(): return lax.all_to_all(messages, axis, 0, 0, tiled=True)]
    pallas_call x0 -> x19, Pallas kernels: none -> 19 us  [call(): pl.pallas_call(body, out_shape=outs, in_specs=specs, out_specs=[pl.BlockS...]
  transfers between devices with their start and end apart: 2 -> 8, of which waited for: 1 -> 6; matrix products, arithmetic and copies ran while one was open for 0% -> 0% of each run, Pallas kernels for 0% -> 6%
where the time goes in v1:
time: 286 us; the launch traced here: 285 us
  blocking collectives  135 us (47%)
  waiting for transfers between devices  48.2 us (17%)
  local copies, waits for them, and re-layouts  37.5 us (13%)
  starting transfers between devices  30.1 us (11%)
  Pallas kernels  19 us (7%)
  between operations  14.4 us (5%)
    all_to_all x7, blocking collectives, exchange(): return lax.all_to_all(messages, axis, 0, 0, tiled=True)  135 us
    all_to_all x6, waiting for transfers between devices, exchange(): return lax.all_to_all(messages, axis, 0, 0, tiled=True)  47.5 us
    unnamed x92, local copies, waits for them, and re-layouts  36.6 us
    all_to_all x6, starting transfers between devices, exchange(): return lax.all_to_all(messages, axis, 0, 0, tiled=True)  30 us
    pallas_call x19, Pallas kernels, call(): pl.pallas_call(body, out_shape=outs, in_specs=specs, out_specs=[pl.BlockS...  19 us
  transfers between devices with their start and end apart: 8, of which 6 were waited for; matrix products, arithmetic and copies ran while one was open for 0% of the time, Pallas kernels for 6%

profile of v1, /device:TPU:1, one launch (start us, length us, event | category | flops | bytes accessed | tf_op | source)
XLA Modules:
  0.0 284.6 jit_solution(18295913170374538787)
XLA Ops:
  7.9 1.4 copy-done.3
  9.3 0.9 copy-done.16
  11.7 24.5 %all_to_all.65.x_ref = f32[64,1,384]{2,1,0:T(1,128)S(1)} all-to-all(f32[64,1,384]{2,1,0:T(1,128)S(1)} %get-tuple-element.58), channel_id=1, replica_groups=mesh['dp'=12,'cls'=64] {'cls'}, dimensions={0} | all-to-all | bytes 196608 | tf_op jit(solution)/shard_map/all_to_all | solution.py:296
  37.2 26.1 %all_to_all.66.y_ref = f32[12,1,3328]{2,1,0:T(1,128)S(1)} all-to-all(f32[12,1,3328]{2,1,0:T(1,128)S(1)} %get-tuple-element.60), channel_id=1, replica_groups=mesh['dp'=12,'cls'=64] {'dp'}, dimensions={0} | all-to-all | bytes 319488 | tf_op jit(solution)/shard_map/all_to_all | solution.py:296
  63.7 16.0 %all_to_all.67.x_ref = f32[64,1,256]{2,1,0:T(1,128)S(1)} all-to-all(f32[64,1,256]{2,1,0:T(1,128)S(1)} %get-tuple-element.62), channel_id=1, replica_groups=mesh['dp'=12,'cls'=64] {'cls'}, dimensions={0} | all-to-all | bytes 131072 | tf_op jit(solution)/shard_map/all_to_all | solution.py:296
  80.2 14.6 %all_to_all.68.y_ref = f32[12,1,3328]{2,1,0:T(1,128)S(1)} all-to-all(f32[12,1,3328]{2,1,0:T(1,128)S(1)} %get-tuple-element.63), channel_id=1, replica_groups=mesh['dp'=12,'cls'=64] {'dp'}, dimensions={0} | all-to-all | bytes 319488 | tf_op jit(solution)/shard_map/all_to_all | solution.py:296
  96.4 15.2 %all_to_all.69.x_ref = f32[64,1,256]{2,1,0:T(1,128)S(1)} all-to-all(f32[64,1,256]{2,1,0:T(1,128)S(1)} %get-tuple-element.64), channel_id=1, replica_groups=mesh['dp'=12,'cls'=64] {'cls'}, dimensions={0} | all-to-all | bytes 131072 | tf_op jit(solution)/shard_map/all_to_all | solution.py:296
  111.6 1.4 copy-done.7
  114.5 3.6 %all-to-all-start.5 = ((f32[12,1,6400]{2,1,0:T(1,128)}), f32[12,1,6400]{2,1,0:T(1,128)S(1)}, u32[]{:S(2)}, u32[]{:S(2)}) async-start(f32[12,1,6400]{2,1,0:T(1,128)} %copy-done.19), calls=%async_computation.5 | async-start | bytes 614400 | tf_op jit(solution)/shard_map/all_to_all | solution.py:296
  118.1 1.4 copy-done.8
  119.5 0.9 copy-done.17
  120.4 1.2 weighted_product.1
  121.6 1.6 copy-done.13
  123.3 10.8 %all-to-all-done.5.y_ref = f32[12,1,6400]{2,1,0:T(1,128)S(1)} async-done(((f32[12,1,6400]{2,1,0:T(1,128)}), f32[12,1,6400]{2,1,0:T(1,128)S(1)}, u32[]{:S(2)}, u32[]{:S(2)}) %all-to-all-start.5) | async-done | bytes 307232 | tf_op jit(solution)/shard_map/all_to_all | solution.py:296
  134.1 1.4 copy-done.9
  135.5 1.0 rows_last.1
  137.1 7.4 %all-to-all-start.6 = ((f32[64,1,256]{2,1,0:T(1,128)}), f32[64,1,256]{2,1,0:T(1,128)S(1)}, u32[]{:S(2)}, u32[]{:S(2)}) async-start(f32[64,1,256]{2,1,0:T(1,128)} %copy-done.24), calls=%async_computation.6 | async-start | bytes 131072 | tf_op jit(solution)/shard_map/all_to_all | solution.py:296
  144.5 1.4 copy-done.4
  145.9 1.0 plain_product.1.extra_ref
  146.9 7.7 %all-to-all-done.6.du_ref = f32[64,1,256]{2,1,0:T(1,128)S(1)} async-done(((f32[64,1,256]{2,1,0:T(1,128)}), f32[64,1,256]{2,1,0:T(1,128)S(1)}, u32[]{:S(2)}, u32[]{:S(2)}) %all-to-all-start.6) | async-done | bytes 65568 | tf_op jit(solution)/shard_map/all_to_all | solution.py:296
  156.3 4.5 %all-to-all-start.7 = ((f32[12,1,3328]{2,1,0:T(1,128)}), f32[12,1,3328]{2,1,0:T(1,128)}, u32[]{:S(2)}, u32[]{:S(2)}) async-start(f32[12,1,3328]{2,1,0:T(1,128)} %copy-done.23), calls=%async_computation.7 | async-start | bytes 319488 | tf_op jit(solution)/shard_map/all_to_all | solution.py:296
  160.8 0.9 constant_dynamic-slice_fusion.left_ref
  161.7 1.4 copy-done.14
  163.8 1.7 copy-done
  165.4 8.1 %all-to-all-done.7.dv_ref = f32[12,1,3328]{2,1,0:T(1,128)} async-done(((f32[12,1,3328]{2,1,0:T(1,128)}), f32[12,1,3328]{2,1,0:T(1,128)}, u32[]{:S(2)}, u32[]{:S(2)}) %all-to-all-start.7) | async-done | bytes 159776 | tf_op jit(solution)/shard_map/all_to_all | solution.py:296
  173.6 1.3 back_rows.1
  174.9 21.0 %all_to_all.70.du_ref = f32[64,1,1280]{2,1,0:T(1,128)S(1)} all-to-all(f32[64,1,1280]{2,1,0:T(1,128)S(1)} %get-tuple-element.83), channel_id=1, replica_groups=mesh['dp'=12,'cls'=64] {'cls'}, dimensions={0} | all-to-all | bytes 655360 | tf_op jit(solution)/shard_map/all_to_all | solution.py:296
  195.9 1.2 back_columns_slice.1
  197.7 4.2 %all-to-all-start.9 = ((f32[12,1,3328]{2,1,0:T(1,128)}), f32[12,1,3328]{2,1,0:T(1,128)}, u32[]{:S(2)}, u32[]{:S(2)}) async-start(f32[12,1,3328]{2,1,0:T(1,128)} %get-tuple-element.87), calls=%async_computation.9 | async-start | bytes 319488 | tf_op jit(solution)/shard_map/all_to_all | solution.py:296
  201.9 1.4 copy-done.5
  203.3 1.4 copy-done.10
  204.7 1.9 known_product.1.known_ref
  206.6 7.5 %all-to-all-done.9.dv_ref = f32[12,1,3328]{2,1,0:T(1,128)} async-done(((f32[12,1,3328]{2,1,0:T(1,128)}), f32[12,1,3328]{2,1,0:T(1,128)}, u32[]{:S(2)}, u32[]{:S(2)}) %all-to-all-start.9) | async-done | bytes 159776 | tf_op jit(solution)/shard_map/all_to_all | solution.py:296
  214.1 1.4 copy-done.6
  215.5 2.1 last_rows.1
  219.5 7.0 %all-to-all-start.10 = ((f32[64,1,1280]{2,1,0:T(1,128)}), f32[64,1,1280]{2,1,0:T(1,128)S(1)}, u32[]{:S(2)}, u32[]{:S(2)}) async-start(f32[64,1,1280]{2,1,0:T(1,128)} %copy-done.18), calls=%async_computation.10 | async-start | bytes 655360 | tf_op jit(solution)/shard_map/all_to_all | solution.py:296
  226.5 1.9 copy-done.1
  231.9 1.8 known_columns.1.known_ref
  233.7 1.7 copy-done.11
  235.4 5.3 %all-to-all-done.10.du_ref = f32[64,1,1280]{2,1,0:T(1,128)S(1)} async-done(((f32[64,1,1280]{2,1,0:T(1,128)}), f32[64,1,1280]{2,1,0:T(1,128)S(1)}, u32[]{:S(2)}, u32[]{:S(2)}) %all-to-all-start.10) | async-done | bytes 327712 | tf_op jit(solution)/shard_map/all_to_all | solution.py:296
  241.3 18.0 %all_to_all.71.ref = f32[64,1,1024]{2,1,0:T(1,128)S(1)} all-to-all(f32[64,1,1024]{2,1,0:T(1,128)S(1)} %get-tuple-element.110), channel_id=1, replica_groups=mesh['dp'=12,'cls'=64] {'cls'}, dimensions={0} | all-to-all | bytes 524288 | tf_op jit(solution)/shard_map/all_to_all | solution.py:296
  259.4 3.5 %all-to-all-start.12 = ((f32[12,1,256]{2,1,0:T(1,128)}), f32[12,1,256]{2,1,0:T(1,128)S(1)}, u32[]{:S(2)}, u32[]{:S(2)}) async-start(f32[12,1,256]{2,1,0:T(1,128)} %get-tuple-element.111), calls=%async_computation.12 | async-start | bytes 24576 | tf_op jit(solution)/shard_map/all_to_all | solution.py:296
  262.9 0.8 gather_rows.1
  263.6 8.1 %all-to-all-done.12.dx_ref = f32[12,1,256]{2,1,0:T(1,128)S(1)} async-done(((f32[12,1,256]{2,1,0:T(1,128)}), f32[12,1,256]{2,1,0:T(1,128)S(1)}, u32[]{:S(2)}, u32[]{:S(2)}) %all-to-all-start.12) | async-done | bytes 12320 | tf_op jit(solution)/shard_map/all_to_all | solution.py:296
  271.8 1.9 copy-done.12
  273.6 1.4 copy-done.15
  275.1 0.9 copy-done.20
  276.0 1.7 finish_columns.1
  (89 shorter events, 16.9 us)
Async XLA Ops:
  7.2 104.4 %all-gather.2.cloned.1.call-start = ((), (), s32[]{:S(2)}) async-start(), calls=%async_computation.14 | async-start | bytes 1703936 | tf_op jit(solution)/shard_map/all_gather | solution.py:317
  7.9 1.4 copy-start.3
  9.3 0.9 copy-start.16
  10.2 0.7 copy-start.21
  63.7 16.5 %copy-start.27 = (f32[1,3072]{1,0:T(1,128)}, f32[1,3072]{1,0:T(1,128)S(1)}, u32[]{:S(2)}) copy-start(f32[1,3072]{1,0:T(1,128)S(1)} %get-tuple-element.95.y_ref) | copy-start | bytes 36868
  95.8 0.6 copy-start.37
  111.6 1.4 copy-start.7
  113.7 0.7 copy-start.19
  114.5 19.6 %all-to-all-start.5 = ((f32[12,1,6400]{2,1,0:T(1,128)}), f32[12,1,6400]{2,1,0:T(1,128)S(1)}, u32[]{:S(2)}, u32[]{:S(2)}) async-start(f32[12,1,6400]{2,1,0:T(1,128)} %copy-done.19), calls=%async_computation.5 | async-start | bytes 614400 | tf_op jit(solution)/shard_map/all_to_all | solution.py:296
  118.0 153.7 %reduce-scatter.2.cloned.1.call-start = ((), (), s32[]{:S(2)}) async-start(), calls=%async_computation.15 | async-start | bytes 3407872 | tf_op jit(solution)/shard_map/reduce_scatter | solution.py:357
  118.1 1.4 copy-start.8
  119.5 0.9 copy-start.17
  121.6 1.6 copy-start.13
  123.3 10.8 %copy-start.22 = (s32[3072]{0:T(1024)S(1)}, s32[3072]{0:T(1024)}, u32[]{:S(2)}) copy-start(s32[3072]{0:T(1024)} %param.6) | copy-start | bytes 36868
  134.1 1.4 copy-start.9
  136.5 0.6 copy-start.24
  137.1 18.0 %copy-start.29 = (f32[1,3072]{1,0:T(1,128)}, f32[1,3072]{1,0:T(1,128)S(1)}, u32[]{:S(2)}) copy-start(f32[1,3072]{1,0:T(1,128)S(1)} %get-tuple-element.104.u3_ref) | copy-start | bytes 36868
  137.1 17.5 %all-to-all-start.6 = ((f32[64,1,256]{2,1,0:T(1,128)}), f32[64,1,256]{2,1,0:T(1,128)S(1)}, u32[]{:S(2)}, u32[]{:S(2)}) async-start(f32[64,1,256]{2,1,0:T(1,128)} %copy-done.24), calls=%async_computation.6 | async-start | bytes 131072 | tf_op jit(solution)/shard_map/all_to_all | solution.py:296
  144.5 1.4 copy-start.4
  155.1 0.7 copy-start.23
  156.3 17.3 %copy-start.38 = (f32[1,3072]{1,0:T(1,128)S(1)}, f32[1,3072]{1,0:T(1,128)}, u32[]{:S(2)}) copy-start(f32[1,3072]{1,0:T(1,128)} %copy-done.37) | copy-start | bytes 36868
  156.3 17.3 %all-to-all-start.7 = ((f32[12,1,3328]{2,1,0:T(1,128)}), f32[12,1,3328]{2,1,0:T(1,128)}, u32[]{:S(2)}, u32[]{:S(2)}) async-start(f32[12,1,3328]{2,1,0:T(1,128)} %copy-done.23), calls=%async_computation.7 | async-start | bytes 319488 | tf_op jit(solution)/shard_map/all_to_all | solution.py:296
  161.7 1.4 copy-start.14
  163.8 1.7 copy-start
  173.6 28.3 %copy-start.45 = (f32[1,256]{1,0:T(1,128)S(1)}, f32[1,256]{1,0:T(1,128)}, u32[]{:S(2)}) copy-start(f32[1,256]{1,0:T(1,128)} %copy-done.44) | copy-start | bytes 3076
  174.9 27.0 %copy-start.31 = (f32[1,3072]{1,0:T(1,128)}, f32[1,3072]{1,0:T(1,128)S(1)}, u32[]{:S(2)}) copy-start(f32[1,3072]{1,0:T(1,128)S(1)} %get-tuple-element.106.dx3_ref) | copy-start | bytes 36868
  197.7 16.4 %all-to-all-start.9 = ((f32[12,1,3328]{2,1,0:T(1,128)}), f32[12,1,3328]{2,1,0:T(1,128)}, u32[]{:S(2)}, u32[]{:S(2)}) async-start(f32[12,1,3328]{2,1,0:T(1,128)} %get-tuple-element.87), calls=%async_computation.9 | async-start | bytes 319488 | tf_op jit(solution)/shard_map/all_to_all | solution.py:296
  201.9 1.4 copy-start.5
  203.3 1.4 copy-start.10
  204.7 9.4 %copy-start.28 = (f32[1,3072]{1,0:T(1,128)S(1)}, f32[1,3072]{1,0:T(1,128)}, u32[]{:S(2)}) copy-start(f32[1,3072]{1,0:T(1,128)} %copy-done.27) | copy-start | bytes 36868
  204.7 9.4 %copy-start.40 = (f32[1,256]{1,0:T(1,128)S(1)}, f32[1,256]{1,0:T(1,128)}, u32[]{:S(2)}) copy-start(f32[1,256]{1,0:T(1,128)} %copy-done.39) | copy-start | bytes 3076
  214.1 1.4 copy-start.6
  217.6 0.7 copy-start.18
  219.5 21.1 %all-to-all-start.10 = ((f32[64,1,1280]{2,1,0:T(1,128)}), f32[64,1,1280]{2,1,0:T(1,128)S(1)}, u32[]{:S(2)}, u32[]{:S(2)}) async-start(f32[64,1,1280]{2,1,0:T(1,128)} %copy-done.18), calls=%async_computation.10 | async-start | bytes 655360 | tf_op jit(solution)/shard_map/all_to_all | solution.py:296
  226.5 1.9 copy-start.1
  228.3 0.7 copy-start.26
  229.1 0.7 copy-start.30
  229.8 0.7 copy-start.32
  230.5 0.7 copy-start.34
  231.2 0.7 copy-start.36
  231.9 8.8 %copy-start.41 = (f32[1,256]{1,0:T(1,128)S(1)}, f32[1,256]{1,0:T(1,128)}, u32[]{:S(2)}) copy-start(f32[1,256]{1,0:T(1,128)} %copy-done.39) | copy-start | bytes 3076
  231.9 8.8 %copy-start.43 = (f32[1,1024]{1,0:T(1,128)S(1)}, f32[1,1024]{1,0:T(1,128)}, u32[]{:S(2)}) copy-start(f32[1,1024]{1,0:T(1,128)} %copy-done.42) | copy-start | bytes 12292
  231.9 39.9 %copy-start.2 = (f32[256,3072]{1,0:T(8,128)S(1)}, f32[256,3072]{1,0:T(8,128)}, u32[]{:S(2)}) copy-start(f32[256,3072]{1,0:T(8,128)} %copy-done) | copy-start | bytes 9437188
  233.7 1.7 copy-start.11
  259.4 12.4 %all-to-all-start.12 = ((f32[12,1,256]{2,1,0:T(1,128)}), f32[12,1,256]{2,1,0:T(1,128)S(1)}, u32[]{:S(2)}, u32[]{:S(2)}) async-start(f32[12,1,256]{2,1,0:T(1,128)} %get-tuple-element.111), calls=%async_computation.12 | async-start | bytes 24576 | tf_op jit(solution)/shard_map/all_to_all | solution.py:296
  271.8 1.9 copy-start.12
  273.6 1.4 copy-start.15
  275.1 0.9 copy-start.20
  (6 other events, 3.4 us)
Sparse Core Ops, SparseCore 0:
  10.4 64.2 all-gather.1
  134.2 51.5 reduce-scatter.1

commit v2 on v0

v2 whole, which is shorter than its diff:
```python
import functools

import jax
import jax.numpy as jnp
from jax import lax
from jax.experimental import pallas as pl
from jax.experimental.pallas import tpu as pltpu
from jax.sharding import PartitionSpec as P

sharpness = 4.0
relax_power = 0.7

LANES = 128
F32 = jnp.float32
BF16 = jnp.bfloat16


def call(body, outs, args, name, smem=0, flops=0):
    specs = [pl.BlockSpec(memory_space=pltpu.SMEM)] * smem
    specs += [pl.BlockSpec(memory_space=pltpu.VMEM)] * (len(args) - smem)
    moved = sum(a.size * a.dtype.itemsize for a in (*args, *outs))
    return pl.pallas_call(
        body,
        out_shape=outs,
        in_specs=specs,
        out_specs=[pl.BlockSpec(memory_space=pltpu.VMEM)] * len(outs),
        compiler_params=pltpu.CompilerParams(vmem_limit_bytes=24 * 2**20),
        cost_estimate=pl.CostEstimate(flops=flops, bytes_accessed=moved, transcendentals=0),
        name=name,
    )(*args)


def f32(*shape):
    return jax.ShapeDtypeStruct(shape, F32)


def tiles(size, width):
    return [slice(start, start + width) for start in range(0, size, width)]


def down(row, width=LANES):
    return jnp.transpose(jnp.broadcast_to(row, (width, row.shape[1])))


def flat(sums):
    return jnp.sum(jnp.transpose(sums), axis=0, keepdims=True)


def copies(row, count):
    return jnp.broadcast_to(row[None], (count,) + row.shape)


def parts(value):
    high = value.astype(BF16)
    return high, (value - high.astype(F32)).astype(BF16)


def rows_of(kernel_ref, weight):
    sums = 0.0
    for at in tiles(kernel_ref.shape[1], LANES):
        sums = sums + kernel_ref[:, at] * weight(at)
    return flat(sums)


def received(ref, start, stop):
    return jnp.sum(ref[:, :, start:stop], axis=0)


V, Y, TARGET, DY = (0, 1, 2), (3, 4), 5, (3, 4, 5)
U, DX, PLAIN = (0, 1, 2), (None, 4, 3), 8


def carry(old_ref, new_ref):
    new_ref[...] = old_ref[...]


def put(ref, row, value):
    ref[row : row + 1, :] = value


def get(ref, row, at=slice(None)):
    return ref[row : row + 1, at]


def exponential(left, right):
    logits = lax.dot_general(left, right, (((1,), (1,)), ((), ())), preferred_element_type=F32)
    return jnp.exp(sharpness * logits)


def start_body(features_ref, prototypes_ref, counts_ref, kernel_ref, cols_ref, out_ref):
    rows = features_ref.shape[0]
    width = 512
    left = features_ref[...]
    sums, plain = 0.0, 0.0
    for at in tiles(prototypes_ref.shape[0], width):
        right = prototypes_ref[at, :]
        block = exponential(left, right)
        kernel_ref[:, at] = block
        for inner in tiles(width, LANES):
            sums = sums + block[:, inner]
        plain = plain + product(block, right)
    out_ref[:, :, :rows] = copies(flat(sums), out_ref.shape[0])
    scatter_rows(sharpness * plain, out_ref, rows + LANES)
    counts = counts_ref[...].astype(F32)
    cols_ref[...] = jnp.zeros_like(cols_ref)
    put(cols_ref, TARGET, counts)
    total = jnp.sum(counts, axis=1, keepdims=True)
    out_ref[:, :, rows : rows + LANES] = jnp.broadcast_to(total[None], (out_ref.shape[0], 1, LANES))


def column_sums(kernel_ref, row, out_ref):
    columns = kernel_ref.shape[1]
    count = out_ref.shape[0]
    wide = down(row)
    for at in tiles(columns, LANES):
        out_ref[:, :, at] = copies(jnp.sum(kernel_ref[:, at] * wide, axis=0, keepdims=True), count)
    out_ref[:, :, columns:] = copies(row, count)


def columns_first_body(samples_all, x_ref, kernel_ref, cols_ref, cols_out, rws_out, every_out, out_ref):
    rows = kernel_ref.shape[0]
    u = 1.0 / received(x_ref, 0, rows)
    column_sums(kernel_ref, u, out_ref)
    total = received(x_ref, rows, rows + LANES)[:, :1]
    carry(cols_ref, cols_out)
    put(cols_out, TARGET, samples_all * get(cols_ref, TARGET) / total)
    rws_out[...] = jnp.zeros_like(rws_out)
    put(rws_out, U[0], u)
    for i, at in enumerate(tiles(x_ref.shape[2] - rows - LANES, rows)):
        put(rws_out, PLAIN + i, received(x_ref, rows + LANES + at.start, rows + LANES + at.stop))
    every_out[...] = jnp.zeros_like(every_out)


def columns_body(step, x_ref, kernel_ref, rws_ref, rws_out, out_ref):
    u = 1.0 / received(x_ref, 0, kernel_ref.shape[0])
    carry(rws_ref, rws_out)
    put(rws_out, U[step], u)
    column_sums(kernel_ref, u, out_ref)


def columns_last_body(step, protos_all, x_ref, kernel_ref, cotangent_ref, rws_ref, rws_out, out_ref):
    rows, columns = kernel_ref.shape
    count = out_ref.shape[0]
    u = 1.0 / received(x_ref, 0, rows)
    carry(rws_ref, rws_out)
    put(rws_out, U[step], u)
    wide = down(u)
    for at in tiles(columns, LANES):
        weighted = kernel_ref[:, at] * wide
        out_ref[:, :, at] = copies(jnp.sum(weighted, axis=0, keepdims=True), count)
        weighted = weighted * cotangent_ref[:, at].astype(F32)
        later = slice(columns + at.start, columns + at.stop)
        out_ref[:, :, later] = copies(protos_all * jnp.sum(weighted, axis=0, keepdims=True), count)
    out_ref[:, :, 2 * columns :] = copies(u, count)


def spread(ref, every_ref, every_out, row, start):
    carry(every_ref, every_out)
    rows = every_out.shape[1] // ref.shape[0]
    for i in range(ref.shape[0]):
        every_out[row : row + 1, i * rows : (i + 1) * rows] = ref[i, :, start : start + rows]


def relaxed(y, cols_ref):
    return jnp.exp(relax_power * jnp.log(get(cols_ref, TARGET) / y))


def rows_body(step, y_ref, kernel_ref, cols_ref, every_ref, cols_out, every_out, out_ref):
    columns = kernel_ref.shape[1]
    y = received(y_ref, 0, columns)
    carry(cols_ref, cols_out)
    put(cols_out, Y[step], y)
    put(cols_out, V[step], relaxed(y, cols_ref))
    spread(y_ref, every_ref, every_out, U[step], columns)
    out_ref[...] = copies(rows_of(kernel_ref, lambda at: get(cols_out, V[step], at)), out_ref.shape[0])


def rows_last_body(step, protos_all, y_ref, kernel_ref, cotangent_ref, cols_ref, every_ref, cols_out, every_out, out_ref):
    columns = kernel_ref.shape[1]
    y = received(y_ref, 0, columns)
    v = relaxed(y, cols_ref)
    carry(cols_ref, cols_out)
    put(cols_out, V[step], v)
    put(cols_out, DY[step], -relax_power * received(y_ref, columns, 2 * columns) * v / y)
    spread(y_ref, every_ref, every_out, U[step], 2 * columns)

    def weight(at):
        return protos_all * cotangent_ref[:, at].astype(F32) * get(cols_out, V[step], at) + get(cols_out, DY[step], at)

    out_ref[...] = copies(rows_of(kernel_ref, weight), out_ref.shape[0])


def back_columns_body(step, du_ref, kernel_ref, rws_ref, rws_out, out_ref):
    u = get(rws_ref, U[step])
    dx = -received(du_ref, 0, kernel_ref.shape[0]) * u * u
    carry(rws_ref, rws_out)
    put(rws_out, DX[step], dx)
    column_sums(kernel_ref, dx, out_ref)


def column_step(step, dv_ref, cols_ref, every_ref, cols_out, every_out):
    columns = cols_ref.shape[1]
    carry(cols_ref, cols_out)
    dy = -relax_power * received(dv_ref, 0, columns) * get(cols_ref, V[step]) / get(cols_ref, Y[step])
    put(cols_out, DY[step], dy)
    spread(dv_ref, every_ref, every_out, DX[step + 1], columns)


def back_rows_body(step, dv_ref, kernel_ref, cols_ref, every_ref, cols_out, every_out, out_ref):
    column_step(step, dv_ref, cols_ref, every_ref, cols_out, every_out)
    out_ref[...] = copies(rows_of(kernel_ref, lambda at: get(cols_out, DY[step], at)), out_ref.shape[0])


def scatter_rows(value, out_ref, start):
    count = out_ref.shape[0]
    width = value.shape[1]
    for r in range(value.shape[0] // count):
        block = value[r * count : (r + 1) * count, :]
        out_ref[:, :, start + r * width : start + (r + 1) * width] = block[:, None, :]


def product(value, right):
    high, low = parts(value)
    return jnp.dot(high, right, preferred_element_type=F32) + jnp.dot(low, right, preferred_element_type=F32)


def cotangent_products_body(
    protos_all, kernel_ref, cotangent_ref, features_ref, prototypes_ref, cols_ref, rws_ref, weighted_ref, known_ref
):
    width = 256
    u3 = down(get(rws_ref, U[2]), width)
    features = features_ref[...]
    rows = (((0,), (0,)), ((), ()))
    total = 0.0
    for at in tiles(kernel_ref.shape[1], width):
        block = kernel_ref[:, at] * u3
        weighted = protos_all * cotangent_ref[:, at].astype(F32) * block
        high, low = parts(weighted)
        weighted_ref[at, :] = lax.dot_general(high, features, rows, preferred_element_type=F32) + lax.dot_general(
            low, features, rows, preferred_element_type=F32
        )
        known = weighted * get(cols_ref, V[2], at) + block * get(cols_ref, DY[2], at)
        total = total + product(known, prototypes_ref[at, :])
    known_ref[...] = total


def last_rows_body(
    dv_ref, kernel_ref, prototypes_ref, known_ref, cols_ref, rws_ref, every_ref, cols_out, every_out, out_ref
):
    rows, columns = kernel_ref.shape
    column_step(0, dv_ref, cols_ref, every_ref, cols_out, every_out)
    width = 256
    u1, u2, dx2, dx3 = (down(get(rws_ref, row), width) for row in (U[0], U[1], DX[1], DX[2]))
    sums, total = 0.0, known_ref[...]
    for at in tiles(columns, width):
        block = kernel_ref[:, at]
        dy1 = get(cols_out, DY[0], at)
        weighted = block * dy1
        for inner in tiles(width, LANES):
            sums = sums + weighted[:, inner]
        inner = u1 * dy1 + u2 * get(cols_out, DY[1], at) + dx2 * get(cols_out, V[0], at) + dx3 * get(cols_out, V[1], at)
        total = total + product(block * inner, prototypes_ref[at, :])
    out_ref[:, :, :rows] = copies(flat(sums), out_ref.shape[0])
    scatter_rows(sharpness * total, out_ref, rows)


def finish_rows_body(place_ref, du_ref, rws_ref, dx_out_ref, out_ref):
    rows = rws_ref.shape[1]
    u = get(rws_ref, U[0])
    dx = -received(du_ref, 0, rows) * u * u
    dx_out_ref[...] = copies(dx, dx_out_ref.shape[0])
    count = out_ref.shape[0]
    mine = received(du_ref, rows, du_ref.shape[2])
    width = mine.shape[1] * count // rows
    lane = lax.broadcasted_iota(jnp.int32, dx.shape, 1)
    for r in range(rows // count):
        at = slice(r * width, (r + 1) * width)
        value = jnp.sum(jnp.where(lane == r * count + place_ref[0], dx, 0.0), axis=1, keepdims=True)
        out_ref[:, :, at] = copies(mine[:, at] + value * get(rws_ref, PLAIN + r), count)


def own_rows(place_ref, size):
    return pl.ds(pl.multiple_of(place_ref[0] * size, size), size)


def known_columns_body(place_ref, prototypes_ref, features_ref, cols_ref, every_ref, out_ref):
    own, samples = out_ref.shape
    left = prototypes_ref[own_rows(place_ref, own), :]
    mine = cols_ref[:, own_rows(place_ref, own)]
    width = 256
    v1, v2, dy1, dy2, dy3 = (down(mine[row : row + 1, :], width) for row in (V[0], V[1], DY[0], DY[1], DY[2]))
    for at in tiles(samples, width):
        inner = get(every_ref, U[2], at) * dy3 + get(every_ref, DX[2], at) * v2
        inner = inner + get(every_ref, U[1], at) * dy2 + get(every_ref, DX[1], at) * v1 + get(every_ref, U[0], at) * dy1
        out_ref[:, at] = inner * exponential(left, features_ref[at, :])


def finish_columns_body(place_ref, dx_ref, known_ref, prototypes_ref, features_ref, cols_ref, weighted_ref, out_ref):
    own = known_ref.shape[0]
    rows = dx_ref.shape[2]
    left = prototypes_ref[own_rows(place_ref, own), :]
    mine = cols_ref[:, own_rows(place_ref, own)]
    total = down(mine[V[2] : V[2] + 1, :], out_ref.shape[1]) * weighted_ref[...]
    for i in range(dx_ref.shape[0]):
        at = slice(i * rows, (i + 1) * rows)
        right = features_ref[at, :]
        total = total + product(known_ref[:, at] + exponential(left, right) * dx_ref[i], right)
    out_ref[...] = sharpness * total


def gather_rows_body(ref, out_ref):
    count = ref.shape[0]
    width = out_ref.shape[1]
    for r in range(out_ref.shape[0] // count):
        out_ref[r * count : (r + 1) * count, :] = ref[:, 0, r * width : (r + 1) * width]


def exchange(messages, axis):
    return lax.all_to_all(messages, axis, 0, 0, tiled=True)


def together(*arrays):
    return lax.optimization_barrier(arrays)


def per_device(features, prototypes, prior_counts, cotangent):
    rows, width = features.shape
    columns = prototypes.shape[0]
    samples = lax.axis_size("dp")
    classes = lax.axis_size("cls")
    own = columns // samples
    rows_all = rows * samples
    protos_all = float(columns * classes)
    sliced = rows * width // classes
    counts = prior_counts.reshape(1, columns)
    dp_place = lax.axis_index("dp").astype(jnp.int32).reshape(1)
    cls_place = lax.axis_index("cls").astype(jnp.int32).reshape(1)
    once = 2 * rows * columns
    full = once * width

    cols_t, rws_t, every_t = f32(8, columns), f32(16, rows), f32(8, rows_all)
    to_rows = f32(classes, 1, rows)
    to_columns = f32(samples, 1, columns + rows)
    block_t = f32(rows, columns)

    features_all = lax.all_gather(features, "dp", axis=0, tiled=True)
    kernel, cols, message = call(
        start_body, [block_t, cols_t, f32(classes, 1, rows + LANES + sliced)], [features, prototypes, counts], "start", flops=3 * full
    )
    message = exchange(message, "cls")
    cols, rws, every, message = call(
        functools.partial(columns_first_body, float(rows_all)), [cols_t, rws_t, every_t, to_columns], [message, kernel, cols],
        "columns_first", flops=once,
    )
    message = exchange(message, "dp")
    cols, every, message = call(
        functools.partial(rows_body, 0), [cols_t, every_t, to_rows], [message, kernel, cols, every], "rows_0", flops=once
    )
    message = exchange(message, "cls")
    rws, message = call(functools.partial(columns_body, 1), [rws_t, to_columns], [message, kernel, rws], "columns_1", flops=once)
    message = exchange(message, "dp")
    cols, every, message = call(
        functools.partial(rows_body, 1), [cols_t, every_t, to_rows], [message, kernel, cols, every], "rows_1", flops=once
    )
    message = exchange(message, "cls")
    rws, message = call(
        functools.partial(columns_last_body, 2, protos_all), [rws_t, f32(samples, 1, 2 * columns + rows)],
        [message, kernel, cotangent, rws], "columns_last", flops=2 * once,
    )
    message = exchange(message, "dp")
    cols, every, message = call(
        functools.partial(rows_last_body, 2, protos_all), [cols_t, every_t, to_rows], [message, kernel, cotangent, cols, every],
        "rows_last", flops=2 * once,
    )

    message, right = together(message, features)
    weighted, known = call(
        functools.partial(cotangent_products_body, protos_all), [f32(columns, width), f32(rows, width)],
        [kernel, cotangent, right, prototypes, cols, rws], "cotangent_products", flops=4 * full,
    )
    message, weighted, known = together(exchange(message, "cls"), weighted, known)
    weighted = lax.psum_scatter(weighted, "dp", scatter_dimension=0, tiled=True)
    rws, message = call(functools.partial(back_columns_body, 2), [rws_t, to_columns], [message, kernel, rws], "back_columns_2", flops=once)
    message = exchange(message, "dp")
    cols, every, message = call(
        functools.partial(back_rows_body, 1), [cols_t, every_t, to_rows], [message, kernel, cols, every], "back_rows_1", flops=once
    )
    message = exchange(message, "cls")
    rws, message = call(functools.partial(back_columns_body, 1), [rws_t, to_columns], [message, kernel, rws], "back_columns_1", flops=once)
    message = exchange(message, "dp")
    cols, every, message = call(
        last_rows_body, [cols_t, every_t, f32(classes, 1, rows + sliced)], [message, kernel, prototypes, known, cols, rws, every],
        "last_rows", flops=2 * full,
    )

    message, every, features_all = together(message, every, features_all)
    (known_columns,) = call(
        known_columns_body, [f32(own, rows_all)], [dp_place, prototypes, features_all, cols, every], "known_columns", smem=1, flops=full
    )
    message, known_columns = together(exchange(message, "cls"), known_columns)
    dx_message, message = call(
        finish_rows_body, [f32(samples, 1, rows), f32(classes, 1, sliced)], [cls_place, message, rws], "finish_rows", smem=1
    )
    dx1, message = together(exchange(dx_message, "dp"), message)
    gathered = exchange(message, "cls")
    (prototype_grad,) = call(
        finish_columns_body, [f32(own, width)], [dp_place, dx1, known_columns, prototypes, features_all, cols, weighted],
        "finish_columns", smem=1, flops=3 * full,
    )
    gathered, prototype_grad = together(gathered, prototype_grad)
    (feature_grad,) = call(gather_rows_body, [f32(rows, width)], [gathered], "gather_rows")
    return (feature_grad, prototype_grad)


def solution(mesh):
    return jax.shard_map(
        per_device,
        mesh=mesh,
        in_specs=(P("dp", None), P("cls", None), P("cls"), P("dp", "cls")),
        out_specs=(P("dp", None), P(("cls", "dp"), None)),
        check_vma=False,
    )
```

time: 1230 us -> 272 us (0.22)
  blocking collectives: 964 us -> 183 us
  waiting for transfers between devices: 187 us -> 15.8 us
  matrix products: 52.1 us -> 0 us
  starting transfers between devices: 0.08 us -> 19.5 us
  local copies, waits for them, and re-layouts: 3.36 us -> 20.8 us
  Pallas kernels: 0 us -> 16.8 us
    psum x11 -> x0, blocking collectives: 964 us -> none  [the longest x6 811 us: row_total(): return lax.psum(partial_rows, 'cls')]
    psum x1 -> x0, waiting for transfers between devices: 187 us -> none  [per_device(): lax.psum(jnp.dot(dlogits, prototypes, preferred_element_type=jnp.float32)...]
    all_to_all x0 -> x10, blocking collectives: none -> 183 us  [exchange(): return lax.all_to_all(messages, axis, 0, 0, tiled=True)]
    dot_general x16 -> x0, matrix products: 52.1 us -> none  [the longest x7 27.5 us: matvec(): return jnp.dot(kernel, vector, precision=lax.Precision.HIGHEST)]
    all_to_all x0 -> x3, starting transfers between devices: none -> 19.2 us  [exchange(): return lax.all_to_all(messages, axis, 0, 0, tiled=True)]
    unnamed x15 -> x52, local copies, waits for them, and re-layouts: 3.36 us -> 20.8 us
    pallas_call x0 -> x16, Pallas kernels: none -> 16.8 us  [call(): pl.pallas_call(body, out_shape=outs, in_specs=specs, out_specs=[pl.BlockS...]
    all_to_all x0 -> x3, waiting for transfers between devices: none -> 15.1 us  [exchange(): return lax.all_to_all(messages, axis, 0, 0, tiled=True)]
  transfers between devices with their start and end apart: 2 -> 5, of which waited for: 1 -> 3; matrix products, arithmetic and copies ran while one was open for 0% -> 0% of each run, Pallas kernels for 0% -> 6%
where the time goes in v2:
time: 272 us; the launch traced here: 270 us
  blocking collectives  183 us (67%)
  local copies, waits for them, and re-layouts  20.8 us (8%)
  starting transfers between devices  19.5 us (7%)
  Pallas kernels  16.8 us (6%)
  waiting for transfers between devices  15.8 us (6%)
  between operations  14.3 us (5%)
    all_to_all x10, blocking collectives, exchange(): return lax.all_to_all(messages, axis, 0, 0, tiled=True)  183 us
    unnamed x52, local copies, waits for them, and re-layouts  20.8 us
    all_to_all x3, starting transfers between devices, exchange(): return lax.all_to_all(messages, axis, 0, 0, tiled=True)  19.2 us
    pallas_call x16, Pallas kernels, call(): pl.pallas_call(body, out_shape=outs, in_specs=specs, out_specs=[pl.BlockS...  16.8 us
    all_to_all x3, waiting for transfers between devices, exchange(): return lax.all_to_all(messages, axis, 0, 0, tiled=True)  15.1 us
  transfers between devices with their start and end apart: 5, of which 3 were waited for; matrix products, arithmetic and copies ran while one was open for 0% of the time, Pallas kernels for 6%

profile of v2, /device:TPU:1, one launch (start us, length us, event | category | flops | bytes accessed | tf_op | source)
XLA Modules:
  0.0 270.5 jit_solution(17018720395390767857)
XLA Ops:
  7.2 0.7 all-gather.2.cloned.1.call-update
  7.9 1.4 copy-done
  9.3 0.9 copy-done.12
  10.2 0.7 copy-done.25
  10.9 2.1 start.1
  13.0 28.4 %all_to_all.65.x_ref = f32[64,1,1408]{2,1,0:T(1,128)S(1)} all-to-all(f32[64,1,1408]{2,1,0:T(1,128)S(1)} %get-tuple-element.50), channel_id=1, replica_groups=mesh['dp'=12,'cls'=64] {'cls'}, dimensions={0} | all-to-all | bytes 720896 | tf_op jit(solution)/shard_map/all_to_all | solution.py:319
  41.4 0.6 columns_first.1
  42.0 26.5 %all_to_all.66.y_ref = f32[12,1,3328]{2,1,0:T(1,128)S(1)} all-to-all(f32[12,1,3328]{2,1,0:T(1,128)S(1)} %get-tuple-element.53), channel_id=1, replica_groups=mesh['dp'=12,'cls'=64] {'dp'}, dimensions={0} | all-to-all | bytes 319488 | tf_op jit(solution)/shard_map/all_to_all | solution.py:319
  68.5 0.5 rows_0.1
  69.0 16.7 %all_to_all.67.x_ref = f32[64,1,256]{2,1,0:T(1,128)S(1)} all-to-all(f32[64,1,256]{2,1,0:T(1,128)S(1)} %get-tuple-element.56), channel_id=1, replica_groups=mesh['dp'=12,'cls'=64] {'cls'}, dimensions={0} | all-to-all | bytes 131072 | tf_op jit(solution)/shard_map/all_to_all | solution.py:319
  86.2 14.7 %all_to_all.68.y_ref = f32[12,1,3328]{2,1,0:T(1,128)S(1)} all-to-all(f32[12,1,3328]{2,1,0:T(1,128)S(1)} %get-tuple-element.58), channel_id=1, replica_groups=mesh['dp'=12,'cls'=64] {'dp'}, dimensions={0} | all-to-all | bytes 319488 | tf_op jit(solution)/shard_map/all_to_all | solution.py:319
  100.9 0.5 rows_1.1
  101.4 15.1 %all_to_all.69.x_ref = f32[64,1,256]{2,1,0:T(1,128)S(1)} all-to-all(f32[64,1,256]{2,1,0:T(1,128)S(1)} %get-tuple-element.61), channel_id=1, replica_groups=mesh['dp'=12,'cls'=64] {'cls'}, dimensions={0} | all-to-all | bytes 131072 | tf_op jit(solution)/shard_map/all_to_all | solution.py:319
  116.5 0.8 columns_last.1
  117.3 19.1 %all_to_all.70.y_ref = f32[12,1,6400]{2,1,0:T(1,128)S(1)} all-to-all(f32[12,1,6400]{2,1,0:T(1,128)S(1)} %get-tuple-element.63), channel_id=1, replica_groups=mesh['dp'=12,'cls'=64] {'dp'}, dimensions={0} | all-to-all | bytes 614400 | tf_op jit(solution)/shard_map/all_to_all | solution.py:319
  136.4 0.9 rows_last.1
  137.3 0.6 copy-done.24
  137.9 6.1 %all-to-all-start.6 = ((f32[64,1,256]{2,1,0:T(1,128)}), f32[64,1,256]{2,1,0:T(1,128)S(1)}, u32[]{:S(2)}, u32[]{:S(2)}) async-start(f32[64,1,256]{2,1,0:T(1,128)} %copy-done.24), calls=%async_computation.6 | async-start | bytes 131072 | tf_op jit(solution)/shard_map/all_to_all | solution.py:319
  144.3 1.4 copy-done.1
  145.7 1.4 copy-done.6
  147.1 2.2 cotangent_products.1
  149.3 1.6 copy-done.11
  150.9 0.7 copy-done.19
  151.6 2.5 all-to-all-done.6.du_ref
  154.6 14.7 %all_to_all.71.dv_ref = f32[12,1,3328]{2,1,0:T(1,128)S(1)} all-to-all(f32[12,1,3328]{2,1,0:T(1,128)S(1)} %get-tuple-element.74), channel_id=1, replica_groups=mesh['dp'=12,'cls'=64] {'dp'}, dimensions={0} | all-to-all | bytes 319488 | tf_op jit(solution)/shard_map/all_to_all | solution.py:319
  169.3 0.4 back_rows_1.1
  169.8 19.6 %all_to_all.72.du_ref = f32[64,1,256]{2,1,0:T(1,128)S(1)} all-to-all(f32[64,1,256]{2,1,0:T(1,128)S(1)} %get-tuple-element.76), channel_id=1, replica_groups=mesh['dp'=12,'cls'=64] {'cls'}, dimensions={0} | all-to-all | bytes 131072 | tf_op jit(solution)/shard_map/all_to_all | solution.py:319
  189.8 17.0 %all_to_all.73.dv_ref = f32[12,1,3328]{2,1,0:T(1,128)S(1)} all-to-all(f32[12,1,3328]{2,1,0:T(1,128)S(1)} %get-tuple-element.78), channel_id=1, replica_groups=mesh['dp'=12,'cls'=64] {'dp'}, dimensions={0} | all-to-all | bytes 319488 | tf_op jit(solution)/shard_map/all_to_all | solution.py:319
  206.8 1.8 last_rows.1
  208.7 0.6 copy-done.14
  209.3 0.7 copy-done.17
  210.1 0.6 copy-done.22
  210.7 6.7 %all-to-all-start.10 = ((f32[64,1,1280]{2,1,0:T(1,128)}), f32[64,1,1280]{2,1,0:T(1,128)S(1)}, u32[]{:S(2)}, u32[]{:S(2)}) async-start(f32[64,1,1280]{2,1,0:T(1,128)} %copy-done.17), calls=%async_computation.10 | async-start | bytes 655360 | tf_op jit(solution)/shard_map/all_to_all | solution.py:319
  217.4 1.4 copy-done.3
  218.8 1.4 copy-done.9
  220.3 0.9 copy-done.15
  221.1 0.9 copy-done.23
  222.0 1.6 known_columns.1.known_ref
  223.7 1.7 copy-done.7
  225.4 6.1 %all-to-all-done.10.du_ref = f32[64,1,1280]{2,1,0:T(1,128)S(1)} async-done(((f32[64,1,1280]{2,1,0:T(1,128)}), f32[64,1,1280]{2,1,0:T(1,128)S(1)}, u32[]{:S(2)}, u32[]{:S(2)}) %all-to-all-start.10) | async-done | bytes 327712 | tf_op jit(solution)/shard_map/all_to_all | solution.py:319
  231.8 11.5 %all_to_all.74.dx_ref = f32[12,1,256]{2,1,0:T(1,128)S(1)} all-to-all(f32[12,1,256]{2,1,0:T(1,128)S(1)} %get-tuple-element.90), channel_id=1, replica_groups=mesh['dp'=12,'cls'=64] {'dp'}, dimensions={0} | all-to-all | bytes 24576 | tf_op jit(solution)/shard_map/all_to_all | solution.py:319
  243.3 6.4 %all-to-all-start.12 = ((f32[64,1,1024]{2,1,0:T(1,128)}), f32[64,1,1024]{2,1,0:T(1,128)S(1)}, u32[]{:S(2)}, u32[]{:S(2)}) async-start(f32[64,1,1024]{2,1,0:T(1,128)} %copy-done.21), calls=%async_computation.12 | async-start | bytes 524288 | tf_op jit(solution)/shard_map/all_to_all | solution.py:319
  249.8 1.9 copy-done.8
  251.7 0.9 copy-done.16
  252.6 0.9 copy-done.18
  253.5 3.0 %finish_columns.1 = f32[256,256]{1,0:T(8,128)} custom-call(s32[1]{0:T(128)} %bitcast.2.place_ref, f32[12,1,256]{2,1,0:T(1,128)S(1)} %all_to_all.74.dx_ref, f32[256,3072]{1,0:T(8,128)S(1)} %copy-done.8, bf16[3072,256]{1,0:T(8,128)(2,1)S(1)} %copy-done.4, bf16[3072,256]{1,0:T(8,128)(2,1)S(1)} %copy-done.10, f32[8,3072]{1,0:T(8,128)S(1)} %copy-done.16, ...), custom_call_target="tpu_custom_call" | custom-call | flops 1207959552 | bytes 6926340 | tf_op jit(solution)/shard_map/finish_columns/pallas_call | solution.py:22
  256.5 6.4 %all-to-all-done.12.ref = f32[64,1,1024]{2,1,0:T(1,128)S(1)} async-done(((f32[64,1,1024]{2,1,0:T(1,128)}), f32[64,1,1024]{2,1,0:T(1,128)S(1)}, u32[]{:S(2)}, u32[]{:S(2)}) %all-to-all-start.12) | async-done | bytes 262176 | tf_op jit(solution)/shard_map/all_to_all | solution.py:319
  262.9 0.8 gather_rows.1
  (42 shorter events, 2.0 us)
Async XLA Ops:
  7.2 203.5 %all-gather.2.cloned.1.call-start = ((), (), s32[]{:S(2)}) async-start(), calls=%async_computation.14 | async-start | bytes 1703936 | tf_op jit(solution)/shard_map/all_gather | solution.py:346
  7.9 1.4 copy-start
  9.3 0.9 copy-start.12
  10.2 0.7 copy-start.25
  85.7 30.8 %copy-start.5 = (bf16[256,3072]{1,0:T(8,128)(2,1)S(1)}, bf16[256,3072]{1,0:T(8,128)(2,1)}, u32[]{:S(2)}) copy-start(bf16[256,3072]{1,0:T(8,128)(2,1)} %cotangent_ref.5) | copy-start | bytes 4718596
  117.3 27.0 %copy-start.13 = (bf16[256,256]{1,0:T(8,128)(2,1)S(1)}, bf16[256,256]{1,0:T(8,128)(2,1)}, u32[]{:S(2)}) copy-start(bf16[256,256]{1,0:T(8,128)(2,1)} %features_ref.2) | copy-start | bytes 393220
  137.3 0.6 copy-start.24
  137.9 16.2 %all-to-all-start.6 = ((f32[64,1,256]{2,1,0:T(1,128)}), f32[64,1,256]{2,1,0:T(1,128)S(1)}, u32[]{:S(2)}, u32[]{:S(2)}) async-start(f32[64,1,256]{2,1,0:T(1,128)} %copy-done.24), calls=%async_computation.6 | async-start | bytes 131072 | tf_op jit(solution)/shard_map/all_to_all | solution.py:319
  144.0 105.7 %reduce-scatter.2.cloned.1.call-start = ((), (), s32[]{:S(2)}) async-start(), calls=%async_computation.15 | async-start | bytes 3407872 | tf_op jit(solution)/shard_map/reduce_scatter | solution.py:382
  144.2 1.4 copy-start.1
  145.7 1.4 copy-start.6
  149.3 1.6 copy-start.11
  150.9 0.7 copy-start.19
  169.3 37.5 %copy-start.2 = (bf16[3072,256]{1,0:T(8,128)(2,1)S(1)}, bf16[3072,256]{1,0:T(8,128)(2,1)}, u32[]{:S(2)}) copy-start(bf16[3072,256]{1,0:T(8,128)(2,1)} %prototypes_ref.9) | copy-start | bytes 4718596
  169.3 37.5 %copy-start.20 = (f32[256,256]{1,0:T(8,128)S(1)}, f32[256,256]{1,0:T(8,128)}, u32[]{:S(2)}) copy-start(f32[256,256]{1,0:T(8,128)} %copy-done.19) | copy-start | bytes 786436
  208.7 0.6 copy-start.14
  209.3 0.7 copy-start.17
  210.1 0.6 copy-start.22
  210.7 20.8 %all-to-all-start.10 = ((f32[64,1,1280]{2,1,0:T(1,128)}), f32[64,1,1280]{2,1,0:T(1,128)S(1)}, u32[]{:S(2)}, u32[]{:S(2)}) async-start(f32[64,1,1280]{2,1,0:T(1,128)} %copy-done.17), calls=%async_computation.10 | async-start | bytes 655360 | tf_op jit(solution)/shard_map/all_to_all | solution.py:319
  217.4 1.4 copy-start.3
  218.8 1.4 copy-start.9
  220.2 0.9 copy-start.15
  221.1 0.9 copy-start.23
  222.0 27.7 %copy-start.4 = (bf16[3072,256]{1,0:T(8,128)(2,1)S(1)}, bf16[3072,256]{1,0:T(8,128)(2,1)}, u32[]{:S(2)}) copy-start(bf16[3072,256]{1,0:T(8,128)(2,1)} %prototypes_ref.9) | copy-start | bytes 4718596
  222.0 27.7 %copy-start.10 = (bf16[3072,256]{1,0:T(8,128)(2,1)S(1)}, bf16[3072,256]{1,0:T(8,128)(2,1)}, u32[]{:S(2)}) copy-start(bf16[3072,256]{1,0:T(8,128)(2,1)} %all-gather.2.cloned.1.call-done.features_ref) | copy-start | bytes 4718596
  223.7 1.7 copy-start.7
  231.8 11.5 %copy-start.21 = (f32[64,1,1024]{2,1,0:T(1,128)}, f32[64,1,1024]{2,1,0:T(1,128)S(1)}, u32[]{:S(2)}) copy-start(f32[64,1,1024]{2,1,0:T(1,128)S(1)} %get-tuple-element.92) | copy-start | bytes 786436
  243.3 19.6 %all-to-all-start.12 = ((f32[64,1,1024]{2,1,0:T(1,128)}), f32[64,1,1024]{2,1,0:T(1,128)S(1)}, u32[]{:S(2)}, u32[]{:S(2)}) async-start(f32[64,1,1024]{2,1,0:T(1,128)} %copy-done.21), calls=%async_computation.12 | async-start | bytes 524288 | tf_op jit(solution)/shard_map/all_to_all | solution.py:319
  249.8 1.9 copy-start.8
  251.7 0.9 copy-start.16
  252.6 0.9 copy-start.18
Sparse Core Ops, SparseCore 0:
  10.4 63.9 all-gather.1
  154.3 54.5 reduce-scatter.1

commit v3 on v2

--- a/solution.py
+++ b/solution.py
@@ -108,13 +108,34 @@
     out_ref[:, :, rows : rows + LANES] = jnp.broadcast_to(total[None], (out_ref.shape[0], 1, LANES))
 
 
+def message_rows(columns, rows):
+    return -(-(columns + 2 * rows) // LANES // 16) * 16
+
+
 def column_sums(kernel_ref, row, out_ref):
     columns = kernel_ref.shape[1]
-    count = out_ref.shape[0]
     wide = down(row)
-    for at in tiles(columns, LANES):
-        out_ref[:, :, at] = copies(jnp.sum(kernel_ref[:, at] * wide, axis=0, keepdims=True), count)
-    out_ref[:, :, columns:] = copies(row, count)
+    values = [jnp.sum(kernel_ref[:, at] * wide, axis=0, keepdims=True) for at in tiles(columns, LANES)]
+    for part in parts(row):
+        values += [part.astype(F32)[:, at] for at in tiles(row.shape[1], LANES)]
+    spare = out_ref.shape[1] - len(values)
+    if spare:
+        values.append(jnp.zeros((spare, LANES), F32))
+    out_ref[...] = copies(jnp.concatenate(values, axis=0).astype(BF16), out_ref.shape[0])
+
+
+def received_columns(ref, columns, every_ref, every_out, row):
+    values = ref[...].astype(F32)
+    sums = jnp.sum(values, axis=0)
+    carry(every_ref, every_out)
+    first = columns // LANES
+    count = every_out.shape[1] // ref.shape[0] // LANES
+    samples = values[:, first : first + count, :] + values[:, first + count : first + 2 * count, :]
+    for i in range(ref.shape[0]):
+        for j in range(count):
+            at = (i * count + j) * LANES
+            every_out[row : row + 1, at : at + LANES] = samples[i, j : j + 1, :]
+    return jnp.concatenate([sums[i : i + 1, :] for i in range(first)], axis=1)
 
 
 def columns_first_body(samples_all, x_ref, kernel_ref, cols_ref, cols_out, rws_out, every_out, out_ref):
@@ -166,12 +187,10 @@
 
 
 def rows_body(step, y_ref, kernel_ref, cols_ref, every_ref, cols_out, every_out, out_ref):
-    columns = kernel_ref.shape[1]
-    y = received(y_ref, 0, columns)
+    y = received_columns(y_ref, kernel_ref.shape[1], every_ref, every_out, U[step])
     carry(cols_ref, cols_out)
     put(cols_out, Y[step], y)
     put(cols_out, V[step], relaxed(y, cols_ref))
-    spread(y_ref, every_ref, every_out, U[step], columns)
     out_ref[...] = copies(rows_of(kernel_ref, lambda at: get(cols_out, V[step], at)), out_ref.shape[0])
 
 
@@ -199,11 +218,9 @@
 
 
 def column_step(step, dv_ref, cols_ref, every_ref, cols_out, every_out):
-    columns = cols_ref.shape[1]
+    dv = received_columns(dv_ref, cols_ref.shape[1], every_ref, every_out, DX[step + 1])
     carry(cols_ref, cols_out)
-    dy = -relax_power * received(dv_ref, 0, columns) * get(cols_ref, V[step]) / get(cols_ref, Y[step])
-    put(cols_out, DY[step], dy)
-    spread(dv_ref, every_ref, every_out, DX[step + 1], columns)
+    put(cols_out, DY[step], -relax_power * dv * get(cols_ref, V[step]) / get(cols_ref, Y[step]))
 
 
 def back_rows_body(step, dv_ref, kernel_ref, cols_ref, every_ref, cols_out, every_out, out_ref):
@@ -245,9 +262,10 @@
 
 
 def last_rows_body(
-    dv_ref, kernel_ref, prototypes_ref, known_ref, cols_ref, rws_ref, every_ref, cols_out, every_out, out_ref
+    dv_ref, kernel_ref, prototypes_ref, known_ref, cols_ref, rws_ref, every_ref, both_ref, out_ref
 ):
     rows, columns = kernel_ref.shape
+    cols_out, every_out = both_ref.at[:8, :columns], both_ref.at[8:, : every_ref.shape[1]]
     column_step(0, dv_ref, cols_ref, every_ref, cols_out, every_out)
     width = 256
     u1, u2, dx2, dx3 = (down(get(rws_ref, row), width) for row in (U[0], U[1], DX[1], DX[2]))
@@ -273,18 +291,22 @@
     mine = received(du_ref, rows, du_ref.shape[2])
     width = mine.shape[1] * count // rows
     lane = lax.broadcasted_iota(jnp.int32, dx.shape, 1)
+    values = []
     for r in range(rows // count):
-        at = slice(r * width, (r + 1) * width)
-        value = jnp.sum(jnp.where(lane == r * count + place_ref[0], dx, 0.0), axis=1, keepdims=True)
-        out_ref[:, :, at] = copies(mine[:, at] + value * get(rws_ref, PLAIN + r), count)
+        row = r * count + place_ref[0]
+        value = jnp.sum(jnp.where(lane == row, dx, 0.0), axis=1, keepdims=True)
+        value = mine[:, r * width : (r + 1) * width] + value * get(rws_ref, PLAIN + r)
+        values += [value[:, at] for at in tiles(width, LANES)]
+    out_ref[...] = copies(jnp.concatenate(values, axis=0).astype(BF16), count)
 
 
 def own_rows(place_ref, size):
     return pl.ds(pl.multiple_of(place_ref[0] * size, size), size)
 
 
-def known_columns_body(place_ref, prototypes_ref, features_ref, cols_ref, every_ref, out_ref):
+def known_columns_body(place_ref, prototypes_ref, features_ref, both_ref, out_ref):
     own, samples = out_ref.shape
+    cols_ref, every_ref = both_ref.at[:8, :], both_ref.at[8:, :]
     left = prototypes_ref[own_rows(place_ref, own), :]
     mine = cols_ref[:, own_rows(place_ref, own)]
     width = 256
@@ -295,11 +317,11 @@
         out_ref[:, at] = inner * exponential(left, features_ref[at, :])
 
 
-def finish_columns_body(place_ref, dx_ref, known_ref, prototypes_ref, features_ref, cols_ref, weighted_ref, out_ref):
+def finish_columns_body(place_ref, dx_ref, known_ref, prototypes_ref, features_ref, both_ref, weighted_ref, out_ref):
     own = known_ref.shape[0]
     rows = dx_ref.shape[2]
     left = prototypes_ref[own_rows(place_ref, own), :]
-    mine = cols_ref[:, own_rows(place_ref, own)]
+    mine = both_ref[:8, own_rows(place_ref, own)]
     total = down(mine[V[2] : V[2] + 1, :], out_ref.shape[1]) * weighted_ref[...]
     for i in range(dx_ref.shape[0]):
         at = slice(i * rows, (i + 1) * rows)
@@ -310,9 +332,11 @@
 
 def gather_rows_body(ref, out_ref):
     count = ref.shape[0]
-    width = out_ref.shape[1]
-    for r in range(out_ref.shape[0] // count):
-        out_ref[r * count : (r + 1) * count, :] = ref[:, 0, r * width : (r + 1) * width]
+    values = ref[...].astype(F32)
+    blocks = tiles(out_ref.shape[1], LANES)
+    for i in range(ref.shape[1]):
+        r, at = i // len(blocks), blocks[i % len(blocks)]
+        out_ref[r * count : (r + 1) * count, at] = values[:, i, :]
 
 
 def exchange(messages, axis):
@@ -340,7 +364,7 @@
 
     cols_t, rws_t, every_t = f32(8, columns), f32(16, rows), f32(8, rows_all)
     to_rows = f32(classes, 1, rows)
-    to_columns = f32(samples, 1, columns + rows)
+    to_columns = jax.ShapeDtypeStruct((samples, message_rows(columns, rows), LANES), BF16)
     block_t = f32(rows, columns)
 
     features_all = lax.all_gather(features, "dp", axis=0, tiled=True)
@@ -388,23 +412,24 @@
     message = exchange(message, "cls")
     rws, message = call(functools.partial(back_columns_body, 1), [rws_t, to_columns], [message, kernel, rws], "back_columns_1", flops=once)
     message = exchange(message, "dp")
-    cols, every, message = call(
-        last_rows_body, [cols_t, every_t, f32(classes, 1, rows + sliced)], [message, kernel, prototypes, known, cols, rws, every],
+    both, message = call(
+        last_rows_body, [f32(16, max(columns, rows_all)), f32(classes, 1, rows + sliced)], [message, kernel, prototypes, known, cols, rws, every],
         "last_rows", flops=2 * full,
     )
 
-    message, every, features_all = together(message, every, features_all)
+    message, both, features_all = together(message, both, features_all)
     (known_columns,) = call(
-        known_columns_body, [f32(own, rows_all)], [dp_place, prototypes, features_all, cols, every], "known_columns", smem=1, flops=full
+        known_columns_body, [f32(own, rows_all)], [dp_place, prototypes, features_all, both], "known_columns", smem=1, flops=full
     )
     message, known_columns = together(exchange(message, "cls"), known_columns)
     dx_message, message = call(
-        finish_rows_body, [f32(samples, 1, rows), f32(classes, 1, sliced)], [cls_place, message, rws], "finish_rows", smem=1
+        finish_rows_body, [f32(samples, 1, rows), jax.ShapeDtypeStruct((classes, sliced // LANES, LANES), BF16)],
+        [cls_place, message, rws], "finish_rows", smem=1,
     )
     dx1, message = together(exchange(dx_message, "dp"), message)
     gathered = exchange(message, "cls")
     (prototype_grad,) = call(
-        finish_columns_body, [f32(own, width)], [dp_place, dx1, known_columns, prototypes, features_all, cols, weighted],
+        finish_columns_body, [f32(own, width)], [dp_place, dx1, known_columns, prototypes, features_all, both, weighted],
         "finish_columns", smem=1, flops=3 * full,
     )
     gathered, prototype_grad = together(gathered, prototype_grad)

time: 272 us -> 260 us (0.956)
  blocking collectives: 183 us -> 174 us
    all_to_all x10, blocking collectives: 183 us -> 174 us  [exchange(): return lax.all_to_all(messages, axis, 0, 0, tiled=True)]
    unnamed x52 -> x48, local copies, waits for them, and re-layouts: 20.8 us -> 20 us
where the time goes in v3:
time: 260 us; the launch traced here: 259 us
  blocking collectives  174 us (67%)
  local copies, waits for them, and re-layouts  20 us (8%)
  starting transfers between devices  19.6 us (8%)
  Pallas kernels  16.3 us (6%)
  waiting for transfers between devices  14.5 us (6%)
  between operations  14.3 us (6%)
    all_to_all x10, blocking collectives, exchange(): return lax.all_to_all(messages, axis, 0, 0, tiled=True)  174 us
    unnamed x48, local copies, waits for them, and re-layouts  20 us
    all_to_all x3, starting transfers between devices, exchange(): return lax.all_to_all(messages, axis, 0, 0, tiled=True)  19.4 us
    pallas_call x16, Pallas kernels, call(): pl.pallas_call(body, out_shape=outs, in_specs=specs, out_specs=[pl.BlockS...  16.3 us
    all_to_all x3, waiting for transfers between devices, exchange(): return lax.all_to_all(messages, axis, 0, 0, tiled=True)  13.8 us
  transfers between devices with their start and end apart: 5, of which 3 were waited for; matrix products, arithmetic and copies ran while one was open for 0% of the time, Pallas kernels for 6%

profile of v3, /device:TPU:1, one launch (start us, length us, event | category | flops | bytes accessed | tf_op | source)
XLA Modules:
  0.0 259.3 jit_solution(12780050351676526289)
XLA Ops:
  7.2 0.7 all-gather.2.cloned.1.call-update
  7.9 1.4 copy-done
  9.3 0.9 copy-done.15
  10.2 0.7 copy-done.23
  10.9 2.1 start.1
  13.0 28.4 %all_to_all.65.x_ref = f32[64,1,1408]{2,1,0:T(1,128)S(1)} all-to-all(f32[64,1,1408]{2,1,0:T(1,128)S(1)} %get-tuple-element.49), channel_id=1, replica_groups=mesh['dp'=12,'cls'=64] {'cls'}, dimensions={0} | all-to-all | bytes 720896 | tf_op jit(solution)/shard_map/all_to_all | solution.py:343
  41.4 0.6 columns_first.1
  42.0 24.2 %all_to_all.66.y_ref = bf16[12,32,128]{2,1,0:T(8,128)(2,1)S(1)} all-to-all(bf16[12,32,128]{2,1,0:T(8,128)(2,1)S(1)} %get-tuple-element.52), channel_id=1, replica_groups=mesh['dp'=12,'cls'=64] {'dp'}, dimensions={0} | all-to-all | bytes 196608 | tf_op jit(solution)/shard_map/all_to_all | solution.py:343
  66.5 16.7 %all_to_all.67.x_ref = f32[64,1,256]{2,1,0:T(1,128)S(1)} all-to-all(f32[64,1,256]{2,1,0:T(1,128)S(1)} %get-tuple-element.55), channel_id=1, replica_groups=mesh['dp'=12,'cls'=64] {'cls'}, dimensions={0} | all-to-all | bytes 131072 | tf_op jit(solution)/shard_map/all_to_all | solution.py:343
  83.2 0.4 columns_1.1
  83.6 13.2 %all_to_all.68.y_ref = bf16[12,32,128]{2,1,0:T(8,128)(2,1)S(1)} all-to-all(bf16[12,32,128]{2,1,0:T(8,128)(2,1)S(1)} %get-tuple-element.57), channel_id=1, replica_groups=mesh['dp'=12,'cls'=64] {'dp'}, dimensions={0} | all-to-all | bytes 196608 | tf_op jit(solution)/shard_map/all_to_all | solution.py:343
  97.2 15.1 %all_to_all.69.x_ref = f32[64,1,256]{2,1,0:T(1,128)S(1)} all-to-all(f32[64,1,256]{2,1,0:T(1,128)S(1)} %get-tuple-element.60), channel_id=1, replica_groups=mesh['dp'=12,'cls'=64] {'cls'}, dimensions={0} | all-to-all | bytes 131072 | tf_op jit(solution)/shard_map/all_to_all | solution.py:343
  112.3 0.8 columns_last.1
  113.1 18.0 %all_to_all.70.y_ref = f32[12,1,6400]{2,1,0:T(1,128)S(1)} all-to-all(f32[12,1,6400]{2,1,0:T(1,128)S(1)} %get-tuple-element.62), channel_id=1, replica_groups=mesh['dp'=12,'cls'=64] {'dp'}, dimensions={0} | all-to-all | bytes 614400 | tf_op jit(solution)/shard_map/all_to_all | solution.py:343
  131.1 0.9 rows_last.1
  132.0 0.6 copy-done.22
  132.6 6.8 %all-to-all-start.6 = ((f32[64,1,256]{2,1,0:T(1,128)}), f32[64,1,256]{2,1,0:T(1,128)S(1)}, u32[]{:S(2)}, u32[]{:S(2)}) async-start(f32[64,1,256]{2,1,0:T(1,128)} %copy-done.22), calls=%async_computation.6 | async-start | bytes 131072 | tf_op jit(solution)/shard_map/all_to_all | solution.py:343
  139.7 1.4 copy-done.1
  141.1 1.4 copy-done.6
  142.5 2.2 cotangent_products.1
  144.7 1.6 copy-done.11
  146.3 0.7 copy-done.19
  147.0 2.5 all-to-all-done.6.du_ref
  149.6 0.4 back_columns_2.1
  150.0 13.1 %all_to_all.71.dv_ref = bf16[12,32,128]{2,1,0:T(8,128)(2,1)S(1)} all-to-all(bf16[12,32,128]{2,1,0:T(8,128)(2,1)S(1)} %get-tuple-element.73), channel_id=1, replica_groups=mesh['dp'=12,'cls'=64] {'dp'}, dimensions={0} | all-to-all | bytes 196608 | tf_op jit(solution)/shard_map/all_to_all | solution.py:343
  163.1 0.4 back_rows_1.1
  163.5 19.8 %all_to_all.72.du_ref = f32[64,1,256]{2,1,0:T(1,128)S(1)} all-to-all(f32[64,1,256]{2,1,0:T(1,128)S(1)} %get-tuple-element.75), channel_id=1, replica_groups=mesh['dp'=12,'cls'=64] {'cls'}, dimensions={0} | all-to-all | bytes 131072 | tf_op jit(solution)/shard_map/all_to_all | solution.py:343
  183.3 0.4 back_columns_1.1
  183.7 14.6 %all_to_all.73.dv_ref = bf16[12,32,128]{2,1,0:T(8,128)(2,1)S(1)} all-to-all(bf16[12,32,128]{2,1,0:T(8,128)(2,1)S(1)} %get-tuple-element.77), channel_id=1, replica_groups=mesh['dp'=12,'cls'=64] {'dp'}, dimensions={0} | all-to-all | bytes 196608 | tf_op jit(solution)/shard_map/all_to_all | solution.py:343
  198.3 1.7 last_rows.1
  200.0 0.7 copy-done.12
  200.7 0.7 copy-done.17
  201.4 6.2 %all-to-all-start.10 = ((f32[64,1,1280]{2,1,0:T(1,128)}), f32[64,1,1280]{2,1,0:T(1,128)S(1)}, u32[]{:S(2)}, u32[]{:S(2)}) async-start(f32[64,1,1280]{2,1,0:T(1,128)} %copy-done.17), calls=%async_computation.10 | async-start | bytes 655360 | tf_op jit(solution)/shard_map/all_to_all | solution.py:343
  207.6 1.4 copy-done.3
  209.0 1.4 copy-done.9
  210.4 0.9 copy-done.13
  211.4 1.6 known_columns.1.known_ref
  213.0 1.7 copy-done.7
  214.7 7.0 %all-to-all-done.10.du_ref = f32[64,1,1280]{2,1,0:T(1,128)S(1)} async-done(((f32[64,1,1280]{2,1,0:T(1,128)}), f32[64,1,1280]{2,1,0:T(1,128)S(1)}, u32[]{:S(2)}, u32[]{:S(2)}) %all-to-all-start.10) | async-done | bytes 327712 | tf_op jit(solution)/shard_map/all_to_all | solution.py:343
  221.9 0.6 copy-done.21
  222.6 11.4 %all_to_all.74.dx_ref = f32[12,1,256]{2,1,0:T(1,128)S(1)} all-to-all(f32[12,1,256]{2,1,0:T(1,128)S(1)} %get-tuple-element.88), channel_id=1, replica_groups=mesh['dp'=12,'cls'=64] {'dp'}, dimensions={0} | all-to-all | bytes 24576 | tf_op jit(solution)/shard_map/all_to_all | solution.py:343
  234.0 6.4 %all-to-all-start.12 = ((bf16[64,8,128]{2,1,0:T(8,128)(2,1)}), bf16[64,8,128]{2,1,0:T(8,128)(2,1)S(1)}, u32[]{:S(2)}, u32[]{:S(2)}) async-start(bf16[64,8,128]{2,1,0:T(8,128)(2,1)} %copy-done.21), calls=%async_computation.12 | async-start | bytes 262144 | tf_op jit(solution)/shard_map/all_to_all | solution.py:343
  240.5 1.9 copy-done.8
  242.4 0.9 copy-done.14
  243.4 0.9 copy-done.18
  244.3 3.0 %finish_columns.1 = f32[256,256]{1,0:T(8,128)} custom-call(s32[1]{0:T(128)} %bitcast.2.place_ref, f32[12,1,256]{2,1,0:T(1,128)S(1)} %all_to_all.74.dx_ref, f32[256,3072]{1,0:T(8,128)S(1)} %copy-done.8, bf16[3072,256]{1,0:T(8,128)(2,1)S(1)} %copy-done.4, bf16[3072,256]{1,0:T(8,128)(2,1)S(1)} %copy-done.10, f32[16,3072]{1,0:T(8,128)S(1)} %copy-done.14, ...), custom_call_target="tpu_custom_call" | custom-call | flops 1207959552 | bytes 7024644 | tf_op jit(solution)/shard_map/finish_columns/pallas_call | solution.py:22
  247.3 4.3 %all-to-all-done.12.ref = bf16[64,8,128]{2,1,0:T(8,128)(2,1)S(1)} async-done(((bf16[64,8,128]{2,1,0:T(8,128)(2,1)}), bf16[64,8,128]{2,1,0:T(8,128)(2,1)S(1)}, u32[]{:S(2)}, u32[]{:S(2)}) %all-to-all-start.12) | async-done | bytes 131104 | tf_op jit(solution)/shard_map/all_to_all | solution.py:343
  251.6 0.8 gather_rows.1
  (38 shorter events, 1.3 us)
Async XLA Ops:
  7.2 194.3 %all-gather.2.cloned.1.call-start = ((), (), s32[]{:S(2)}) async-start(), calls=%async_computation.14 | async-start | bytes 1703936 | tf_op jit(solution)/shard_map/all_gather | solution.py:370
  7.9 1.4 copy-start
  9.3 0.9 copy-start.15
  10.2 0.7 copy-start.23
  83.2 29.1 %copy-start.5 = (bf16[256,3072]{1,0:T(8,128)(2,1)S(1)}, bf16[256,3072]{1,0:T(8,128)(2,1)}, u32[]{:S(2)}) copy-start(bf16[256,3072]{1,0:T(8,128)(2,1)} %cotangent_ref.5) | copy-start | bytes 4718596
  113.0 26.6 %copy-start.16 = (bf16[256,256]{1,0:T(8,128)(2,1)S(1)}, bf16[256,256]{1,0:T(8,128)(2,1)}, u32[]{:S(2)}) copy-start(bf16[256,256]{1,0:T(8,128)(2,1)} %features_ref.2) | copy-start | bytes 393220
  132.0 0.6 copy-start.22
  132.6 16.9 %all-to-all-start.6 = ((f32[64,1,256]{2,1,0:T(1,128)}), f32[64,1,256]{2,1,0:T(1,128)S(1)}, u32[]{:S(2)}, u32[]{:S(2)}) async-start(f32[64,1,256]{2,1,0:T(1,128)} %copy-done.22), calls=%async_computation.6 | async-start | bytes 131072 | tf_op jit(solution)/shard_map/all_to_all | solution.py:343
  139.4 101.1 %reduce-scatter.2.cloned.1.call-start = ((), (), s32[]{:S(2)}) async-start(), calls=%async_computation.15 | async-start | bytes 3407872 | tf_op jit(solution)/shard_map/reduce_scatter | solution.py:406
  139.6 1.4 copy-start.1
  141.1 1.4 copy-start.6
  144.7 1.6 copy-start.11
  146.3 0.7 copy-start.19
  163.1 35.1 %copy-start.2 = (bf16[3072,256]{1,0:T(8,128)(2,1)S(1)}, bf16[3072,256]{1,0:T(8,128)(2,1)}, u32[]{:S(2)}) copy-start(bf16[3072,256]{1,0:T(8,128)(2,1)} %prototypes_ref.9) | copy-start | bytes 4718596
  163.1 35.1 %copy-start.20 = (f32[256,256]{1,0:T(8,128)S(1)}, f32[256,256]{1,0:T(8,128)}, u32[]{:S(2)}) copy-start(f32[256,256]{1,0:T(8,128)} %copy-done.19) | copy-start | bytes 786436
  200.0 0.7 copy-start.12
  200.7 0.7 copy-start.17
  201.4 20.3 %all-to-all-start.10 = ((f32[64,1,1280]{2,1,0:T(1,128)}), f32[64,1,1280]{2,1,0:T(1,128)S(1)}, u32[]{:S(2)}, u32[]{:S(2)}) async-start(f32[64,1,1280]{2,1,0:T(1,128)} %copy-done.17), calls=%async_computation.10 | async-start | bytes 655360 | tf_op jit(solution)/shard_map/all_to_all | solution.py:343
  207.6 1.4 copy-start.3
  209.0 1.4 copy-start.9
  210.4 0.9 copy-start.13
  211.4 29.2 %copy-start.4 = (bf16[3072,256]{1,0:T(8,128)(2,1)S(1)}, bf16[3072,256]{1,0:T(8,128)(2,1)}, u32[]{:S(2)}) copy-start(bf16[3072,256]{1,0:T(8,128)(2,1)} %prototypes_ref.9) | copy-start | bytes 4718596
  211.4 29.2 %copy-start.10 = (bf16[3072,256]{1,0:T(8,128)(2,1)S(1)}, bf16[3072,256]{1,0:T(8,128)(2,1)}, u32[]{:S(2)}) copy-start(bf16[3072,256]{1,0:T(8,128)(2,1)} %all-gather.2.cloned.1.call-done.features_ref) | copy-start | bytes 4718596
  213.0 1.7 copy-start.7
  221.9 0.7 copy-start.21
  234.0 17.6 %all-to-all-start.12 = ((bf16[64,8,128]{2,1,0:T(8,128)(2,1)}), bf16[64,8,128]{2,1,0:T(8,128)(2,1)S(1)}, u32[]{:S(2)}, u32[]{:S(2)}) async-start(bf16[64,8,128]{2,1,0:T(8,128)(2,1)} %copy-done.21), calls=%async_computation.12 | async-start | bytes 262144 | tf_op jit(solution)/shard_map/all_to_all | solution.py:343
  240.5 1.9 copy-start.8
  242.4 0.9 copy-start.14
  243.4 0.9 copy-start.18
Sparse Core Ops, SparseCore 0:
  10.4 62.4 all-gather.1
  149.7 52.8 reduce-scatter.1

commit v4 on v3

--- a/solution.py
+++ b/solution.py
@@ -90,7 +90,7 @@
 def start_body(features_ref, prototypes_ref, counts_ref, kernel_ref, cols_ref, out_ref):
     rows = features_ref.shape[0]
     width = 512
-    left = features_ref[...]
+    left = features_ref[...].astype(BF16)
     sums, plain = 0.0, 0.0
     for at in tiles(prototypes_ref.shape[0], width):
         right = prototypes_ref[at, :]
@@ -101,7 +101,7 @@
         plain = plain + product(block, right)
     out_ref[:, :, :rows] = copies(flat(sums), out_ref.shape[0])
     scatter_rows(sharpness * plain, out_ref, rows + LANES)
-    counts = counts_ref[...].astype(F32)
+    counts = counts_ref[...]
     cols_ref[...] = jnp.zeros_like(cols_ref)
     put(cols_ref, TARGET, counts)
     total = jnp.sum(counts, axis=1, keepdims=True)
@@ -116,6 +116,9 @@
     columns = kernel_ref.shape[1]
     wide = down(row)
     values = [jnp.sum(kernel_ref[:, at] * wide, axis=0, keepdims=True) for at in tiles(columns, LANES)]
+    if out_ref.dtype == F32:
+        out_ref[...] = copies(jnp.concatenate([*values, row], axis=1), out_ref.shape[0])
+        return
     for part in parts(row):
         values += [part.astype(F32)[:, at] for at in tiles(row.shape[1], LANES)]
     spare = out_ref.shape[1] - len(values)
@@ -125,6 +128,9 @@
 
 
 def received_columns(ref, columns, every_ref, every_out, row):
+    if ref.dtype == F32:
+        spread(ref, every_ref, every_out, row, columns)
+        return received(ref, 0, columns)
     values = ref[...].astype(F32)
     sums = jnp.sum(values, axis=0)
     carry(every_ref, every_out)
@@ -291,13 +297,10 @@
     mine = received(du_ref, rows, du_ref.shape[2])
     width = mine.shape[1] * count // rows
     lane = lax.broadcasted_iota(jnp.int32, dx.shape, 1)
-    values = []
     for r in range(rows // count):
-        row = r * count + place_ref[0]
-        value = jnp.sum(jnp.where(lane == row, dx, 0.0), axis=1, keepdims=True)
-        value = mine[:, r * width : (r + 1) * width] + value * get(rws_ref, PLAIN + r)
-        values += [value[:, at] for at in tiles(width, LANES)]
-    out_ref[...] = copies(jnp.concatenate(values, axis=0).astype(BF16), count)
+        at = slice(r * width, (r + 1) * width)
+        value = jnp.sum(jnp.where(lane == r * count + place_ref[0], dx, 0.0), axis=1, keepdims=True)
+        out_ref[:, :, at] = copies(mine[:, at] + value * get(rws_ref, PLAIN + r), count)
 
 
 def own_rows(place_ref, size):
@@ -332,11 +335,9 @@
 
 def gather_rows_body(ref, out_ref):
     count = ref.shape[0]
-    values = ref[...].astype(F32)
-    blocks = tiles(out_ref.shape[1], LANES)
-    for i in range(ref.shape[1]):
-        r, at = i // len(blocks), blocks[i % len(blocks)]
-        out_ref[r * count : (r + 1) * count, at] = values[:, i, :]
+    width = out_ref.shape[1]
+    for r in range(out_ref.shape[0] // count):
+        out_ref[r * count : (r + 1) * count, :] = ref[:, 0, r * width : (r + 1) * width]
 
 
 def exchange(messages, axis):
@@ -356,7 +357,7 @@
     rows_all = rows * samples
     protos_all = float(columns * classes)
     sliced = rows * width // classes
-    counts = prior_counts.reshape(1, columns)
+    counts = prior_counts.astype(F32).reshape(1, columns)
     dp_place = lax.axis_index("dp").astype(jnp.int32).reshape(1)
     cls_place = lax.axis_index("cls").astype(jnp.int32).reshape(1)
     once = 2 * rows * columns
@@ -364,12 +365,13 @@
 
     cols_t, rws_t, every_t = f32(8, columns), f32(16, rows), f32(8, rows_all)
     to_rows = f32(classes, 1, rows)
+    to_columns_exact = f32(samples, 1, columns + rows)
     to_columns = jax.ShapeDtypeStruct((samples, message_rows(columns, rows), LANES), BF16)
     block_t = f32(rows, columns)
 
     features_all = lax.all_gather(features, "dp", axis=0, tiled=True)
     kernel, cols, message = call(
-        start_body, [block_t, cols_t, f32(classes, 1, rows + LANES + sliced)], [features, prototypes, counts], "start", flops=3 * full
+        start_body, [block_t, cols_t, f32(classes, 1, rows + LANES + sliced)], [features.astype(F32), prototypes, counts], "start", flops=3 * full
     )
     message = exchange(message, "cls")
     cols, rws, every, message = call(
@@ -404,7 +406,7 @@
     )
     message, weighted, known = together(exchange(message, "cls"), weighted, known)
     weighted = lax.psum_scatter(weighted, "dp", scatter_dimension=0, tiled=True)
-    rws, message = call(functools.partial(back_columns_body, 2), [rws_t, to_columns], [message, kernel, rws], "back_columns_2", flops=once)
+    rws, message = call(functools.partial(back_columns_body, 2), [rws_t, to_columns_exact], [message, kernel, rws], "back_columns_2", flops=once)
     message = exchange(message, "dp")
     cols, every, message = call(
         functools.partial(back_rows_body, 1), [cols_t, every_t, to_rows], [message, kernel, cols, every], "back_rows_1", flops=once
@@ -423,8 +425,7 @@
     )
     message, known_columns = together(exchange(message, "cls"), known_columns)
     dx_message, message = call(
-        finish_rows_body, [f32(samples, 1, rows), jax.ShapeDtypeStruct((classes, sliced // LANES, LANES), BF16)],
-        [cls_place, message, rws], "finish_rows", smem=1,
+        finish_rows_body, [f32(samples, 1, rows), f32(classes, 1, sliced)], [cls_place, message, rws], "finish_rows", smem=1
     )
     dx1, message = together(exchange(dx_message, "dp"), message)
     gathered = exchange(message, "cls")

time: 260 us -> 264 us (1.015)
    unnamed x48 -> x44, local copies, waits for them, and re-layouts: 20 us -> 18.5 us
  transfers between devices with their start and end apart: 5 -> 5, of which waited for: 3 -> 3; matrix products, arithmetic and copies ran while one was open for 0% -> 1% of each run, Pallas kernels for 6% -> 6%
where the time goes in v4:
time: 264 us; the launch traced here: 263 us
  blocking collectives  175 us (66%)
  starting transfers between devices  20.5 us (8%)
  local copies, waits for them, and re-layouts  18.5 us (7%)
  waiting for transfers between devices  16.6 us (6%)
  Pallas kernels  16.3 us (6%)
  between operations  14.3 us (5%)
    all_to_all x10, blocking collectives, exchange(): return lax.all_to_all(messages, axis, 0, 0, tiled=True)  175 us
    all_to_all x3, starting transfers between devices, exchange(): return lax.all_to_all(messages, axis, 0, 0, tiled=True)  20.3 us
    unnamed x44, local copies, waits for them, and re-layouts  18.5 us
    pallas_call x16, Pallas kernels, call(): pl.pallas_call(body, out_shape=outs, in_specs=specs, out_specs=[pl.BlockS...  16.3 us
    all_to_all x3, waiting for transfers between devices, exchange(): return lax.all_to_all(messages, axis, 0, 0, tiled=True)  15.9 us
  transfers between devices with their start and end apart: 5, of which 3 were waited for; matrix products, arithmetic and copies ran while one was open for 1% of the time, Pallas kernels for 6%

profile of v4, /device:TPU:1, one launch (start us, length us, event | category | flops | bytes accessed | tf_op | source)
XLA Modules:
  0.0 263.1 jit_solution(13299909089837859865)
XLA Ops:
  7.2 0.7 all-gather.2.cloned.1.call-update
  7.9 0.9 convert_element_type.6.features_ref
  8.8 0.7 convert_element_type.7
  9.5 1.4 copy-done
  10.9 2.1 start.1
  13.0 28.4 %all_to_all.65.x_ref = f32[64,1,1408]{2,1,0:T(1,128)S(1)} all-to-all(f32[64,1,1408]{2,1,0:T(1,128)S(1)} %get-tuple-element.49), channel_id=1, replica_groups=mesh['dp'=12,'cls'=64] {'cls'}, dimensions={0} | all-to-all | bytes 720896 | tf_op jit(solution)/shard_map/all_to_all | solution.py:344
  41.4 0.6 columns_first.1
  42.0 24.0 %all_to_all.66.y_ref = bf16[12,32,128]{2,1,0:T(8,128)(2,1)S(1)} all-to-all(bf16[12,32,128]{2,1,0:T(8,128)(2,1)S(1)} %get-tuple-element.52), channel_id=1, replica_groups=mesh['dp'=12,'cls'=64] {'dp'}, dimensions={0} | all-to-all | bytes 196608 | tf_op jit(solution)/shard_map/all_to_all | solution.py:344
  66.4 16.8 %all_to_all.67.x_ref = f32[64,1,256]{2,1,0:T(1,128)S(1)} all-to-all(f32[64,1,256]{2,1,0:T(1,128)S(1)} %get-tuple-element.55), channel_id=1, replica_groups=mesh['dp'=12,'cls'=64] {'cls'}, dimensions={0} | all-to-all | bytes 131072 | tf_op jit(solution)/shard_map/all_to_all | solution.py:344
  83.2 0.4 columns_1.1
  83.6 13.2 %all_to_all.68.y_ref = bf16[12,32,128]{2,1,0:T(8,128)(2,1)S(1)} all-to-all(bf16[12,32,128]{2,1,0:T(8,128)(2,1)S(1)} %get-tuple-element.57), channel_id=1, replica_groups=mesh['dp'=12,'cls'=64] {'dp'}, dimensions={0} | all-to-all | bytes 196608 | tf_op jit(solution)/shard_map/all_to_all | solution.py:344
  97.2 15.1 %all_to_all.69.x_ref = f32[64,1,256]{2,1,0:T(1,128)S(1)} all-to-all(f32[64,1,256]{2,1,0:T(1,128)S(1)} %get-tuple-element.60), channel_id=1, replica_groups=mesh['dp'=12,'cls'=64] {'cls'}, dimensions={0} | all-to-all | bytes 131072 | tf_op jit(solution)/shard_map/all_to_all | solution.py:344
  112.3 0.8 columns_last.1
  113.1 18.0 %all_to_all.70.y_ref = f32[12,1,6400]{2,1,0:T(1,128)S(1)} all-to-all(f32[12,1,6400]{2,1,0:T(1,128)S(1)} %get-tuple-element.62), channel_id=1, replica_groups=mesh['dp'=12,'cls'=64] {'dp'}, dimensions={0} | all-to-all | bytes 614400 | tf_op jit(solution)/shard_map/all_to_all | solution.py:344
  131.1 0.9 rows_last.1
  132.0 0.6 copy-done.21
  132.6 6.8 %all-to-all-start.6 = ((f32[64,1,256]{2,1,0:T(1,128)}), f32[64,1,256]{2,1,0:T(1,128)S(1)}, u32[]{:S(2)}, u32[]{:S(2)}) async-start(f32[64,1,256]{2,1,0:T(1,128)} %copy-done.21), calls=%async_computation.6 | async-start | bytes 131072 | tf_op jit(solution)/shard_map/all_to_all | solution.py:344
  139.7 1.4 copy-done.1
  141.1 1.4 copy-done.6
  142.5 2.2 cotangent_products.1
  144.7 1.6 copy-done.11
  146.3 0.7 copy-done.18
  147.0 2.5 all-to-all-done.6.du_ref
  149.6 0.4 back_columns_2.1
  150.0 14.9 %all_to_all.71.dv_ref = f32[12,1,3328]{2,1,0:T(1,128)S(1)} all-to-all(f32[12,1,3328]{2,1,0:T(1,128)S(1)} %get-tuple-element.73), channel_id=1, replica_groups=mesh['dp'=12,'cls'=64] {'dp'}, dimensions={0} | all-to-all | bytes 319488 | tf_op jit(solution)/shard_map/all_to_all | solution.py:344
  164.9 0.4 back_rows_1.1
  165.4 19.6 %all_to_all.72.du_ref = f32[64,1,256]{2,1,0:T(1,128)S(1)} all-to-all(f32[64,1,256]{2,1,0:T(1,128)S(1)} %get-tuple-element.75), channel_id=1, replica_groups=mesh['dp'=12,'cls'=64] {'cls'}, dimensions={0} | all-to-all | bytes 131072 | tf_op jit(solution)/shard_map/all_to_all | solution.py:344
  184.9 0.4 back_columns_1.1
  185.3 13.8 %all_to_all.73.dv_ref = bf16[12,32,128]{2,1,0:T(8,128)(2,1)S(1)} all-to-all(bf16[12,32,128]{2,1,0:T(8,128)(2,1)S(1)} %get-tuple-element.77), channel_id=1, replica_groups=mesh['dp'=12,'cls'=64] {'dp'}, dimensions={0} | all-to-all | bytes 196608 | tf_op jit(solution)/shard_map/all_to_all | solution.py:344
  199.1 1.7 last_rows.1
  200.9 0.7 copy-done.13
  201.6 0.7 copy-done.16
  202.3 7.0 %all-to-all-start.10 = ((f32[64,1,1280]{2,1,0:T(1,128)}), f32[64,1,1280]{2,1,0:T(1,128)S(1)}, u32[]{:S(2)}, u32[]{:S(2)}) async-start(f32[64,1,1280]{2,1,0:T(1,128)} %copy-done.16), calls=%async_computation.10 | async-start | bytes 655360 | tf_op jit(solution)/shard_map/all_to_all | solution.py:344
  209.4 1.4 copy-done.3
  210.8 1.4 copy-done.9
  212.2 0.9 copy-done.14
  213.1 1.6 known_columns.1.known_ref
  214.8 1.7 copy-done.7
  216.5 7.0 %all-to-all-done.10.du_ref = f32[64,1,1280]{2,1,0:T(1,128)S(1)} async-done(((f32[64,1,1280]{2,1,0:T(1,128)}), f32[64,1,1280]{2,1,0:T(1,128)S(1)}, u32[]{:S(2)}, u32[]{:S(2)}) %all-to-all-start.10) | async-done | bytes 327712 | tf_op jit(solution)/shard_map/all_to_all | solution.py:344
  223.7 0.7 copy-done.20
  224.4 11.4 %all_to_all.74.dx_ref = f32[12,1,256]{2,1,0:T(1,128)S(1)} all-to-all(f32[12,1,256]{2,1,0:T(1,128)S(1)} %get-tuple-element.88), channel_id=1, replica_groups=mesh['dp'=12,'cls'=64] {'dp'}, dimensions={0} | all-to-all | bytes 24576 | tf_op jit(solution)/shard_map/all_to_all | solution.py:344
  235.9 6.4 %all-to-all-start.12 = ((f32[64,1,1024]{2,1,0:T(1,128)}), f32[64,1,1024]{2,1,0:T(1,128)S(1)}, u32[]{:S(2)}, u32[]{:S(2)}) async-start(f32[64,1,1024]{2,1,0:T(1,128)} %copy-done.20), calls=%async_computation.12 | async-start | bytes 524288 | tf_op jit(solution)/shard_map/all_to_all | solution.py:344
  242.4 1.9 copy-done.8
  244.3 0.9 copy-done.15
  245.2 0.9 copy-done.17
  246.2 3.0 %finish_columns.1 = f32[256,256]{1,0:T(8,128)} custom-call(s32[1]{0:T(128)} %bitcast.2.place_ref, f32[12,1,256]{2,1,0:T(1,128)S(1)} %all_to_all.74.dx_ref, f32[256,3072]{1,0:T(8,128)S(1)} %copy-done.8, bf16[3072,256]{1,0:T(8,128)(2,1)S(1)} %copy-done.4, bf16[3072,256]{1,0:T(8,128)(2,1)S(1)} %copy-done.10, f32[16,3072]{1,0:T(8,128)S(1)} %copy-done.15, ...), custom_call_target="tpu_custom_call" | custom-call | flops 1207959552 | bytes 7024644 | tf_op jit(solution)/shard_map/finish_columns/pallas_call | solution.py:22
  249.1 6.4 %all-to-all-done.12.ref = f32[64,1,1024]{2,1,0:T(1,128)S(1)} async-done(((f32[64,1,1024]{2,1,0:T(1,128)}), f32[64,1,1024]{2,1,0:T(1,128)S(1)}, u32[]{:S(2)}, u32[]{:S(2)}) %all-to-all-start.12) | async-done | bytes 262176 | tf_op jit(solution)/shard_map/all_to_all | solution.py:344
  255.5 0.8 gather_rows.1
  (36 shorter events, 1.4 us)
Async XLA Ops:
  7.2 195.1 %all-gather.2.cloned.1.call-start = ((), (), s32[]{:S(2)}) async-start(), calls=%async_computation.14 | async-start | bytes 1703936 | tf_op jit(solution)/shard_map/all_gather | solution.py:372
  9.5 1.4 copy-start
  83.2 29.1 %copy-start.5 = (bf16[256,3072]{1,0:T(8,128)(2,1)S(1)}, bf16[256,3072]{1,0:T(8,128)(2,1)}, u32[]{:S(2)}) copy-start(bf16[256,3072]{1,0:T(8,128)(2,1)} %cotangent_ref.5) | copy-start | bytes 4718596
  113.0 26.6 %copy-start.12 = (bf16[256,256]{1,0:T(8,128)(2,1)S(1)}, bf16[256,256]{1,0:T(8,128)(2,1)}, u32[]{:S(2)}) copy-start(bf16[256,256]{1,0:T(8,128)(2,1)} %features_ref) | copy-start | bytes 393220
  132.0 0.6 copy-start.21
  132.6 16.9 %all-to-all-start.6 = ((f32[64,1,256]{2,1,0:T(1,128)}), f32[64,1,256]{2,1,0:T(1,128)S(1)}, u32[]{:S(2)}, u32[]{:S(2)}) async-start(f32[64,1,256]{2,1,0:T(1,128)} %copy-done.21), calls=%async_computation.6 | async-start | bytes 131072 | tf_op jit(solution)/shard_map/all_to_all | solution.py:344
  139.4 102.9 %reduce-scatter.2.cloned.1.call-start = ((), (), s32[]{:S(2)}) async-start(), calls=%async_computation.15 | async-start | bytes 3407872 | tf_op jit(solution)/shard_map/reduce_scatter | solution.py:408
  139.7 1.4 copy-start.1
  141.1 1.4 copy-start.6
  144.7 1.6 copy-start.11
  146.3 0.7 copy-start.18
  164.9 34.2 %copy-start.2 = (bf16[3072,256]{1,0:T(8,128)(2,1)S(1)}, bf16[3072,256]{1,0:T(8,128)(2,1)}, u32[]{:S(2)}) copy-start(bf16[3072,256]{1,0:T(8,128)(2,1)} %prototypes_ref.9) | copy-start | bytes 4718596
  164.9 34.2 %copy-start.19 = (f32[256,256]{1,0:T(8,128)S(1)}, f32[256,256]{1,0:T(8,128)}, u32[]{:S(2)}) copy-start(f32[256,256]{1,0:T(8,128)} %copy-done.18) | copy-start | bytes 786436
  200.9 0.7 copy-start.13
  201.6 0.7 copy-start.16
  202.3 21.1 %all-to-all-start.10 = ((f32[64,1,1280]{2,1,0:T(1,128)}), f32[64,1,1280]{2,1,0:T(1,128)S(1)}, u32[]{:S(2)}, u32[]{:S(2)}) async-start(f32[64,1,1280]{2,1,0:T(1,128)} %copy-done.16), calls=%async_computation.10 | async-start | bytes 655360 | tf_op jit(solution)/shard_map/all_to_all | solution.py:344
  209.4 1.4 copy-start.3
  210.8 1.4 copy-start.9
  212.2 0.9 copy-start.14
  213.1 29.2 %copy-start.4 = (bf16[3072,256]{1,0:T(8,128)(2,1)S(1)}, bf16[3072,256]{1,0:T(8,128)(2,1)}, u32[]{:S(2)}) copy-start(bf16[3072,256]{1,0:T(8,128)(2,1)} %prototypes_ref.9) | copy-start | bytes 4718596
  213.1 29.3 %copy-start.10 = (bf16[3072,256]{1,0:T(8,128)(2,1)S(1)}, bf16[3072,256]{1,0:T(8,128)(2,1)}, u32[]{:S(2)}) copy-start(bf16[3072,256]{1,0:T(8,128)(2,1)} %all-gather.2.cloned.1.call-done.features_ref) | copy-start | bytes 4718596
  214.8 1.7 copy-start.7
  223.7 0.7 copy-start.20
  235.9 19.6 %all-to-all-start.12 = ((f32[64,1,1024]{2,1,0:T(1,128)}), f32[64,1,1024]{2,1,0:T(1,128)S(1)}, u32[]{:S(2)}, u32[]{:S(2)}) async-start(f32[64,1,1024]{2,1,0:T(1,128)} %copy-done.20), calls=%async_computation.12 | async-start | bytes 524288 | tf_op jit(solution)/shard_map/all_to_all | solution.py:344
  242.4 1.9 copy-start.8
  244.3 0.9 copy-start.15
  245.2 0.9 copy-start.17
Sparse Core Ops, SparseCore 0:
  10.4 62.8 all-gather.1
  149.7 52.9 reduce-scatter.1

commit v5 on v4

--- a/solution.py
+++ b/solution.py
@@ -383,7 +383,7 @@
         functools.partial(rows_body, 0), [cols_t, every_t, to_rows], [message, kernel, cols, every], "rows_0", flops=once
     )
     message = exchange(message, "cls")
-    rws, message = call(functools.partial(columns_body, 1), [rws_t, to_columns], [message, kernel, rws], "columns_1", flops=once)
+    rws, message = call(functools.partial(columns_body, 1), [rws_t, to_columns_exact], [message, kernel, rws], "columns_1", flops=once)
     message = exchange(message, "dp")
     cols, every, message = call(
         functools.partial(rows_body, 1), [cols_t, every_t, to_rows], [message, kernel, cols, every], "rows_1", flops=once

time: 264 us -> 266 us (level)
  blocking collectives: 175 us -> 178 us
    all_to_all x10, blocking collectives: 175 us -> 178 us  [exchange(): return lax.all_to_all(messages, axis, 0, 0, tiled=True)]
where the time goes in v5:
time: 266 us; the launch traced here: 265 us
  blocking collectives  178 us (67%)
  starting transfers between devices  19.6 us (7%)
  local copies, waits for them, and re-layouts  18.5 us (7%)
  waiting for transfers between devices  16.6 us (6%)
  Pallas kernels  16.4 us (6%)
  between operations  14.3 us (5%)
    all_to_all x10, blocking collectives, exchange(): return lax.all_to_all(messages, axis, 0, 0, tiled=True)  178 us
    all_to_all x3, starting transfers between devices, exchange(): return lax.all_to_all(messages, axis, 0, 0, tiled=True)  19.3 us
    unnamed x44, local copies, waits for them, and re-layouts  18.5 us
    pallas_call x16, Pallas kernels, call(): pl.pallas_call(body, out_shape=outs, in_specs=specs, out_specs=[pl.BlockS...  16.4 us
    all_to_all x3, waiting for transfers between devices, exchange(): return lax.all_to_all(messages, axis, 0, 0, tiled=True)  15.9 us
  transfers between devices with their start and end apart: 5, of which 3 were waited for; matrix products, arithmetic and copies ran while one was open for 1% of the time, Pallas kernels for 6%

profile of v5, /device:TPU:1, one launch (start us, length us, event | category | flops | bytes accessed | tf_op | source)
XLA Modules:
  0.0 265.1 jit_solution(17973509535144251361)
XLA Ops:
  7.2 0.7 all-gather.2.cloned.1.call-update
  7.9 0.9 convert_element_type.6.features_ref
  8.8 0.7 convert_element_type.7
  9.5 1.4 copy-done
  10.9 2.1 start.1
  13.0 28.4 %all_to_all.65.x_ref = f32[64,1,1408]{2,1,0:T(1,128)S(1)} all-to-all(f32[64,1,1408]{2,1,0:T(1,128)S(1)} %get-tuple-element.49), channel_id=1, replica_groups=mesh['dp'=12,'cls'=64] {'cls'}, dimensions={0} | all-to-all | bytes 720896 | tf_op jit(solution)/shard_map/all_to_all | solution.py:344
  41.4 0.6 columns_first.1
  42.0 24.0 %all_to_all.66.y_ref = bf16[12,32,128]{2,1,0:T(8,128)(2,1)S(1)} all-to-all(bf16[12,32,128]{2,1,0:T(8,128)(2,1)S(1)} %get-tuple-element.52), channel_id=1, replica_groups=mesh['dp'=12,'cls'=64] {'dp'}, dimensions={0} | all-to-all | bytes 196608 | tf_op jit(solution)/shard_map/all_to_all | solution.py:344
  66.4 16.8 %all_to_all.67.x_ref = f32[64,1,256]{2,1,0:T(1,128)S(1)} all-to-all(f32[64,1,256]{2,1,0:T(1,128)S(1)} %get-tuple-element.55), channel_id=1, replica_groups=mesh['dp'=12,'cls'=64] {'cls'}, dimensions={0} | all-to-all | bytes 131072 | tf_op jit(solution)/shard_map/all_to_all | solution.py:344
  83.2 0.4 columns_1.1
  83.6 14.7 %all_to_all.68.y_ref = f32[12,1,3328]{2,1,0:T(1,128)S(1)} all-to-all(f32[12,1,3328]{2,1,0:T(1,128)S(1)} %get-tuple-element.57), channel_id=1, replica_groups=mesh['dp'=12,'cls'=64] {'dp'}, dimensions={0} | all-to-all | bytes 319488 | tf_op jit(solution)/shard_map/all_to_all | solution.py:344
  98.3 0.4 rows_1.1
  98.8 15.1 %all_to_all.69.x_ref = f32[64,1,256]{2,1,0:T(1,128)S(1)} all-to-all(f32[64,1,256]{2,1,0:T(1,128)S(1)} %get-tuple-element.60), channel_id=1, replica_groups=mesh['dp'=12,'cls'=64] {'cls'}, dimensions={0} | all-to-all | bytes 131072 | tf_op jit(solution)/shard_map/all_to_all | solution.py:344
  113.9 0.8 columns_last.1
  114.7 19.1 %all_to_all.70.y_ref = f32[12,1,6400]{2,1,0:T(1,128)S(1)} all-to-all(f32[12,1,6400]{2,1,0:T(1,128)S(1)} %get-tuple-element.62), channel_id=1, replica_groups=mesh['dp'=12,'cls'=64] {'dp'}, dimensions={0} | all-to-all | bytes 614400 | tf_op jit(solution)/shard_map/all_to_all | solution.py:344
  133.8 0.9 rows_last.1
  134.7 0.6 copy-done.21
  135.4 6.1 %all-to-all-start.6 = ((f32[64,1,256]{2,1,0:T(1,128)}), f32[64,1,256]{2,1,0:T(1,128)S(1)}, u32[]{:S(2)}, u32[]{:S(2)}) async-start(f32[64,1,256]{2,1,0:T(1,128)} %copy-done.21), calls=%async_computation.6 | async-start | bytes 131072 | tf_op jit(solution)/shard_map/all_to_all | solution.py:344
  141.7 1.4 copy-done.1
  143.1 1.4 copy-done.6
  144.5 2.2 cotangent_products.1
  146.7 1.6 copy-done.11
  148.3 0.7 copy-done.18
  149.0 2.5 all-to-all-done.6.du_ref
  151.6 0.4 back_columns_2.1
  152.0 14.7 %all_to_all.71.dv_ref = f32[12,1,3328]{2,1,0:T(1,128)S(1)} all-to-all(f32[12,1,3328]{2,1,0:T(1,128)S(1)} %get-tuple-element.73), channel_id=1, replica_groups=mesh['dp'=12,'cls'=64] {'dp'}, dimensions={0} | all-to-all | bytes 319488 | tf_op jit(solution)/shard_map/all_to_all | solution.py:344
  166.7 0.4 back_rows_1.1
  167.2 19.6 %all_to_all.72.du_ref = f32[64,1,256]{2,1,0:T(1,128)S(1)} all-to-all(f32[64,1,256]{2,1,0:T(1,128)S(1)} %get-tuple-element.75), channel_id=1, replica_groups=mesh['dp'=12,'cls'=64] {'cls'}, dimensions={0} | all-to-all | bytes 131072 | tf_op jit(solution)/shard_map/all_to_all | solution.py:344
  187.2 14.2 %all_to_all.73.dv_ref = bf16[12,32,128]{2,1,0:T(8,128)(2,1)S(1)} all-to-all(bf16[12,32,128]{2,1,0:T(8,128)(2,1)S(1)} %get-tuple-element.77), channel_id=1, replica_groups=mesh['dp'=12,'cls'=64] {'dp'}, dimensions={0} | all-to-all | bytes 196608 | tf_op jit(solution)/shard_map/all_to_all | solution.py:344
  201.4 1.7 last_rows.1
  203.1 0.7 copy-done.13
  203.8 0.7 copy-done.16
  204.5 6.8 %all-to-all-start.10 = ((f32[64,1,1280]{2,1,0:T(1,128)}), f32[64,1,1280]{2,1,0:T(1,128)S(1)}, u32[]{:S(2)}, u32[]{:S(2)}) async-start(f32[64,1,1280]{2,1,0:T(1,128)} %copy-done.16), calls=%async_computation.10 | async-start | bytes 655360 | tf_op jit(solution)/shard_map/all_to_all | solution.py:344
  211.4 1.4 copy-done.3
  212.8 1.4 copy-done.9
  214.2 0.9 copy-done.14
  215.1 1.6 known_columns.1.known_ref
  216.8 1.7 copy-done.7
  218.4 7.0 %all-to-all-done.10.du_ref = f32[64,1,1280]{2,1,0:T(1,128)S(1)} async-done(((f32[64,1,1280]{2,1,0:T(1,128)}), f32[64,1,1280]{2,1,0:T(1,128)S(1)}, u32[]{:S(2)}, u32[]{:S(2)}) %all-to-all-start.10) | async-done | bytes 327712 | tf_op jit(solution)/shard_map/all_to_all | solution.py:344
  225.7 0.7 copy-done.20
  226.4 11.4 %all_to_all.74.dx_ref = f32[12,1,256]{2,1,0:T(1,128)S(1)} all-to-all(f32[12,1,256]{2,1,0:T(1,128)S(1)} %get-tuple-element.88), channel_id=1, replica_groups=mesh['dp'=12,'cls'=64] {'dp'}, dimensions={0} | all-to-all | bytes 24576 | tf_op jit(solution)/shard_map/all_to_all | solution.py:344
  237.9 6.4 %all-to-all-start.12 = ((f32[64,1,1024]{2,1,0:T(1,128)}), f32[64,1,1024]{2,1,0:T(1,128)S(1)}, u32[]{:S(2)}, u32[]{:S(2)}) async-start(f32[64,1,1024]{2,1,0:T(1,128)} %copy-done.20), calls=%async_computation.12 | async-start | bytes 524288 | tf_op jit(solution)/shard_map/all_to_all | solution.py:344
  244.4 1.9 copy-done.8
  246.3 0.9 copy-done.15
  247.2 0.9 copy-done.17
  248.1 3.0 %finish_columns.1 = f32[256,256]{1,0:T(8,128)} custom-call(s32[1]{0:T(128)} %bitcast.2.place_ref, f32[12,1,256]{2,1,0:T(1,128)S(1)} %all_to_all.74.dx_ref, f32[256,3072]{1,0:T(8,128)S(1)} %copy-done.8, bf16[3072,256]{1,0:T(8,128)(2,1)S(1)} %copy-done.4, bf16[3072,256]{1,0:T(8,128)(2,1)S(1)} %copy-done.10, f32[16,3072]{1,0:T(8,128)S(1)} %copy-done.15, ...), custom_call_target="tpu_custom_call" | custom-call | flops 1207959552 | bytes 7024644 | tf_op jit(solution)/shard_map/finish_columns/pallas_call | solution.py:22
  251.1 6.4 %all-to-all-done.12.ref = f32[64,1,1024]{2,1,0:T(1,128)S(1)} async-done(((f32[64,1,1024]{2,1,0:T(1,128)}), f32[64,1,1024]{2,1,0:T(1,128)S(1)}, u32[]{:S(2)}, u32[]{:S(2)}) %all-to-all-start.12) | async-done | bytes 262176 | tf_op jit(solution)/shard_map/all_to_all | solution.py:344
  257.5 0.8 gather_rows.1
  (36 shorter events, 1.4 us)
Async XLA Ops:
  7.2 197.4 %all-gather.2.cloned.1.call-start = ((), (), s32[]{:S(2)}) async-start(), calls=%async_computation.14 | async-start | bytes 1703936 | tf_op jit(solution)/shard_map/all_gather | solution.py:372
  9.5 1.4 copy-start
  83.2 30.7 %copy-start.5 = (bf16[256,3072]{1,0:T(8,128)(2,1)S(1)}, bf16[256,3072]{1,0:T(8,128)(2,1)}, u32[]{:S(2)}) copy-start(bf16[256,3072]{1,0:T(8,128)(2,1)} %cotangent_ref.5) | copy-start | bytes 4718596
  114.7 27.0 %copy-start.12 = (bf16[256,256]{1,0:T(8,128)(2,1)S(1)}, bf16[256,256]{1,0:T(8,128)(2,1)}, u32[]{:S(2)}) copy-start(bf16[256,256]{1,0:T(8,128)(2,1)} %features_ref) | copy-start | bytes 393220
  134.7 0.6 copy-start.21
  135.4 16.2 %all-to-all-start.6 = ((f32[64,1,256]{2,1,0:T(1,128)}), f32[64,1,256]{2,1,0:T(1,128)S(1)}, u32[]{:S(2)}, u32[]{:S(2)}) async-start(f32[64,1,256]{2,1,0:T(1,128)} %copy-done.21), calls=%async_computation.6 | async-start | bytes 131072 | tf_op jit(solution)/shard_map/all_to_all | solution.py:344
  141.4 102.9 %reduce-scatter.2.cloned.1.call-start = ((), (), s32[]{:S(2)}) async-start(), calls=%async_computation.15 | async-start | bytes 3407872 | tf_op jit(solution)/shard_map/reduce_scatter | solution.py:408
  141.7 1.4 copy-start.1
  143.1 1.4 copy-start.6
  146.7 1.6 copy-start.11
  148.3 0.7 copy-start.18
  166.7 34.6 %copy-start.2 = (bf16[3072,256]{1,0:T(8,128)(2,1)S(1)}, bf16[3072,256]{1,0:T(8,128)(2,1)}, u32[]{:S(2)}) copy-start(bf16[3072,256]{1,0:T(8,128)(2,1)} %prototypes_ref.9) | copy-start | bytes 4718596
  166.7 34.6 %copy-start.19 = (f32[256,256]{1,0:T(8,128)S(1)}, f32[256,256]{1,0:T(8,128)}, u32[]{:S(2)}) copy-start(f32[256,256]{1,0:T(8,128)} %copy-done.18) | copy-start | bytes 786436
  203.1 0.7 copy-start.13
  203.8 0.7 copy-start.16
  204.5 20.9 %all-to-all-start.10 = ((f32[64,1,1280]{2,1,0:T(1,128)}), f32[64,1,1280]{2,1,0:T(1,128)S(1)}, u32[]{:S(2)}, u32[]{:S(2)}) async-start(f32[64,1,1280]{2,1,0:T(1,128)} %copy-done.16), calls=%async_computation.10 | async-start | bytes 655360 | tf_op jit(solution)/shard_map/all_to_all | solution.py:344
  211.3 1.4 copy-start.3
  212.8 1.4 copy-start.9
  214.2 0.9 copy-start.14
  215.1 29.2 %copy-start.4 = (bf16[3072,256]{1,0:T(8,128)(2,1)S(1)}, bf16[3072,256]{1,0:T(8,128)(2,1)}, u32[]{:S(2)}) copy-start(bf16[3072,256]{1,0:T(8,128)(2,1)} %prototypes_ref.9) | copy-start | bytes 4718596
  215.1 29.3 %copy-start.10 = (bf16[3072,256]{1,0:T(8,128)(2,1)S(1)}, bf16[3072,256]{1,0:T(8,128)(2,1)}, u32[]{:S(2)}) copy-start(bf16[3072,256]{1,0:T(8,128)(2,1)} %all-gather.2.cloned.1.call-done.features_ref) | copy-start | bytes 4718596
  216.7 1.7 copy-start.7
  225.7 0.7 copy-start.20
  237.9 19.6 %all-to-all-start.12 = ((f32[64,1,1024]{2,1,0:T(1,128)}), f32[64,1,1024]{2,1,0:T(1,128)S(1)}, u32[]{:S(2)}, u32[]{:S(2)}) async-start(f32[64,1,1024]{2,1,0:T(1,128)} %copy-done.20), calls=%async_computation.12 | async-start | bytes 524288 | tf_op jit(solution)/shard_map/all_to_all | solution.py:344
  244.4 1.9 copy-start.8
  246.3 0.9 copy-start.15
  247.2 0.9 copy-start.17
Sparse Core Ops, SparseCore 0:
  10.4 62.8 all-gather.1
  151.7 52.6 reduce-scatter.1

commit v6 on v5

--- a/solution.py
+++ b/solution.py
@@ -399,6 +399,12 @@
         "rows_last", flops=2 * once,
     )
 
+    message = exchange(message, "cls")
+    rws, message = call(functools.partial(back_columns_body, 2), [rws_t, to_columns_exact], [message, kernel, rws], "back_columns_2", flops=once)
+    message = exchange(message, "dp")
+    cols, every, message = call(
+        functools.partial(back_rows_body, 1), [cols_t, every_t, to_rows], [message, kernel, cols, every], "back_rows_1", flops=once
+    )
     message, right = together(message, features)
     weighted, known = call(
         functools.partial(cotangent_products_body, protos_all), [f32(columns, width), f32(rows, width)],
@@ -406,12 +412,6 @@
     )
     message, weighted, known = together(exchange(message, "cls"), weighted, known)
     weighted = lax.psum_scatter(weighted, "dp", scatter_dimension=0, tiled=True)
-    rws, message = call(functools.partial(back_columns_body, 2), [rws_t, to_columns_exact], [message, kernel, rws], "back_columns_2", flops=once)
-    message = exchange(message, "dp")
-    cols, every, message = call(
-        functools.partial(back_rows_body, 1), [cols_t, every_t, to_rows], [message, kernel, cols, every], "back_rows_1", flops=once
-    )
-    message = exchange(message, "cls")
     rws, message = call(functools.partial(back_columns_body, 1), [rws_t, to_columns], [message, kernel, rws], "back_columns_1", flops=once)
     message = exchange(message, "dp")
     both, message = call(

time: 266 us -> 269 us (1.011)
  blocking collectives: 178 us -> 145 us
  starting transfers between devices: 19.6 us -> 37.2 us
  waiting for transfers between devices: 16.6 us -> 30.6 us
  local copies, waits for them, and re-layouts: 18.5 us -> 22.2 us
    all_to_all x10 -> x9, blocking collectives: 178 us -> 145 us  [exchange(): return lax.all_to_all(messages, axis, 0, 0, tiled=True)]
    all_to_all x3 -> x4, starting transfers between devices: 19.3 us -> 36.9 us  [exchange(): return lax.all_to_all(messages, axis, 0, 0, tiled=True)]
    all_to_all x3 -> x4, waiting for transfers between devices: 15.9 us -> 29.9 us  [exchange(): return lax.all_to_all(messages, axis, 0, 0, tiled=True)]
    unnamed x44 -> x56, local copies, waits for them, and re-layouts: 18.5 us -> 22.2 us
  transfers between devices with their start and end apart: 5 -> 6, of which waited for: 3 -> 4; matrix products, arithmetic and copies ran while one was open for 1% -> 0% of each run, Pallas kernels for 6% -> 5%
where the time goes in v6:
time: 269 us; the launch traced here: 268 us
  blocking collectives  145 us (54%)
  starting transfers between devices  37.2 us (14%)
  waiting for transfers between devices  30.6 us (11%)
  local copies, waits for them, and re-layouts  22.2 us (8%)
  Pallas kernels  17.1 us (6%)
  between operations  14.3 us (5%)
    all_to_all x9, blocking collectives, exchange(): return lax.all_to_all(messages, axis, 0, 0, tiled=True)  145 us
    all_to_all x4, starting transfers between devices, exchange(): return lax.all_to_all(messages, axis, 0, 0, tiled=True)  36.9 us
    all_to_all x4, waiting for transfers between devices, exchange(): return lax.all_to_all(messages, axis, 0, 0, tiled=True)  29.9 us
    unnamed x56, local copies, waits for them, and re-layouts  22.2 us
    pallas_call x16, Pallas kernels, call(): pl.pallas_call(body, out_shape=outs, in_specs=specs, out_specs=[pl.BlockS...  17.1 us
  transfers between devices with their start and end apart: 6, of which 4 were waited for; matrix products, arithmetic and copies ran while one was open for 0% of the time, Pallas kernels for 5%

profile of v6, /device:TPU:1, one launch (start us, length us, event | category | flops | bytes accessed | tf_op | source)
XLA Modules:
  0.0 268.1 jit_solution(11319085403408049780)
XLA Ops:
  7.2 0.7 convert_element_type.7
  7.9 0.9 convert_element_type.6.features_ref
  8.8 1.4 copy-done
  10.2 2.1 start.1
  12.3 0.7 copy-done.16
  13.0 0.6 copy-done.24
  13.7 14.6 %all-to-all-start = ((f32[64,1,1408]{2,1,0:T(1,128)}), f32[64,1,1408]{2,1,0:T(1,128)S(1)}, u32[]{:S(2)}, u32[]{:S(2)}) async-start(f32[64,1,1408]{2,1,0:T(1,128)} %copy-done.16), calls=%async_computation | async-start | bytes 720896 | tf_op jit(solution)/shard_map/all_to_all | solution.py:344
  28.3 0.7 all-gather.2.cloned.1.call-update
  29.0 13.9 %all-to-all-done.x_ref = f32[64,1,1408]{2,1,0:T(1,128)S(1)} async-done(((f32[64,1,1408]{2,1,0:T(1,128)}), f32[64,1,1408]{2,1,0:T(1,128)S(1)}, u32[]{:S(2)}, u32[]{:S(2)}) %all-to-all-start) | async-done | bytes 360480 | tf_op jit(solution)/shard_map/all_to_all | solution.py:344
  42.9 0.9 copy-done.25
  44.4 23.0 %all_to_all.65.y_ref = bf16[12,32,128]{2,1,0:T(8,128)(2,1)S(1)} all-to-all(bf16[12,32,128]{2,1,0:T(8,128)(2,1)S(1)} %get-tuple-element.52), channel_id=1, replica_groups=mesh['dp'=12,'cls'=64] {'dp'}, dimensions={0} | all-to-all | bytes 196608 | tf_op jit(solution)/shard_map/all_to_all | solution.py:344
  67.7 17.2 %all_to_all.66.x_ref = f32[64,1,256]{2,1,0:T(1,128)S(1)} all-to-all(f32[64,1,256]{2,1,0:T(1,128)S(1)} %get-tuple-element.55), channel_id=1, replica_groups=mesh['dp'=12,'cls'=64] {'cls'}, dimensions={0} | all-to-all | bytes 131072 | tf_op jit(solution)/shard_map/all_to_all | solution.py:344
  85.3 15.5 %all_to_all.67.y_ref = f32[12,1,3328]{2,1,0:T(1,128)S(1)} all-to-all(f32[12,1,3328]{2,1,0:T(1,128)S(1)} %get-tuple-element.57), channel_id=1, replica_groups=mesh['dp'=12,'cls'=64] {'dp'}, dimensions={0} | all-to-all | bytes 319488 | tf_op jit(solution)/shard_map/all_to_all | solution.py:344
  101.3 15.5 %all_to_all.68.x_ref = f32[64,1,256]{2,1,0:T(1,128)S(1)} all-to-all(f32[64,1,256]{2,1,0:T(1,128)S(1)} %get-tuple-element.60), channel_id=1, replica_groups=mesh['dp'=12,'cls'=64] {'cls'}, dimensions={0} | all-to-all | bytes 131072 | tf_op jit(solution)/shard_map/all_to_all | solution.py:344
  116.8 0.8 columns_last.1
  117.6 19.2 %all_to_all.69.y_ref = f32[12,1,6400]{2,1,0:T(1,128)S(1)} all-to-all(f32[12,1,6400]{2,1,0:T(1,128)S(1)} %get-tuple-element.62), channel_id=1, replica_groups=mesh['dp'=12,'cls'=64] {'dp'}, dimensions={0} | all-to-all | bytes 614400 | tf_op jit(solution)/shard_map/all_to_all | solution.py:344
  136.8 1.0 rows_last.1
  137.8 15.4 %all_to_all.70.du_ref = f32[64,1,256]{2,1,0:T(1,128)S(1)} all-to-all(f32[64,1,256]{2,1,0:T(1,128)S(1)} %get-tuple-element.65), channel_id=1, replica_groups=mesh['dp'=12,'cls'=64] {'cls'}, dimensions={0} | all-to-all | bytes 131072 | tf_op jit(solution)/shard_map/all_to_all | solution.py:344
  153.6 14.7 %all_to_all.71.dv_ref = f32[12,1,3328]{2,1,0:T(1,128)S(1)} all-to-all(f32[12,1,3328]{2,1,0:T(1,128)S(1)} %get-tuple-element.67), channel_id=1, replica_groups=mesh['dp'=12,'cls'=64] {'dp'}, dimensions={0} | all-to-all | bytes 319488 | tf_op jit(solution)/shard_map/all_to_all | solution.py:344
  168.3 1.0 back_rows_1.1
  170.0 6.0 %all-to-all-start.8 = ((f32[64,1,256]{2,1,0:T(1,128)}), f32[64,1,256]{2,1,0:T(1,128)S(1)}, u32[]{:S(2)}, u32[]{:S(2)}) async-start(f32[64,1,256]{2,1,0:T(1,128)} %get-tuple-element.71), calls=%async_computation.8 | async-start | bytes 131072 | tf_op jit(solution)/shard_map/all_to_all | solution.py:344
  176.3 1.4 copy-done.1
  177.7 1.4 copy-done.6
  179.1 2.2 cotangent_products.1
  181.4 1.6 copy-done.11
  183.0 0.7 copy-done.19
  183.7 2.6 all-to-all-done.8.du_ref
  186.9 0.9 copy-done.22
  188.2 12.9 %all_to_all.72.dv_ref = bf16[12,32,128]{2,1,0:T(8,128)(2,1)S(1)} all-to-all(bf16[12,32,128]{2,1,0:T(8,128)(2,1)S(1)} %get-tuple-element.78), channel_id=1, replica_groups=mesh['dp'=12,'cls'=64] {'dp'}, dimensions={0} | all-to-all | bytes 196608 | tf_op jit(solution)/shard_map/all_to_all | solution.py:344
  201.1 1.7 last_rows.1
  202.9 0.7 copy-done.13
  203.5 0.7 copy-done.17
  204.3 9.7 %all-to-all-start.10 = ((f32[64,1,1280]{2,1,0:T(1,128)}), f32[64,1,1280]{2,1,0:T(1,128)S(1)}, u32[]{:S(2)}, u32[]{:S(2)}) async-start(f32[64,1,1280]{2,1,0:T(1,128)} %copy-done.17), calls=%async_computation.10 | async-start | bytes 655360 | tf_op jit(solution)/shard_map/all_to_all | solution.py:344
  214.0 1.4 copy-done.3
  215.4 1.4 copy-done.9
  216.8 0.9 copy-done.14
  217.8 1.6 known_columns.1.known_ref
  219.4 1.7 copy-done.7
  221.1 7.1 %all-to-all-done.10.du_ref = f32[64,1,1280]{2,1,0:T(1,128)S(1)} async-done(((f32[64,1,1280]{2,1,0:T(1,128)}), f32[64,1,1280]{2,1,0:T(1,128)S(1)}, u32[]{:S(2)}, u32[]{:S(2)}) %all-to-all-start.10) | async-done | bytes 327712 | tf_op jit(solution)/shard_map/all_to_all | solution.py:344
  228.5 0.7 copy-done.23
  229.2 11.6 %all_to_all.73.dx_ref = f32[12,1,256]{2,1,0:T(1,128)S(1)} all-to-all(f32[12,1,256]{2,1,0:T(1,128)S(1)} %get-tuple-element.88), channel_id=1, replica_groups=mesh['dp'=12,'cls'=64] {'dp'}, dimensions={0} | all-to-all | bytes 24576 | tf_op jit(solution)/shard_map/all_to_all | solution.py:344
  240.7 6.6 %all-to-all-start.12 = ((f32[64,1,1024]{2,1,0:T(1,128)}), f32[64,1,1024]{2,1,0:T(1,128)S(1)}, u32[]{:S(2)}, u32[]{:S(2)}) async-start(f32[64,1,1024]{2,1,0:T(1,128)} %copy-done.23), calls=%async_computation.12 | async-start | bytes 524288 | tf_op jit(solution)/shard_map/all_to_all | solution.py:344
  247.4 1.9 copy-done.8
  249.3 0.9 copy-done.15
  250.2 0.9 copy-done.18
  251.1 3.0 %finish_columns.1 = f32[256,256]{1,0:T(8,128)} custom-call(s32[1]{0:T(128)} %bitcast.2.place_ref, f32[12,1,256]{2,1,0:T(1,128)S(1)} %all_to_all.73.dx_ref, f32[256,3072]{1,0:T(8,128)S(1)} %copy-done.8, bf16[3072,256]{1,0:T(8,128)(2,1)S(1)} %copy-done.4, bf16[3072,256]{1,0:T(8,128)(2,1)S(1)} %copy-done.10, f32[16,3072]{1,0:T(8,128)S(1)} %copy-done.15, ...), custom_call_target="tpu_custom_call" | custom-call | flops 1207959552 | bytes 7024644 | tf_op jit(solution)/shard_map/finish_columns/pallas_call | solution.py:22
  254.1 6.4 %all-to-all-done.12.ref = f32[64,1,1024]{2,1,0:T(1,128)S(1)} async-done(((f32[64,1,1024]{2,1,0:T(1,128)}), f32[64,1,1024]{2,1,0:T(1,128)S(1)}, u32[]{:S(2)}, u32[]{:S(2)}) %all-to-all-start.12) | async-done | bytes 262176 | tf_op jit(solution)/shard_map/all_to_all | solution.py:344
  260.5 0.8 gather_rows.1
  (49 shorter events, 4.6 us)
Async XLA Ops:
  8.8 1.4 copy-start
  12.3 0.7 copy-start.16
  13.0 0.6 copy-start.24
  13.7 29.2 %all-to-all-start = ((f32[64,1,1408]{2,1,0:T(1,128)}), f32[64,1,1408]{2,1,0:T(1,128)S(1)}, u32[]{:S(2)}, u32[]{:S(2)}) async-start(f32[64,1,1408]{2,1,0:T(1,128)} %copy-done.16), calls=%async_computation | async-start | bytes 720896 | tf_op jit(solution)/shard_map/all_to_all | solution.py:344
  28.2 176.0 %all-gather.2.cloned.1.call-start = ((), (), s32[]{:S(2)}) async-start(), calls=%async_computation.14 | async-start | bytes 1703936 | tf_op jit(solution)/shard_map/all_gather | solution.py:372
  42.9 0.9 copy-start.25
  84.9 31.9 %copy-start.5 = (bf16[256,3072]{1,0:T(8,128)(2,1)S(1)}, bf16[256,3072]{1,0:T(8,128)(2,1)}, u32[]{:S(2)}) copy-start(bf16[256,3072]{1,0:T(8,128)(2,1)} %cotangent_ref.5) | copy-start | bytes 4718596
  153.2 23.1 %copy-start.12 = (bf16[256,256]{1,0:T(8,128)(2,1)S(1)}, bf16[256,256]{1,0:T(8,128)(2,1)}, u32[]{:S(2)}) copy-start(bf16[256,256]{1,0:T(8,128)(2,1)} %features_ref) | copy-start | bytes 393220
  169.4 0.6 copy-start.26
  170.0 16.2 %all-to-all-start.8 = ((f32[64,1,256]{2,1,0:T(1,128)}), f32[64,1,256]{2,1,0:T(1,128)S(1)}, u32[]{:S(2)}, u32[]{:S(2)}) async-start(f32[64,1,256]{2,1,0:T(1,128)} %get-tuple-element.71), calls=%async_computation.8 | async-start | bytes 131072 | tf_op jit(solution)/shard_map/all_to_all | solution.py:344
  176.1 71.3 %reduce-scatter.2.cloned.1.call-start = ((), (), s32[]{:S(2)}) async-start(), calls=%async_computation.15 | async-start | bytes 3407872 | tf_op jit(solution)/shard_map/reduce_scatter | solution.py:414
  176.3 1.4 copy-start.1
  177.7 1.4 copy-start.6
  181.4 1.6 copy-start.11
  183.0 0.7 copy-start.19
  186.2 0.6 copy-start.21
  186.9 14.2 %copy-start.20 = (f32[256,256]{1,0:T(8,128)S(1)}, f32[256,256]{1,0:T(8,128)}, u32[]{:S(2)}) copy-start(f32[256,256]{1,0:T(8,128)} %copy-done.19) | copy-start | bytes 786436
  186.9 0.9 copy-start.22
  187.8 13.3 %copy-start.2 = (bf16[3072,256]{1,0:T(8,128)(2,1)S(1)}, bf16[3072,256]{1,0:T(8,128)(2,1)}, u32[]{:S(2)}) copy-start(bf16[3072,256]{1,0:T(8,128)(2,1)} %prototypes_ref.9) | copy-start | bytes 4718596
  187.8 13.3 %copy-start.27 = (f32[8,3072]{1,0:T(8,128)S(1)}, f32[8,3072]{1,0:T(8,128)}, u32[]{:S(2)}) copy-start(f32[8,3072]{1,0:T(8,128)} %copy-done.26) | copy-start | bytes 294916
  202.8 0.7 copy-start.13
  203.5 0.7 copy-start.17
  204.3 23.9 %all-to-all-start.10 = ((f32[64,1,1280]{2,1,0:T(1,128)}), f32[64,1,1280]{2,1,0:T(1,128)S(1)}, u32[]{:S(2)}, u32[]{:S(2)}) async-start(f32[64,1,1280]{2,1,0:T(1,128)} %copy-done.17), calls=%async_computation.10 | async-start | bytes 655360 | tf_op jit(solution)/shard_map/all_to_all | solution.py:344
  214.0 1.4 copy-start.3
  215.4 1.4 copy-start.9
  216.8 0.9 copy-start.14
  217.8 29.6 %copy-start.4 = (bf16[3072,256]{1,0:T(8,128)(2,1)S(1)}, bf16[3072,256]{1,0:T(8,128)(2,1)}, u32[]{:S(2)}) copy-start(bf16[3072,256]{1,0:T(8,128)(2,1)} %prototypes_ref.9) | copy-start | bytes 4718596
  217.8 29.6 %copy-start.10 = (bf16[3072,256]{1,0:T(8,128)(2,1)S(1)}, bf16[3072,256]{1,0:T(8,128)(2,1)}, u32[]{:S(2)}) copy-start(bf16[3072,256]{1,0:T(8,128)(2,1)} %all-gather.2.cloned.1.call-done.features_ref) | copy-start | bytes 4718596
  219.4 1.7 copy-start.7
  228.5 0.7 copy-start.23
  240.7 19.8 %all-to-all-start.12 = ((f32[64,1,1024]{2,1,0:T(1,128)}), f32[64,1,1024]{2,1,0:T(1,128)S(1)}, u32[]{:S(2)}, u32[]{:S(2)}) async-start(f32[64,1,1024]{2,1,0:T(1,128)} %copy-done.23), calls=%async_computation.12 | async-start | bytes 524288 | tf_op jit(solution)/shard_map/all_to_all | solution.py:344
  247.4 1.9 copy-start.8
  249.3 0.9 copy-start.15
  250.2 0.9 copy-start.18
Sparse Core Ops, SparseCore 0:
  31.5 58.9 all-gather.1
  187.0 49.6 reduce-scatter.1

commit v7 on v5

--- a/solution.py
+++ b/solution.py
@@ -307,29 +307,20 @@
     return pl.ds(pl.multiple_of(place_ref[0] * size, size), size)
 
 
-def known_columns_body(place_ref, prototypes_ref, features_ref, both_ref, out_ref):
-    own, samples = out_ref.shape
-    cols_ref, every_ref = both_ref.at[:8, :], both_ref.at[8:, :]
-    left = prototypes_ref[own_rows(place_ref, own), :]
-    mine = cols_ref[:, own_rows(place_ref, own)]
-    width = 256
-    v1, v2, dy1, dy2, dy3 = (down(mine[row : row + 1, :], width) for row in (V[0], V[1], DY[0], DY[1], DY[2]))
-    for at in tiles(samples, width):
-        inner = get(every_ref, U[2], at) * dy3 + get(every_ref, DX[2], at) * v2
-        inner = inner + get(every_ref, U[1], at) * dy2 + get(every_ref, DX[1], at) * v1 + get(every_ref, U[0], at) * dy1
-        out_ref[:, at] = inner * exponential(left, features_ref[at, :])
-
-
-def finish_columns_body(place_ref, dx_ref, known_ref, prototypes_ref, features_ref, both_ref, weighted_ref, out_ref):
-    own = known_ref.shape[0]
+def finish_columns_body(place_ref, dx_ref, prototypes_ref, features_ref, both_ref, weighted_ref, out_ref):
+    own = out_ref.shape[0]
     rows = dx_ref.shape[2]
+    every_ref = both_ref.at[8:, :]
     left = prototypes_ref[own_rows(place_ref, own), :]
     mine = both_ref[:8, own_rows(place_ref, own)]
-    total = down(mine[V[2] : V[2] + 1, :], out_ref.shape[1]) * weighted_ref[...]
+    v1, v2, v3, dy1, dy2, dy3 = (down(mine[row : row + 1, :], rows) for row in (*V, *DY))
+    total = v3 * weighted_ref[...]
     for i in range(dx_ref.shape[0]):
         at = slice(i * rows, (i + 1) * rows)
         right = features_ref[at, :]
-        total = total + product(known_ref[:, at] + exponential(left, right) * dx_ref[i], right)
+        inner = get(every_ref, U[2], at) * dy3 + get(every_ref, DX[2], at) * v2
+        inner = inner + get(every_ref, U[1], at) * dy2 + get(every_ref, DX[1], at) * v1 + get(every_ref, U[0], at) * dy1
+        total = total + product((inner + dx_ref[i]) * exponential(left, right), right)
     out_ref[...] = sharpness * total
 
 
@@ -419,18 +410,14 @@
         "last_rows", flops=2 * full,
     )
 
-    message, both, features_all = together(message, both, features_all)
-    (known_columns,) = call(
-        known_columns_body, [f32(own, rows_all)], [dp_place, prototypes, features_all, both], "known_columns", smem=1, flops=full
-    )
-    message, known_columns = together(exchange(message, "cls"), known_columns)
+    message = exchange(message, "cls")
     dx_message, message = call(
         finish_rows_body, [f32(samples, 1, rows), f32(classes, 1, sliced)], [cls_place, message, rws], "finish_rows", smem=1
     )
     dx1, message = together(exchange(dx_message, "dp"), message)
     gathered = exchange(message, "cls")
     (prototype_grad,) = call(
-        finish_columns_body, [f32(own, width)], [dp_place, dx1, known_columns, prototypes, features_all, both, weighted],
+        finish_columns_body, [f32(own, width)], [dp_place, dx1, prototypes, features_all, both, weighted],
         "finish_columns", smem=1, flops=3 * full,
     )
     gathered, prototype_grad = together(gathered, prototype_grad)

time: 266 us -> 265 us (level)
  local copies, waits for them, and re-layouts: 18.5 us -> 10.9 us
  waiting for transfers between devices: 16.6 us -> 23.6 us
    unnamed x44 -> x26, local copies, waits for them, and re-layouts: 18.5 us -> 10.9 us
    all_to_all x3, waiting for transfers between devices: 15.9 us -> 22.9 us  [exchange(): return lax.all_to_all(messages, axis, 0, 0, tiled=True)]
    pallas_call x16 -> x15, Pallas kernels: 16.4 us -> 16.3 us  [call(): pl.pallas_call(body, out_shape=outs, in_specs=specs, out_specs=[pl.BlockS...]
where the time goes in v7:
time: 265 us; the launch traced here: 264 us
  blocking collectives  178 us (67%)
  waiting for transfers between devices  23.6 us (9%)
  starting transfers between devices  19.4 us (7%)
  Pallas kernels  16.3 us (6%)
  between operations  14.2 us (5%)
  local copies, waits for them, and re-layouts  10.9 us (4%)
    all_to_all x10, blocking collectives, exchange(): return lax.all_to_all(messages, axis, 0, 0, tiled=True)  178 us
    all_to_all x3, waiting for transfers between devices, exchange(): return lax.all_to_all(messages, axis, 0, 0, tiled=True)  22.9 us
    all_to_all x3, starting transfers between devices, exchange(): return lax.all_to_all(messages, axis, 0, 0, tiled=True)  19.1 us
    pallas_call x15, Pallas kernels, call(): pl.pallas_call(body, out_shape=outs, in_specs=specs, out_specs=[pl.BlockS...  16.3 us
    unnamed x26, local copies, waits for them, and re-layouts  10.9 us
  transfers between devices with their start and end apart: 5, of which 3 were waited for; matrix products, arithmetic and copies ran while one was open for 1% of the time, Pallas kernels for 6%

profile of v7, /device:TPU:1, one launch (start us, length us, event | category | flops | bytes accessed | tf_op | source)
XLA Modules:
  0.0 264.2 jit_solution(11960230320508018927)
XLA Ops:
  7.2 0.0 all-gather.2.cloned.1.call-start
  7.2 0.7 all-gather.2.cloned.1.call-update
  7.9 0.9 convert_element_type.6.features_ref
  8.8 0.7 convert_element_type.7
  9.5 1.4 copy-done.2
  10.9 2.1 start.1
  13.0 28.4 %all_to_all.65.x_ref = f32[64,1,1408]{2,1,0:T(1,128)S(1)} all-to-all(f32[64,1,1408]{2,1,0:T(1,128)S(1)} %get-tuple-element.44), channel_id=1, replica_groups=mesh['dp'=12,'cls'=64] {'cls'}, dimensions={0} | all-to-all | bytes 720896 | tf_op jit(solution)/shard_map/all_to_all | solution.py:335
  41.4 0.6 columns_first.1
  42.0 24.0 %all_to_all.66.y_ref = bf16[12,32,128]{2,1,0:T(8,128)(2,1)S(1)} all-to-all(bf16[12,32,128]{2,1,0:T(8,128)(2,1)S(1)} %get-tuple-element.47), channel_id=1, replica_groups=mesh['dp'=12,'cls'=64] {'dp'}, dimensions={0} | all-to-all | bytes 196608 | tf_op jit(solution)/shard_map/all_to_all | solution.py:335
  66.0 0.4 rows_0.1
  66.4 16.8 %all_to_all.67.x_ref = f32[64,1,256]{2,1,0:T(1,128)S(1)} all-to-all(f32[64,1,256]{2,1,0:T(1,128)S(1)} %get-tuple-element.50), channel_id=1, replica_groups=mesh['dp'=12,'cls'=64] {'cls'}, dimensions={0} | all-to-all | bytes 131072 | tf_op jit(solution)/shard_map/all_to_all | solution.py:335
  83.2 0.4 columns_1.1
  83.6 14.6 %all_to_all.68.y_ref = f32[12,1,3328]{2,1,0:T(1,128)S(1)} all-to-all(f32[12,1,3328]{2,1,0:T(1,128)S(1)} %get-tuple-element.52), channel_id=1, replica_groups=mesh['dp'=12,'cls'=64] {'dp'}, dimensions={0} | all-to-all | bytes 319488 | tf_op jit(solution)/shard_map/all_to_all | solution.py:335
  98.2 0.4 rows_1.1
  98.7 15.3 %all_to_all.69.x_ref = f32[64,1,256]{2,1,0:T(1,128)S(1)} all-to-all(f32[64,1,256]{2,1,0:T(1,128)S(1)} %get-tuple-element.55), channel_id=1, replica_groups=mesh['dp'=12,'cls'=64] {'cls'}, dimensions={0} | all-to-all | bytes 131072 | tf_op jit(solution)/shard_map/all_to_all | solution.py:335
  113.9 0.8 columns_last.1
  114.7 19.0 %all_to_all.70.y_ref = f32[12,1,6400]{2,1,0:T(1,128)S(1)} all-to-all(f32[12,1,6400]{2,1,0:T(1,128)S(1)} %get-tuple-element.57), channel_id=1, replica_groups=mesh['dp'=12,'cls'=64] {'dp'}, dimensions={0} | all-to-all | bytes 614400 | tf_op jit(solution)/shard_map/all_to_all | solution.py:335
  133.7 0.9 rows_last.1
  134.6 0.6 copy-done.10
  135.2 6.1 %all-to-all-start.6 = ((f32[64,1,256]{2,1,0:T(1,128)}), f32[64,1,256]{2,1,0:T(1,128)S(1)}, u32[]{:S(2)}, u32[]{:S(2)}) async-start(f32[64,1,256]{2,1,0:T(1,128)} %copy-done.10), calls=%async_computation.6 | async-start | bytes 131072 | tf_op jit(solution)/shard_map/all_to_all | solution.py:335
  141.3 0.2 reduce-scatter.2.cloned.1.call-start
  141.5 1.4 copy-done.1
  142.9 1.4 copy-done.3
  144.4 2.2 cotangent_products.1
  146.6 1.6 copy-done.6
  148.2 0.7 copy-done.8
  148.9 2.5 all-to-all-done.6.du_ref
  151.4 0.0 reduce-scatter.2.cloned.1.call-update
  151.4 0.4 back_columns_2.1
  151.9 14.7 %all_to_all.71.dv_ref = f32[12,1,3328]{2,1,0:T(1,128)S(1)} all-to-all(f32[12,1,3328]{2,1,0:T(1,128)S(1)} %get-tuple-element.68), channel_id=1, replica_groups=mesh['dp'=12,'cls'=64] {'dp'}, dimensions={0} | all-to-all | bytes 319488 | tf_op jit(solution)/shard_map/all_to_all | solution.py:335
  166.6 0.4 back_rows_1.1
  167.0 19.4 %all_to_all.72.du_ref = f32[64,1,256]{2,1,0:T(1,128)S(1)} all-to-all(f32[64,1,256]{2,1,0:T(1,128)S(1)} %get-tuple-element.70), channel_id=1, replica_groups=mesh['dp'=12,'cls'=64] {'cls'}, dimensions={0} | all-to-all | bytes 131072 | tf_op jit(solution)/shard_map/all_to_all | solution.py:335
  186.5 0.4 back_columns_1.1
  186.9 14.5 %all_to_all.73.dv_ref = bf16[12,32,128]{2,1,0:T(8,128)(2,1)S(1)} all-to-all(bf16[12,32,128]{2,1,0:T(8,128)(2,1)S(1)} %get-tuple-element.72), channel_id=1, replica_groups=mesh['dp'=12,'cls'=64] {'dp'}, dimensions={0} | all-to-all | bytes 196608 | tf_op jit(solution)/shard_map/all_to_all | solution.py:335
  201.3 2.5 last_rows.1
  203.8 6.6 %all-to-all-start.10 = ((f32[64,1,1280]{2,1,0:T(1,128)}), f32[64,1,1280]{2,1,0:T(1,128)S(1)}, u32[]{:S(2)}, u32[]{:S(2)}) async-start(f32[64,1,1280]{2,1,0:T(1,128)} %get-tuple-element.77), calls=%async_computation.10 | async-start | bytes 655360 | tf_op jit(solution)/shard_map/all_to_all | solution.py:335
  210.4 14.1 %all-to-all-done.10.du_ref = f32[64,1,1280]{2,1,0:T(1,128)S(1)} async-done(((f32[64,1,1280]{2,1,0:T(1,128)}), f32[64,1,1280]{2,1,0:T(1,128)S(1)}, u32[]{:S(2)}, u32[]{:S(2)}) %all-to-all-start.10) | async-done | bytes 327712 | tf_op jit(solution)/shard_map/all_to_all | solution.py:335
  224.5 1.0 finish_rows.1
  225.5 11.4 %all_to_all.74.dx_ref = f32[12,1,256]{2,1,0:T(1,128)S(1)} all-to-all(f32[12,1,256]{2,1,0:T(1,128)S(1)} %get-tuple-element.78), channel_id=1, replica_groups=mesh['dp'=12,'cls'=64] {'dp'}, dimensions={0} | all-to-all | bytes 24576 | tf_op jit(solution)/shard_map/all_to_all | solution.py:335
  237.0 6.4 %all-to-all-start.12 = ((f32[64,1,1024]{2,1,0:T(1,128)}), f32[64,1,1024]{2,1,0:T(1,128)S(1)}, u32[]{:S(2)}, u32[]{:S(2)}) async-start(f32[64,1,1024]{2,1,0:T(1,128)} %get-tuple-element.80), calls=%async_computation.12 | async-start | bytes 524288 | tf_op jit(solution)/shard_map/all_to_all | solution.py:335
  243.4 0.0 all-gather.2.cloned.1.call-done.features_ref
  243.5 0.0 reduce-scatter.2.cloned.1.call-done.weighted_ref
  243.5 1.4 copy-done.5
  244.9 1.4 copy-done.11
  246.3 0.9 copy-done.12
  247.2 3.1 %finish_columns.1 = f32[256,256]{1,0:T(8,128)} custom-call(s32[1]{0:T(128)} %bitcast.2.place_ref, f32[12,1,256]{2,1,0:T(1,128)S(1)} %all_to_all.74.dx_ref, bf16[3072,256]{1,0:T(8,128)(2,1)S(1)} %copy-done.5, bf16[3072,256]{1,0:T(8,128)(2,1)S(1)} %copy-done.11, f32[16,3072]{1,0:T(8,128)S(1)} %get-tuple-element.82.both_ref, f32[256,256]{1,0:T(8,128)S(1)} %copy-done.12), custom_call_target="tpu_custom_call" | custom-call | flops 1207959552 | bytes 3878916 | tf_op jit(solution)/shard_map/finish_columns/pallas_call | solution.py:22
  250.3 6.3 %all-to-all-done.12.ref = f32[64,1,1024]{2,1,0:T(1,128)S(1)} async-done(((f32[64,1,1024]{2,1,0:T(1,128)}), f32[64,1,1024]{2,1,0:T(1,128)S(1)}, u32[]{:S(2)}, u32[]{:S(2)}) %all-to-all-start.12) | async-done | bytes 262176 | tf_op jit(solution)/shard_map/all_to_all | solution.py:335
  256.6 0.8 gather_rows.1
  (17 shorter events, 0.0 us)
Async XLA Ops:
  7.2 236.3 %all-gather.2.cloned.1.call-start = ((), (), s32[]{:S(2)}) async-start(), calls=%async_computation.14 | async-start | bytes 1703936 | tf_op jit(solution)/shard_map/all_gather | solution.py:363
  9.5 1.4 copy-start.2
  98.2 15.7 %copy-start = (bf16[256,3072]{1,0:T(8,128)(2,1)S(1)}, bf16[256,3072]{1,0:T(8,128)(2,1)}, u32[]{:S(2)}) copy-start(bf16[256,3072]{1,0:T(8,128)(2,1)} %cotangent_ref.5) | copy-start | bytes 4718596
  133.7 7.9 %copy-start.7 = (bf16[256,256]{1,0:T(8,128)(2,1)S(1)}, bf16[256,256]{1,0:T(8,128)(2,1)}, u32[]{:S(2)}) copy-start(bf16[256,256]{1,0:T(8,128)(2,1)} %features_ref) | copy-start | bytes 393220
  134.6 0.6 copy-start.10
  135.2 16.2 %all-to-all-start.6 = ((f32[64,1,256]{2,1,0:T(1,128)}), f32[64,1,256]{2,1,0:T(1,128)S(1)}, u32[]{:S(2)}, u32[]{:S(2)}) async-start(f32[64,1,256]{2,1,0:T(1,128)} %copy-done.10), calls=%async_computation.6 | async-start | bytes 131072 | tf_op jit(solution)/shard_map/all_to_all | solution.py:335
  141.3 102.2 %reduce-scatter.2.cloned.1.call-start = ((), (), s32[]{:S(2)}) async-start(), calls=%async_computation.15 | async-start | bytes 3407872 | tf_op jit(solution)/shard_map/reduce_scatter | solution.py:399
  141.5 1.4 copy-start.1
  142.9 1.4 copy-start.3
  146.6 1.6 copy-start.6
  148.2 0.7 copy-start.8
  186.4 14.9 %copy-start.4 = (bf16[3072,256]{1,0:T(8,128)(2,1)S(1)}, bf16[3072,256]{1,0:T(8,128)(2,1)}, u32[]{:S(2)}) copy-start(bf16[3072,256]{1,0:T(8,128)(2,1)} %prototypes_ref.7) | copy-start | bytes 4718596
  186.5 14.9 %copy-start.9 = (f32[256,256]{1,0:T(8,128)S(1)}, f32[256,256]{1,0:T(8,128)}, u32[]{:S(2)}) copy-start(f32[256,256]{1,0:T(8,128)} %copy-done.8) | copy-start | bytes 786436
  203.8 20.7 %all-to-all-start.10 = ((f32[64,1,1280]{2,1,0:T(1,128)}), f32[64,1,1280]{2,1,0:T(1,128)S(1)}, u32[]{:S(2)}, u32[]{:S(2)}) async-start(f32[64,1,1280]{2,1,0:T(1,128)} %get-tuple-element.77), calls=%async_computation.10 | async-start | bytes 655360 | tf_op jit(solution)/shard_map/all_to_all | solution.py:335
  237.0 19.6 %all-to-all-start.12 = ((f32[64,1,1024]{2,1,0:T(1,128)}), f32[64,1,1024]{2,1,0:T(1,128)S(1)}, u32[]{:S(2)}, u32[]{:S(2)}) async-start(f32[64,1,1024]{2,1,0:T(1,128)} %get-tuple-element.80), calls=%async_computation.12 | async-start | bytes 524288 | tf_op jit(solution)/shard_map/all_to_all | solution.py:335
  243.5 1.4 copy-start.5
  244.9 1.4 copy-start.11
  246.3 0.9 copy-start.12
Sparse Core Ops, SparseCore 0:
  10.4 62.8 all-gather.1
  151.6 52.6 reduce-scatter.1

commit v8 on v7

--- a/solution.py
+++ b/solution.py
@@ -364,6 +364,7 @@
     kernel, cols, message = call(
         start_body, [block_t, cols_t, f32(classes, 1, rows + LANES + sliced)], [features.astype(F32), prototypes, counts], "start", flops=3 * full
     )
+    message, dp_place, cls_place = together(message, dp_place, cls_place)
     message = exchange(message, "cls")
     cols, rws, every, message = call(
         functools.partial(columns_first_body, float(rows_all)), [cols_t, rws_t, every_t, to_columns], [message, kernel, cols],

time: 265 us -> 264 us (level)
  blocking collectives: 178 us -> 198 us
  waiting for transfers between devices: 23.6 us -> 9.53 us
  starting transfers between devices: 19.4 us -> 12.8 us
    all_to_all x10 -> x11, blocking collectives: 178 us -> 198 us  [exchange(): return lax.all_to_all(messages, axis, 0, 0, tiled=True)]
    all_to_all x3 -> x2, waiting for transfers between devices: 22.9 us -> 8.79 us  [exchange(): return lax.all_to_all(messages, axis, 0, 0, tiled=True)]
    all_to_all x3 -> x2, starting transfers between devices: 19.1 us -> 12.5 us  [exchange(): return lax.all_to_all(messages, axis, 0, 0, tiled=True)]
  transfers between devices with their start and end apart: 5 -> 4, of which waited for: 3 -> 2; matrix products, arithmetic and copies ran while one was open for 1% -> 1% of each run, Pallas kernels for 6% -> 6%
where the time goes in v8:
time: 264 us; the launch traced here: 263 us
  blocking collectives  198 us (75%)
  Pallas kernels  15.6 us (6%)
  between operations  14.2 us (5%)
  starting transfers between devices  12.8 us (5%)
  local copies, waits for them, and re-layouts  10.9 us (4%)
  waiting for transfers between devices  9.53 us (4%)
    all_to_all x11, blocking collectives, exchange(): return lax.all_to_all(messages, axis, 0, 0, tiled=True)  198 us
    pallas_call x15, Pallas kernels, call(): pl.pallas_call(body, out_shape=outs, in_specs=specs, out_specs=[pl.BlockS...  15.6 us
    all_to_all x2, starting transfers between devices, exchange(): return lax.all_to_all(messages, axis, 0, 0, tiled=True)  12.5 us
    unnamed x26, local copies, waits for them, and re-layouts  10.9 us
    all_to_all x2, waiting for transfers between devices, exchange(): return lax.all_to_all(messages, axis, 0, 0, tiled=True)  8.79 us
  transfers between devices with their start and end apart: 4, of which 2 were waited for; matrix products, arithmetic and copies ran while one was open for 1% of the time, Pallas kernels for 6%

profile of v8, /device:TPU:1, one launch (start us, length us, event | category | flops | bytes accessed | tf_op | source)
XLA Modules:
  0.0 262.7 jit_solution(4933045145071302062)
XLA Ops:
  7.2 0.0 all-gather.2.cloned.1.call-start
  7.2 0.7 all-gather.2.cloned.1.call-update
  7.9 0.9 convert_element_type.6.features_ref
  8.8 0.7 convert_element_type.7
  9.5 1.4 copy-done.2
  10.9 2.1 start.1
  13.0 28.4 %all_to_all.65.x_ref = f32[64,1,1408]{2,1,0:T(1,128)S(1)} all-to-all(f32[64,1,1408]{2,1,0:T(1,128)S(1)} %get-tuple-element.49), channel_id=1, replica_groups=mesh['dp'=12,'cls'=64] {'cls'}, dimensions={0} | all-to-all | bytes 720896 | tf_op jit(solution)/shard_map/all_to_all | solution.py:335
  41.4 0.6 columns_first.1
  42.0 24.0 %all_to_all.66.y_ref = bf16[12,32,128]{2,1,0:T(8,128)(2,1)S(1)} all-to-all(bf16[12,32,128]{2,1,0:T(8,128)(2,1)S(1)} %get-tuple-element.52), channel_id=1, replica_groups=mesh['dp'=12,'cls'=64] {'dp'}, dimensions={0} | all-to-all | bytes 196608 | tf_op jit(solution)/shard_map/all_to_all | solution.py:335
  66.0 0.4 rows_0.1
  66.4 16.8 %all_to_all.67.x_ref = f32[64,1,256]{2,1,0:T(1,128)S(1)} all-to-all(f32[64,1,256]{2,1,0:T(1,128)S(1)} %get-tuple-element.55), channel_id=1, replica_groups=mesh['dp'=12,'cls'=64] {'cls'}, dimensions={0} | all-to-all | bytes 131072 | tf_op jit(solution)/shard_map/all_to_all | solution.py:335
  83.2 0.4 columns_1.1
  83.6 14.6 %all_to_all.68.y_ref = f32[12,1,3328]{2,1,0:T(1,128)S(1)} all-to-all(f32[12,1,3328]{2,1,0:T(1,128)S(1)} %get-tuple-element.57), channel_id=1, replica_groups=mesh['dp'=12,'cls'=64] {'dp'}, dimensions={0} | all-to-all | bytes 319488 | tf_op jit(solution)/shard_map/all_to_all | solution.py:335
  98.2 0.4 rows_1.1
  98.7 15.3 %all_to_all.69.x_ref = f32[64,1,256]{2,1,0:T(1,128)S(1)} all-to-all(f32[64,1,256]{2,1,0:T(1,128)S(1)} %get-tuple-element.60), channel_id=1, replica_groups=mesh['dp'=12,'cls'=64] {'cls'}, dimensions={0} | all-to-all | bytes 131072 | tf_op jit(solution)/shard_map/all_to_all | solution.py:335
  113.9 0.8 columns_last.1
  114.7 19.0 %all_to_all.70.y_ref = f32[12,1,6400]{2,1,0:T(1,128)S(1)} all-to-all(f32[12,1,6400]{2,1,0:T(1,128)S(1)} %get-tuple-element.62), channel_id=1, replica_groups=mesh['dp'=12,'cls'=64] {'dp'}, dimensions={0} | all-to-all | bytes 614400 | tf_op jit(solution)/shard_map/all_to_all | solution.py:335
  133.7 0.9 rows_last.1
  134.6 0.0 copy-start.10
  134.6 0.6 copy-done.10
  135.2 6.1 %all-to-all-start.6 = ((f32[64,1,256]{2,1,0:T(1,128)}), f32[64,1,256]{2,1,0:T(1,128)S(1)}, u32[]{:S(2)}, u32[]{:S(2)}) async-start(f32[64,1,256]{2,1,0:T(1,128)} %copy-done.10), calls=%async_computation.6 | async-start | bytes 131072 | tf_op jit(solution)/shard_map/all_to_all | solution.py:335
  141.3 0.2 reduce-scatter.2.cloned.1.call-start
  141.5 1.4 copy-done.1
  142.9 1.4 copy-done.3
  144.4 2.2 cotangent_products.1
  146.6 1.6 copy-done.6
  148.2 0.7 copy-done.8
  148.9 2.5 all-to-all-done.6.du_ref
  151.4 0.0 reduce-scatter.2.cloned.1.call-update
  151.5 0.4 back_columns_2.1
  151.9 14.7 %all_to_all.71.dv_ref = f32[12,1,3328]{2,1,0:T(1,128)S(1)} all-to-all(f32[12,1,3328]{2,1,0:T(1,128)S(1)} %get-tuple-element.73), channel_id=1, replica_groups=mesh['dp'=12,'cls'=64] {'dp'}, dimensions={0} | all-to-all | bytes 319488 | tf_op jit(solution)/shard_map/all_to_all | solution.py:335
  166.6 0.4 back_rows_1.1
  167.0 19.4 %all_to_all.72.du_ref = f32[64,1,256]{2,1,0:T(1,128)S(1)} all-to-all(f32[64,1,256]{2,1,0:T(1,128)S(1)} %get-tuple-element.75), channel_id=1, replica_groups=mesh['dp'=12,'cls'=64] {'cls'}, dimensions={0} | all-to-all | bytes 131072 | tf_op jit(solution)/shard_map/all_to_all | solution.py:335
  186.5 0.4 back_columns_1.1
  186.9 14.5 %all_to_all.73.dv_ref = bf16[12,32,128]{2,1,0:T(8,128)(2,1)S(1)} all-to-all(bf16[12,32,128]{2,1,0:T(8,128)(2,1)S(1)} %get-tuple-element.77), channel_id=1, replica_groups=mesh['dp'=12,'cls'=64] {'dp'}, dimensions={0} | all-to-all | bytes 196608 | tf_op jit(solution)/shard_map/all_to_all | solution.py:335
  201.4 1.7 last_rows.1
  203.1 19.9 %all_to_all.74.du_ref = f32[64,1,1280]{2,1,0:T(1,128)S(1)} all-to-all(f32[64,1,1280]{2,1,0:T(1,128)S(1)} %get-tuple-element.82), channel_id=1, replica_groups=mesh['dp'=12,'cls'=64] {'cls'}, dimensions={0} | all-to-all | bytes 655360 | tf_op jit(solution)/shard_map/all_to_all | solution.py:335
  223.0 1.0 finish_rows.1
  224.0 11.4 %all_to_all.75.dx_ref = f32[12,1,256]{2,1,0:T(1,128)S(1)} all-to-all(f32[12,1,256]{2,1,0:T(1,128)S(1)} %get-tuple-element.83), channel_id=1, replica_groups=mesh['dp'=12,'cls'=64] {'dp'}, dimensions={0} | all-to-all | bytes 24576 | tf_op jit(solution)/shard_map/all_to_all | solution.py:335
  235.4 6.4 %all-to-all-start.12 = ((f32[64,1,1024]{2,1,0:T(1,128)}), f32[64,1,1024]{2,1,0:T(1,128)S(1)}, u32[]{:S(2)}, u32[]{:S(2)}) async-start(f32[64,1,1024]{2,1,0:T(1,128)} %get-tuple-element.85), calls=%async_computation.12 | async-start | bytes 524288 | tf_op jit(solution)/shard_map/all_to_all | solution.py:335
  241.9 0.0 all-gather.2.cloned.1.call-done.features_ref
  241.9 0.0 reduce-scatter.2.cloned.1.call-done.weighted_ref
  242.0 1.4 copy-done.5
  243.4 1.4 copy-done.11
  244.8 0.9 copy-done.12
  245.7 3.1 %finish_columns.1 = f32[256,256]{1,0:T(8,128)} custom-call(s32[1]{0:T(128)} %bitcast.1.place_ref, f32[12,1,256]{2,1,0:T(1,128)S(1)} %all_to_all.75.dx_ref, bf16[3072,256]{1,0:T(8,128)(2,1)S(1)} %copy-done.5, bf16[3072,256]{1,0:T(8,128)(2,1)S(1)} %copy-done.11, f32[16,3072]{1,0:T(8,128)S(1)} %get-tuple-element.88.both_ref, f32[256,256]{1,0:T(8,128)S(1)} %copy-done.12), custom_call_target="tpu_custom_call" | custom-call | flops 1207959552 | bytes 3878916 | tf_op jit(solution)/shard_map/finish_columns/pallas_call | solution.py:22
  248.8 6.3 %all-to-all-done.12.ref = f32[64,1,1024]{2,1,0:T(1,128)S(1)} async-done(((f32[64,1,1024]{2,1,0:T(1,128)}), f32[64,1,1024]{2,1,0:T(1,128)S(1)}, u32[]{:S(2)}, u32[]{:S(2)}) %all-to-all-start.12) | async-done | bytes 262176 | tf_op jit(solution)/shard_map/all_to_all | solution.py:335
  255.1 0.8 gather_rows.1
  (16 shorter events, 0.0 us)
Async XLA Ops:
  7.2 234.7 %all-gather.2.cloned.1.call-start = ((), (), s32[]{:S(2)}) async-start(), calls=%async_computation.14 | async-start | bytes 1703936 | tf_op jit(solution)/shard_map/all_gather | solution.py:363
  9.5 1.4 copy-start.2
  98.2 15.7 %copy-start = (bf16[256,3072]{1,0:T(8,128)(2,1)S(1)}, bf16[256,3072]{1,0:T(8,128)(2,1)}, u32[]{:S(2)}) copy-start(bf16[256,3072]{1,0:T(8,128)(2,1)} %cotangent_ref.5) | copy-start | bytes 4718596
  133.7 7.9 %copy-start.7 = (bf16[256,256]{1,0:T(8,128)(2,1)S(1)}, bf16[256,256]{1,0:T(8,128)(2,1)}, u32[]{:S(2)}) copy-start(bf16[256,256]{1,0:T(8,128)(2,1)} %features_ref) | copy-start | bytes 393220
  134.6 0.6 copy-start.10
  135.2 16.2 %all-to-all-start.6 = ((f32[64,1,256]{2,1,0:T(1,128)}), f32[64,1,256]{2,1,0:T(1,128)S(1)}, u32[]{:S(2)}, u32[]{:S(2)}) async-start(f32[64,1,256]{2,1,0:T(1,128)} %copy-done.10), calls=%async_computation.6 | async-start | bytes 131072 | tf_op jit(solution)/shard_map/all_to_all | solution.py:335
  141.3 100.6 %reduce-scatter.2.cloned.1.call-start = ((), (), s32[]{:S(2)}) async-start(), calls=%async_computation.15 | async-start | bytes 3407872 | tf_op jit(solution)/shard_map/reduce_scatter | solution.py:400
  141.5 1.4 copy-start.1
  142.9 1.4 copy-start.3
  146.6 1.6 copy-start.6
  148.2 0.7 copy-start.8
  186.5 14.9 %copy-start.4 = (bf16[3072,256]{1,0:T(8,128)(2,1)S(1)}, bf16[3072,256]{1,0:T(8,128)(2,1)}, u32[]{:S(2)}) copy-start(bf16[3072,256]{1,0:T(8,128)(2,1)} %prototypes_ref.7) | copy-start | bytes 4718596
  186.5 14.9 %copy-start.9 = (f32[256,256]{1,0:T(8,128)S(1)}, f32[256,256]{1,0:T(8,128)}, u32[]{:S(2)}) copy-start(f32[256,256]{1,0:T(8,128)} %copy-done.8) | copy-start | bytes 786436
  235.4 19.6 %all-to-all-start.12 = ((f32[64,1,1024]{2,1,0:T(1,128)}), f32[64,1,1024]{2,1,0:T(1,128)S(1)}, u32[]{:S(2)}, u32[]{:S(2)}) async-start(f32[64,1,1024]{2,1,0:T(1,128)} %get-tuple-element.85), calls=%async_computation.12 | async-start | bytes 524288 | tf_op jit(solution)/shard_map/all_to_all | solution.py:335
  241.9 1.4 copy-start.5
  243.4 1.4 copy-start.11
  244.8 0.9 copy-start.12
Sparse Core Ops, SparseCore 0:
  10.4 62.8 all-gather.1
  151.6 52.7 reduce-scatter.1
